TPU v7x, 32 devices: a whole 2x2x4 slice. The times are simulated.
32 devices in a mesh: dp: 8 (over z, y), head: 4 (over x, core).
Axes of the slice: x: 2, y: 2, z: 4, core: 2. Of those that a mesh axis runs over, the one named last changes fastest.
Arguments:
- tokens: bfloat16 [32, 1024, 768], P('dp', 'head'), may hold values from -6 to 6
- qkv_weight: float32 [768, 2304], P('dp'), may hold values from -0.21875 to 0.21875
- proj_weight: float32 [768, 768], P('dp'), may hold values from -1.75 to 1.75
- up_weight: float32 [768, 3072], P('dp'), may hold values from -0.21875 to 0.21875
- down_weight: float32 [3072, 768], P('dp'), may hold values from -0.109375 to 0.109375
- attn_gain: float32 [768], P('dp'), may hold values from 0.1 to 1.9
- attn_bias: float32 [768], P('dp'), may hold values from -3 to 3
- ffn_gain: float32 [768], P('dp'), may hold values from 0.1 to 1.9
- ffn_bias: float32 [768], P('dp'), may hold values from -3 to 3
- cotangent: bfloat16 [32, 1024, 768], P('dp', 'head'), may hold values from -6 to 6
Outputs:
- output: bfloat16 [32, 1024, 768], P('dp', 'head')
- grad_tokens: float32 [32, 1024, 768], P('dp', 'head')
- grad_qkv: float32 [768, 2304], P('dp')
- grad_proj: float32 [768, 768], P('dp')
- grad_up: float32 [768, 3072], P('dp')
- grad_down: float32 [3072, 768], P('dp')
- grad_attn_gain: float32 [768], P('dp')
- grad_attn_bias: float32 [768], P('dp')
- grad_ffn_gain: float32 [768], P('dp')
- grad_ffn_bias: float32 [768], P('dp')
All inputs are finite; a program needn't handle non-finite values.
Results may differ from a plain program's by a relative error of at most 0.013.
Values may be sent and summed in bfloat16 or wider, within the bound.
No kernel may reach another device: no remote copies, remote signals or barrier semaphores. Data moves between devices by JAX's collectives and lax.ppermute only.
A program may use at most 192 MiB of HBM per device.

v0:
```python
import jax
import jax.numpy as jnp
from jax import lax
from jax.sharding import PartitionSpec as P

HEADS = 12
HEAD_DIM = 64
SEQ = 1024


EPSILON = 1e-05


def layer_norm(vector, gain_vec, bias_vec):
    row_mean = jnp.mean(vector, axis=-1, keepdims=True)
    centred = vector - row_mean
    variance = jnp.mean(centred * centred, axis=-1, keepdims=True)
    return centred * lax.rsqrt(variance + EPSILON) * gain_vec + bias_vec


def gelu_tanh(vector):
    return jax.nn.gelu(vector, approximate=True)


def contract_rows(left, right):
    return lax.dot_general(
        left, right, (((0,), (0,)), ((), ())), preferred_element_type=jnp.float32
    )


def contract_cols(left, right):
    return lax.dot_general(
        left, right, (((1,), (1,)), ((), ())), preferred_element_type=jnp.float32
    )


def causal_mask(first_row, row_count, key_count):
    query_pos = first_row + jnp.arange(row_count)[:, None]
    key_pos = jnp.arange(key_count)[None, :]
    return query_pos >= key_pos


def attend_sequence(triple):
    query_rows, key_rows, value_rows = triple
    seq_len = query_rows.shape[0]
    block_rows = min(512, seq_len)
    scaling = query_rows.shape[-1] ** (-0.5)
    out_parts = []
    log_parts = []
    for block_id in range(seq_len // block_rows):
        first_row = block_id * block_rows
        last_row = first_row + block_rows
        raw_scores = (
            jnp.einsum(
                "qhd,khd->hqk",
                query_rows[first_row:last_row],
                key_rows[:last_row],
                preferred_element_type=jnp.float32,
            )
            * scaling
        )
        scores = jnp.where(causal_mask(first_row, block_rows, last_row), raw_scores, -1e30)
        row_max = jnp.max(scores, axis=-1, keepdims=True)
        weights = jnp.exp(scores - row_max)
        row_total = jnp.sum(weights, axis=-1, keepdims=True)
        probs_low = (weights / row_total).astype(jnp.bfloat16)
        out_parts.append(
            jnp.einsum(
                "hqk,khd->qhd", probs_low, value_rows[:last_row], preferred_element_type=jnp.float32
            )
        )
        log_parts.append(row_max + jnp.log(row_total))
    return (jnp.concatenate(out_parts, axis=0), jnp.concatenate(log_parts, axis=1))


def sequence_grads(bundle):
    query_rows, key_rows, value_rows, log_totals, grad_rows = bundle
    seq_len = query_rows.shape[0]
    block_rows = min(512, seq_len)
    scaling = query_rows.shape[-1] ** (-0.5)
    query_parts = []
    grad_keys = jnp.zeros(key_rows.shape, jnp.float32)
    grad_values = jnp.zeros(value_rows.shape, jnp.float32)
    for block_id in range(seq_len // block_rows):
        first_row = block_id * block_rows
        last_row = first_row + block_rows
        query_block = query_rows[first_row:last_row]
        key_part = key_rows[:last_row]
        grad_block = grad_rows[first_row:last_row]
        raw_scores = (
            jnp.einsum("qhd,khd->hqk", query_block, key_part, preferred_element_type=jnp.float32)
            * scaling
        )
        scores = jnp.where(causal_mask(first_row, block_rows, last_row), raw_scores, -1e30)
        probs = jnp.exp(scores - log_totals[:, first_row:last_row])
        probs_low = probs.astype(jnp.bfloat16)
        grad_probs = jnp.einsum(
            "qhd,khd->hqk", grad_block, value_rows[:last_row], preferred_element_type=jnp.float32
        )
        grad_values = grad_values.at[:last_row].add(
            jnp.einsum("hqk,qhd->khd", probs_low, grad_block, preferred_element_type=jnp.float32)
        )
        centre = jnp.sum(probs * grad_probs, axis=-1, keepdims=True)
        grad_scores = (probs * (grad_probs - centre)).astype(jnp.bfloat16)
        query_parts.append(
            jnp.einsum("hqk,khd->qhd", grad_scores, key_part, preferred_element_type=jnp.float32)
            * scaling
        )
        grad_keys = grad_keys.at[:last_row].add(
            jnp.einsum("hqk,qhd->khd", grad_scores, query_block, preferred_element_type=jnp.float32)
            * scaling
        )
    return (jnp.concatenate(query_parts, axis=0), grad_keys, grad_values)


def fetch(qkv_weight, proj_weight, up_weight, down_weight, norm_table):
    return (
        lax.all_gather(qkv_weight.astype(jnp.bfloat16), "dp", axis=0, tiled=True),
        lax.all_gather(proj_weight.astype(jnp.bfloat16), "dp", axis=0, tiled=True),
        lax.all_gather(up_weight.astype(jnp.bfloat16), "dp", axis=0, tiled=True),
        lax.all_gather(down_weight.astype(jnp.bfloat16), "dp", axis=0, tiled=True),
        lax.all_gather(norm_table.astype(jnp.bfloat16), "dp", axis=0, tiled=True),
    )


def local(
    tokens,
    qkv_weight,
    proj_weight,
    up_weight,
    down_weight,
    attn_gain,
    attn_bias,
    ffn_gain,
    ffn_bias,
    cotangent,
):
    seq_count, part_rows, model_width = tokens.shape
    tok_rows = seq_count * part_rows
    splits = lax.axis_size("head")
    per_dev = HEADS // splits
    head_cols = per_dev * HEAD_DIM
    norm_table = jnp.stack([attn_gain, attn_bias, ffn_gain, ffn_bias], axis=1)
    full_qkv, full_proj, full_up, full_down, full_table = fetch(
        qkv_weight, proj_weight, up_weight, down_weight, norm_table
    )
    table = full_table.astype(jnp.float32)
    inputs = tokens.astype(jnp.float32).reshape(tok_rows, model_width)
    normed, norm_pull = jax.vjp(layer_norm, inputs, table[:, 0], table[:, 1])
    normed_low = normed.astype(jnp.bfloat16)
    mixed = jnp.dot(normed_low, full_qkv, preferred_element_type=jnp.float32).astype(jnp.bfloat16)
    spread_heads = lax.all_to_all(
        mixed.reshape(seq_count, part_rows, 3, splits, head_cols),
        "head",
        split_axis=3,
        concat_axis=1,
        tiled=True,
    )
    queries = spread_heads[:, :, 0].reshape(seq_count, SEQ, per_dev, HEAD_DIM)
    key_rows = spread_heads[:, :, 1].reshape(seq_count, SEQ, per_dev, HEAD_DIM)
    value_rows = spread_heads[:, :, 2].reshape(seq_count, SEQ, per_dev, HEAD_DIM)
    attended, log_totals = lax.map(attend_sequence, (queries, key_rows, value_rows))
    attended_low = attended.astype(jnp.bfloat16).reshape(seq_count, SEQ, 1, head_cols)
    token_heads = lax.all_to_all(
        attended_low, "head", split_axis=1, concat_axis=2, tiled=True
    ).reshape(tok_rows, model_width)
    middle = inputs + jnp.dot(token_heads, full_proj, preferred_element_type=jnp.float32)
    normed_two, norm_pull_two = jax.vjp(layer_norm, middle, table[:, 2], table[:, 3])
    second_low = normed_two.astype(jnp.bfloat16)
    hidden = jnp.dot(second_low, full_up, preferred_element_type=jnp.float32)
    active, gelu_pull = jax.vjp(gelu_tanh, hidden)
    active_low = active.astype(jnp.bfloat16)
    output = (middle + jnp.dot(active_low, full_down, preferred_element_type=jnp.float32)).astype(
        jnp.bfloat16
    )
    back_qkv, back_proj, back_up, back_down = (full_qkv, full_proj, full_up, full_down)
    flat_cot = cotangent.reshape(tok_rows, model_width)
    upstream = flat_cot.astype(jnp.float32)
    grad_down = contract_rows(active_low, flat_cot)
    (grad_active,) = gelu_pull(contract_cols(flat_cot, back_down))
    grad_hidden = grad_active.astype(jnp.bfloat16)
    grad_up = contract_rows(second_low, grad_hidden)
    grad_second, grad_ffn_gain, grad_ffn_bias = norm_pull_two(contract_cols(grad_hidden, back_up))
    grad_middle = upstream + grad_second
    grad_branch = grad_middle.astype(jnp.bfloat16)
    grad_proj = contract_rows(token_heads, grad_branch)
    grad_heads = contract_cols(grad_branch, back_proj).astype(jnp.bfloat16)
    grad_spread = lax.all_to_all(
        grad_heads.reshape(seq_count, part_rows, splits, head_cols),
        "head",
        split_axis=2,
        concat_axis=1,
        tiled=True,
    )
    grad_attended = grad_spread.reshape(seq_count, SEQ, per_dev, HEAD_DIM)
    grad_query, grad_keys, grad_values = lax.map(
        sequence_grads, (queries, key_rows, value_rows, log_totals, grad_attended)
    )
    grad_mixed = jnp.stack(
        [
            grad_query.reshape(seq_count, SEQ, head_cols),
            grad_keys.reshape(seq_count, SEQ, head_cols),
            grad_values.reshape(seq_count, SEQ, head_cols),
        ],
        axis=2,
    ).astype(jnp.bfloat16)
    back_mixed = lax.all_to_all(
        grad_mixed.reshape(seq_count, SEQ, 3, 1, head_cols),
        "head",
        split_axis=1,
        concat_axis=3,
        tiled=True,
    ).reshape(tok_rows, 3 * model_width)
    grad_qkv = contract_rows(normed_low, back_mixed)
    grad_normed, grad_attn_gain, grad_attn_bias = norm_pull(contract_cols(back_mixed, back_qkv))
    grad_tokens = (grad_middle + grad_normed).reshape(seq_count, part_rows, model_width)
    grad_table = jnp.stack([grad_attn_gain, grad_attn_bias, grad_ffn_gain, grad_ffn_bias], axis=1)
    summed = (
        lax.psum_scatter(grad_qkv, "dp", scatter_dimension=0, tiled=True),
        lax.psum_scatter(grad_proj, "dp", scatter_dimension=0, tiled=True),
        lax.psum_scatter(grad_up, "dp", scatter_dimension=0, tiled=True),
        lax.psum_scatter(grad_down, "dp", scatter_dimension=0, tiled=True),
        lax.psum_scatter(grad_table, "dp", scatter_dimension=0, tiled=True),
    )
    shard_qkv, shard_proj, shard_up, shard_down, shard_table = (
        lax.psum(summed[0].astype(jnp.bfloat16), "head").astype(jnp.float32),
        lax.psum(summed[1].astype(jnp.bfloat16), "head").astype(jnp.float32),
        lax.psum(summed[2].astype(jnp.bfloat16), "head").astype(jnp.float32),
        lax.psum(summed[3].astype(jnp.bfloat16), "head").astype(jnp.float32),
        lax.psum(summed[4].astype(jnp.bfloat16), "head").astype(jnp.float32),
    )
    return (
        output.reshape(seq_count, part_rows, model_width),
        grad_tokens,
        shard_qkv,
        shard_proj,
        shard_up,
        shard_down,
        shard_table[:, 0],
        shard_table[:, 1],
        shard_table[:, 2],
        shard_table[:, 3],
    )


def solution(mesh):
    placed = (
        P("dp", "head", None),
        P("dp", None),
        P("dp", None),
        P("dp", None),
        P("dp", None),
        P("dp"),
        P("dp"),
        P("dp"),
        P("dp"),
        P("dp", "head", None),
    )
    return jax.shard_map(
        local,
        mesh=mesh,
        in_specs=placed,
        out_specs=(
            P("dp", "head", None),
            P("dp", "head", None),
            P("dp", None),
            P("dp", None),
            P("dp", None),
            P("dp", None),
            P("dp"),
            P("dp"),
            P("dp"),
            P("dp"),
        ),
        check_vma=False,
    )
```

profile of v0, /device:TPU:0, one launch (start us, length us, event | category | flops | bytes accessed | tf_op | source)
XLA Modules:
  0.0 994.0 jit_solution(7263086868069828398)
XLA Ops:
  13.8 22.3 %all-gather = bf16[8,96,4]{1,2,0:T(4,128)(2,1)S(1)} all-gather(bf16[1,96,4]{1,2,0:T(4,128)(2,1)S(1)} %maximum_bitcast_fusion.3), channel_id=1, replica_groups=mesh['dp'=8,'head'=4] {'dp'}, dimensions={0}, use_global_device_ids=true | all-gather | bytes 6912 | tf_op jit(solution)/shard_map/all_gather | solution.py:122
  36.8 41.9 %all-gather.6.cloned.1.call-done = bf16[768,2304]{1,0:T(8,128)(2,1)} async-done(((bf16[96,2304]{1,0:T(8,128)(2,1)}), bf16[768,2304]{1,0:T(8,128)(2,1)}) %all-gather.6.cloned.1.call-update) | async-done | bytes 3538960 | tf_op jit(solution)/shard_map/all_gather | solution.py:118
  78.8 7.5 convolution_convert_fusion
  86.3 12.8 %reshape.443 = bf16[4,256,3,4,192]{4,3,2,1,0:T(4,128)(2,1)} reshape(bf16[1024,2304]{1,0:T(8,128)(2,1)} %convolution_convert_fusion) | data formatting | bytes 9437184 | tf_op jit(solution)/shard_map/reshape | solution.py:153
  99.1 11.3 %copy.103 = bf16[4,256,3,4,192]{1,0,4,2,3:T(4,128)(2,1)} copy(bf16[4,256,3,4,192]{4,3,2,1,0:T(4,128)(2,1)} %reshape.443) | data formatting | bytes 9437184 | tf_op jit(solution)/shard_map/reshape | solution.py:153
  110.4 5.1 all-to-all-start
  116.7 52.6 %all-to-all-done = bf16[4,256,3,4,192]{1,0,4,2,3:T(4,128)(2,1)} async-done(((bf16[4,256,3,4,192]{1,0,4,2,3:T(4,128)(2,1)}), bf16[4,256,3,4,192]{1,0,4,2,3:T(4,128)(2,1)}, u32[]{:S(2)}, u32[]{:S(2)}) %all-to-all-start) | async-done | bytes 4718624 | tf_op jit(solution)/shard_map/all_to_all | solution.py:152
  169.3 8.2 copy.104
  177.5 8.7 all_to_all.49
  192.4 51.7 %while.35 = (s32[]{:T(128)}, bf16[4,1024,3,64]{1,3,2,0:T(8,128)(2,1)}, f32[4,3,1024,1]{2,1,3,0:T(4,128)S(1)}, bf16[4,1024,3,64]{1,3,2,0:T(8,128)(2,1)}, bf16[4,1...) while((s32[]{:T(128)}, ...), condition=%wide.region_7.8_spmd, body=%wide.region_2.7_spmd.sunk | while | flops 633864704 | bytes 34347648 | solution.py:162
  248.2 30.5 %all_to_all.63 = bf16[4,1024,1,192]{3,0,2,1:T(4,128)(2,1)} all-to-all(bf16[4,1024,1,192]{3,0,2,1:T(4,128)(2,1)} %copy.105), channel_id=1, replica_groups=mesh['dp'=8,'head'=4] {'head'}, dimensions={1} | all-to-all | bytes 3145728 | tf_op jit(solution)/shard_map/all_to_all | solution.py:164
  293.0 11.2 %fusion.103 = f32[1024,3072]{1,0:T(8,128)} fusion(bf16[768,3072]{1,0:T(8,128)(2,1)} %all-gather.10.cloned.1.call-done, f32[1024,768]{1,0:T(8,128)} %copy-done.3, f32[768]{0:T(1024)S(1)} %get-tuple-element.271, f32[768]{0:T(1024)S(1)} %get-tuple-element.270, f32[1024]{0:T(1024)S(1)} %fusion.97, f32[1024]{0:T(1024)S(1)} %broadcast_multiply_fusion), kind=kOutput, calls=%fused_computation.174 | convolution fusion | flops 4835770368 | bytes 20461568 | tf_op jit(solution)/shard_map/dot_general | solution.py:170
  304.1 14.2 %fusion.80 = bf16[1024,3072]{1,0:T(8,128)(2,1)S(1)} fusion(f32[1024,3072]{1,0:T(8,128)} %fusion.103, bf16[1024,768]{1,0:T(8,128)(2,1)S(1)} %bitcast.334, bf16[3072,768]{1,0:T(8,128)(2,1)} %all-gather.12.cloned.1.call-done), kind=kOutput, calls=%fused_computation.111 | convolution fusion | flops 4894752768 | bytes 25165824 | tf_op jit(solution)/shard_map/dot_general | solution.py:32
  318.4 10.8 %multiply_reduce_fusion.2 = (f32[768]{0:T(1024)}, f32[1024]{0:T(1024)S(1)}, f32[768]{0:T(1024)}, f32[1024,768]{1,0:T(8,128)S(1)}) fusion(f32[1024,768]{1,0:T(8,128)S(1)} %copy-done.4, f32[1024]{0:T(1024)S(1)} %fusion.97, f32[1024]{0:T(1024)S(1)} %broadcast_multiply_fusion, f32[768]{0:T(1024)S(1)} %get-tuple-element.270, ...), kind=kOutput, calls=%fused_computation.136 | convolution fusion | flops 4838126592 | bytes 17323008 | tf_op jit(solution)/shard_map/dot_general | solution.py:32
  336.5 11.0 %fusion.102 = f32[768,3072]{1,0:T(8,128)} fusion(bf16[1024,3072]{1,0:T(8,128)(2,1)} %copy-done.7, f32[1024,768]{1,0:T(8,128)} %copy-done.3, f32[768]{0:T(1024)S(1)} %get-tuple-element.271, f32[768]{0:T(1024)S(1)} %get-tuple-element.270, f32[1024]{0:T(1024)S(1)} %fusion.97, f32[1024]{0:T(1024)S(1)} %broadcast_multiply_fusion), kind=kOutput, calls=%fused_computation.173 | convolution fusion | flops 4835770368 | bytes 18888704 | tf_op jit(solution)/shard_map/dot_general | solution.py:26
  360.5 13.3 %fusion.104 = f32[3072,768]{1,0:T(8,128)} fusion(bf16[1024,768]{1,0:T(8,128)(2,1)} %bitcast.333, f32[1024,3072]{1,0:T(8,128)} %fusion.103), kind=kOutput, calls=%fused_computation.175 | convolution fusion | flops 4860149760 | bytes 23592960 | tf_op jit(solution)/shard_map/dot_general | solution.py:26
  373.8 6.7 all-to-all-done.2
  390.7 81.3 %while.36 = (s32[]{:T(128)}, bf16[4,1024,3,64]{1,3,2,0:T(8,128)(2,1)}, bf16[4,1024,3,64]{1,3,2,0:T(8,128)(2,1)}, bf16[4,1024,3,64]{1,3,2,0:T(8,128)(2,1)}, bf16[...) while((s32[]{:T(128)}, ...), condition=%wide.region_15.16_spmd, body=%wide.region_12.15_spmd.sunk | while | flops 1543271936 | bytes 106348816 | solution.py:196
  472.0 5.0 pad_maximum_fusion
  477.1 10.2 %copy.110 = bf16[4,1024,3,1,192]{4,0,3,2,1:T(4,128)(2,1)} copy(bf16[4,1024,3,1,192]{1,4,0,3,2:T(8,128)(2,1)} %pad_maximum_fusion) | data formatting | bytes 9437184 | tf_op jit(solution)/shard_map/stack | solution.py:199
  487.3 5.4 all-to-all-start.3
  493.7 69.8 %all-to-all-done.3 = bf16[4,1024,3,1,192]{4,0,3,2,1:T(4,128)(2,1)} async-done(((bf16[4,1024,3,1,192]{4,0,3,2,1:T(4,128)(2,1)}), bf16[4,1024,3,1,192]{4,0,3,2,1:T(4,128)(2,1)}, u32[]{:S(2)}, u32[]{:S(2)}) %all-to-all-start.3) | async-done | bytes 4718624 | tf_op jit(solution)/shard_map/all_to_all | solution.py:207
  563.4 11.2 %copy.120 = bf16[4,4,256,3,1,192]{2,1,5,3,0,4:T(4,128)(2,1)} copy(bf16[4,4,256,3,1,192]{5,0,3,2,1,4:T(4,128)(2,1)} %bitcast.53) | data formatting | bytes 9437184 | tf_op jit(solution)/shard_map/all_to_all | solution.py:207
  574.7 6.0 copy.112
  584.3 6.1 fusion.108
  591.1 7.5 fusion.95
  603.3 13.1 %add_convert_fusion = bf16[1024,768]{1,0:T(8,128)(2,1)} fusion(f32[1024,768]{1,0:T(8,128)} %copy-done.3, bf16[3072,768]{1,0:T(8,128)(2,1)} %all-gather.12.cloned.1.call-done, f32[1024,3072]{1,0:T(8,128)} %fusion.103), kind=kOutput, calls=%fused_computation.140 | convolution fusion | flops 4861722624 | bytes 22020096 | tf_op jit(solution)/shard_map/dot_general | solution.py:173
  620.4 114.8 %reduce-scatter.14.cloned.1.call-done = f32[384,768]{1,0:T(8,128)} async-done(((f32[3072,768]{1,0:T(8,128)}), f32[384,768]{1,0:T(8,128)}) %reduce-scatter.14.cloned.1.call-update) | async-done | bytes 1179664 | tf_op jit(solution)/shard_map/reduce_scatter | solution.py:222
  737.3 129.7 %reduce-scatter.8.cloned.1.call-done = f32[96,2304]{1,0:T(8,128)} async-done(((f32[768,2304]{1,0:T(8,128)}), f32[96,2304]{1,0:T(8,128)}) %reduce-scatter.8.cloned.1.call-update) | async-done | bytes 884752 | tf_op jit(solution)/shard_map/reduce_scatter | solution.py:219
  873.8 57.3 %reduce-scatter.16.cloned.1.call-done = f32[96,4]{1,0:T(8,128)} async-done(((f32[768,4]{1,0:T(8,128)}), f32[96,4]{1,0:T(8,128)}) %reduce-scatter.16.cloned.1.call-update) | async-done | bytes 1552
  932.0 5.7 psum.39
  938.2 41.8 %all-reduce.5.cloned.1.call-done = (bf16[96,2304]{1,0:T(8,128)(2,1)}, bf16[96,768]{1,0:T(8,128)(2,1)}, bf16[96,3072]{1,0:T(8,128)(2,1)}, bf16[384,768]{1,0:T(8,128)(2,1)}) async-done(((bf16[96,2304]{1,0:T(8,128)(2,1)}, bf16[96,768]{1,0:T(8,128)(2,1)}, bf16[96,3072]{1,0:T(8,128)(2,1)}, bf16[384,768]{1,0:T(8,128)(2,1)}), (bf16[96,2304]{1,0:T(8,128)(2,1)}, bf16[96,768]{1,0:T(8,128)(2,1)}, ...) | async-done | bytes 1769488 | tf_op jit(solution)/shard_map/psum | solution.py:226
  (319 shorter events, 226.7 us)
Async XLA Ops:
  7.2 71.6 %all-gather.6.cloned.1.call-start = ((), (), s32[]{:S(2)}) async-start(), calls=%async_computation.9 | async-start | bytes 3981312 | tf_op jit(solution)/shard_map/all_gather | solution.py:118
  9.4 277.9 %all-gather.8.cloned.1.call-start = ((), (), s32[]{:S(2)}) async-start(), calls=%async_computation.10 | async-start | bytes 1327104 | tf_op jit(solution)/shard_map/all_gather | solution.py:119
  11.2 281.8 %all-gather.10.cloned.1.call-start = ((), (), s32[]{:S(2)}) async-start(), calls=%async_computation.11 | async-start | bytes 5308416 | tf_op jit(solution)/shard_map/all_gather | solution.py:120
  12.4 23.6 %copy-start.27 = (f32[4,256]{1,0:T(4,128)}, f32[4,256]{1,0:T(4,128)S(1)}, u32[]{:S(2)}) copy-start(f32[4,256]{1,0:T(4,128)S(1)} %get-tuple-element.328) | copy-start | bytes 12292
  12.5 73.8 %copy-start.23 = (f32[1,2,4,128]{3,1,2,0:T(2,128)}, f32[1,2,4,128]{3,1,2,0:T(2,128)S(1)}, u32[]{:S(2)}) copy-start(f32[1,2,4,128]{3,1,2,0:T(2,128)S(1)} %copy.123) | copy-start | bytes 12292
  13.7 22.4 %copy-start.31 = (f32[1,2,4,128]{3,1,2,0:T(2,128)}, f32[1,2,4,128]{3,1,2,0:T(2,128)S(1)}, u32[]{:S(2)}) copy-start(f32[1,2,4,128]{3,1,2,0:T(2,128)S(1)} %copy.124) | copy-start | bytes 12292
  13.7 72.5 %copy-start.25 = (f32[1024]{0:T(1024)}, f32[1024]{0:T(1024)S(1)}, u32[]{:S(2)}) copy-start(f32[1024]{0:T(1024)S(1)} %rsqrt.23) | copy-start | bytes 12292
  36.2 50.1 %copy-start.21 = (f32[768]{0:T(1024)}, f32[768]{0:T(1024)S(1)}, u32[]{:S(2)}) copy-start(f32[768]{0:T(1024)S(1)} %get-tuple-element.273) | copy-start | bytes 9220
  36.2 50.0 %copy-start.29 = (f32[768]{0:T(1024)}, f32[768]{0:T(1024)S(1)}, u32[]{:S(2)}) copy-start(f32[768]{0:T(1024)S(1)} %get-tuple-element.272) | copy-start | bytes 9220
  110.4 58.9 %all-to-all-start = ((bf16[4,256,3,4,192]{1,0,4,2,3:T(4,128)(2,1)}), bf16[4,256,3,4,192]{1,0,4,2,3:T(4,128)(2,1)}, u32[]{:S(2)}, u32[]{:S(2)}) async-start(bf16[4,256,3,4,192]{1,0,4,2,3:T(4,128)(2,1)} %copy.103), calls=%async_computation | async-start | bytes 9437184 | tf_op jit(solution)/shard_map/all_to_all | solution.py:152
  115.5 188.6 %all-gather.12.cloned.1.call-start = ((), (), s32[]{:S(2)}) async-start(), calls=%async_computation.12 | async-start | bytes 5308416 | tf_op jit(solution)/shard_map/all_gather | solution.py:121
  116.4 499.9 %reduce-scatter.10.cloned.1.call-start = ((), (), s32[]{:S(2)}) async-start(), calls=%async_computation.14 | async-start | bytes 2654208 | tf_op jit(solution)/shard_map/reduce_scatter | solution.py:220
  292.9 11.2 %copy-start.12 = (bf16[4,256,768]{2,1,0:T(8,128)(2,1)S(1)}, bf16[4,256,768]{2,1,0:T(8,128)(2,1)}, u32[]{:S(2)}) copy-start(bf16[4,256,768]{2,1,0:T(8,128)(2,1)} %param.35) | copy-start | bytes 4718596
  304.1 14.2 %copy-start.4 = (f32[1024,768]{1,0:T(8,128)S(1)}, f32[1024,768]{1,0:T(8,128)}, u32[]{:S(2)}) copy-start(f32[1024,768]{1,0:T(8,128)} %copy-done.3) | copy-start | bytes 9437188
  318.3 10.9 %copy-start.7 = (bf16[1024,3072]{1,0:T(8,128)(2,1)}, bf16[1024,3072]{1,0:T(8,128)(2,1)S(1)}, u32[]{:S(2)}) copy-start(bf16[1024,3072]{1,0:T(8,128)(2,1)S(1)} %fusion.80) | copy-start | bytes 18874372
  336.4 281.6 %reduce-scatter.12.cloned.1.call-start = ((), (), s32[]{:S(2)}) async-start(), calls=%async_computation.15 | async-start | bytes 10616832 | tf_op jit(solution)/shard_map/reduce_scatter | solution.py:221
  356.8 23.6 %all-to-all-start.2 = ((bf16[4,256,4,192]{1,0,3,2:T(4,128)(2,1)}), bf16[4,256,4,192]{1,0,3,2:T(4,128)(2,1)S(1)}, u32[]{:S(2)}, u32[]{:S(2)}) async-start(bf16[4,256,4,192]{1,0,3,2:T(4,128)(2,1)} %reshape.436), calls=%async_computation.2 | async-start | bytes 3145728 | tf_op jit(solution)/shard_map/all_to_all | solution.py:188
  360.4 374.8 %reduce-scatter.14.cloned.1.call-start = ((), (), s32[]{:S(2)}) async-start(), calls=%async_computation.16 | async-start | bytes 10616832 | tf_op jit(solution)/shard_map/reduce_scatter | solution.py:222
  487.3 5.6 copy-start.1
  487.3 5.7 copy-start.22
  487.3 5.7 copy-start.28
  487.3 5.7 copy-start.30
  487.3 5.7 copy-start.35
  487.3 76.1 %all-to-all-start.3 = ((bf16[4,1024,3,1,192]{4,0,3,2,1:T(4,128)(2,1)}), bf16[4,1024,3,1,192]{4,0,3,2,1:T(4,128)(2,1)}, u32[]{:S(2)}, u32[]{:S(2)}) async-start(bf16[4,1024,3,1,192]{4,0,3,2,1:T(4,128)(2,1)} %copy.110), calls=%async_computation.3 | async-start | bytes 12582912 | tf_op jit(solution)/shard_map/all_to_all | solution.py:207
  492.7 374.3 %reduce-scatter.8.cloned.1.call-start = ((), (), s32[]{:S(2)}) async-start(), calls=%async_computation.13 | async-start | bytes 7962624 | tf_op jit(solution)/shard_map/reduce_scatter | solution.py:219
  590.4 340.8 %reduce-scatter.16.cloned.1.call-start = ((), (), s32[]{:S(2)}) async-start(), calls=%async_computation.17 | async-start | bytes 442368
  591.1 7.5 copy-start.32
  591.1 9.1 copy-start.26
  603.0 377.0 %all-reduce.5.cloned.1.call-start = ((), (), s32[]{:S(2)}) async-start(), calls=%async_computation.18 | async-start | bytes 3538944 | tf_op jit(solution)/shard_map/psum | solution.py:226
  618.0 251.1 %copy-start.13 = (bf16[4,256,768]{2,1,0:T(8,128)(2,1)S(1)}, bf16[4,256,768]{2,1,0:T(8,128)(2,1)}, u32[]{:S(2)}) copy-start(bf16[4,256,768]{2,1,0:T(8,128)(2,1)} %param.35) | copy-start | bytes 4718596
  618.0 251.1 %copy-start.34 = (f32[1024]{0:T(1024)S(1)}, f32[1024]{0:T(1024)}, u32[]{:S(2)}) copy-start(f32[1024]{0:T(1024)} %copy-done.33) | copy-start | bytes 12292
  980.0 5.9 copy-start.20
  (35 other events, 84.9 us)
Sparse Core Ops, SparseCore 0:
  10.8 67.9 all-gather.5
  81.5 39.5 all-gather.7
  123.8 78.6 all-gather.9
  205.1 78.0 all-gather.11
  336.5 66.7 reduce-scatter.9
  406.8 162.3 reduce-scatter.11
  572.8 162.3 reduce-scatter.13
  738.9 128.1 reduce-scatter.7
  870.7 60.4 reduce-scatter.15
  934.4 45.5 all-reduce.4
where the time goes:
time: 1000 us; the launch traced here: 994 us
  waiting for transfers between devices  515 us (52%)
  matrix products  202 us (20%)
  local copies, waits for them, and re-layouts  120 us (12%)
  other arithmetic  68.4 us (7%)
  blocking collectives  58.5 us (6%)
  starting transfers between devices  15.1 us (2%)
  between operations  15 us (2%)
    reduce_scatter x1, waiting for transfers between devices, local(): lax.psum_scatter(grad_qkv, 'dp', scatter_dimension=0, tiled=True)  130 us
    reduce_scatter x1, waiting for transfers between devices, local(): lax.psum_scatter(grad_down, 'dp', scatter_dimension=0, tiled=True)  115 us
    all_to_all x1, waiting for transfers between devices, local(): lax.all_to_all(grad_mixed.reshape(seq_count, SEQ, 3, 1, head_cols), 'head...  69.8 us
    unnamed x11, waiting for transfers between devices  57.5 us
    all_to_all x1, waiting for transfers between devices, local(): lax.all_to_all(mixed.reshape(seq_count, part_rows, 3, splits, head_cols),...  52.6 us
    all_gather x1, waiting for transfers between devices, fetch(): lax.all_gather(qkv_weight.astype(jnp.bfloat16), 'dp', axis=0, tiled=True)  41.9 us
    psum x1, waiting for transfers between devices, local(): lax.psum(summed[0].astype(jnp.bfloat16), 'head').astype(jnp.float32)  41.8 us
    dot_general x4, matrix products, contract_cols(): lax.dot_general(left, right, (((1,), (1,)), ((), ())), preferred_element_...  36.4 us
  transfers between devices with their start and end apart: 13, of which 8 were waited for; matrix products, arithmetic and copies ran while one was open for 33% of the time, Pallas kernels for 0%

commit v1 on v0

v1 whole, which is shorter than its diff:
```python
import jax
import jax.numpy as jnp
from jax import lax
from jax.sharding import PartitionSpec as P

HEADS = 12
HEAD_DIM = 64
SEQ = 1024
EPSILON = 1e-05
BOTH = ("dp", "head")


def layer_norm(vector, gain_vec, bias_vec):
    row_mean = jnp.mean(vector, axis=-1, keepdims=True)
    centred = vector - row_mean
    variance = jnp.mean(centred * centred, axis=-1, keepdims=True)
    return centred * lax.rsqrt(variance + EPSILON) * gain_vec + bias_vec


def gelu_tanh(vector):
    return jax.nn.gelu(vector, approximate=True)


def contract_rows(left, right):
    return lax.dot_general(
        left, right, (((0,), (0,)), ((), ())), preferred_element_type=jnp.float32
    )


def contract_cols(left, right):
    return lax.dot_general(
        left, right, (((1,), (1,)), ((), ())), preferred_element_type=jnp.float32
    )


def causal_mask(first_row, row_count, key_count):
    query_pos = first_row + jnp.arange(row_count)[:, None]
    key_pos = jnp.arange(key_count)[None, :]
    return query_pos >= key_pos


def attend_sequence(triple):
    query_rows, key_rows, value_rows = triple
    seq_len = query_rows.shape[0]
    block_rows = min(512, seq_len)
    scaling = query_rows.shape[-1] ** (-0.5)
    out_parts = []
    log_parts = []
    for block_id in range(seq_len // block_rows):
        first_row = block_id * block_rows
        last_row = first_row + block_rows
        raw_scores = (
            jnp.einsum(
                "qhd,khd->hqk",
                query_rows[first_row:last_row],
                key_rows[:last_row],
                preferred_element_type=jnp.float32,
            )
            * scaling
        )
        scores = jnp.where(causal_mask(first_row, block_rows, last_row), raw_scores, -1e30)
        row_max = jnp.max(scores, axis=-1, keepdims=True)
        weights = jnp.exp(scores - row_max)
        row_total = jnp.sum(weights, axis=-1, keepdims=True)
        probs_low = (weights / row_total).astype(jnp.bfloat16)
        out_parts.append(
            jnp.einsum(
                "hqk,khd->qhd", probs_low, value_rows[:last_row], preferred_element_type=jnp.float32
            )
        )
        log_parts.append(row_max + jnp.log(row_total))
    return (jnp.concatenate(out_parts, axis=0), jnp.concatenate(log_parts, axis=1))


def sequence_grads(bundle):
    query_rows, key_rows, value_rows, log_totals, grad_rows = bundle
    seq_len = query_rows.shape[0]
    block_rows = min(512, seq_len)
    scaling = query_rows.shape[-1] ** (-0.5)
    query_parts = []
    grad_keys = jnp.zeros(key_rows.shape, jnp.float32)
    grad_values = jnp.zeros(value_rows.shape, jnp.float32)
    for block_id in range(seq_len // block_rows):
        first_row = block_id * block_rows
        last_row = first_row + block_rows
        query_block = query_rows[first_row:last_row]
        key_part = key_rows[:last_row]
        grad_block = grad_rows[first_row:last_row]
        raw_scores = (
            jnp.einsum("qhd,khd->hqk", query_block, key_part, preferred_element_type=jnp.float32)
            * scaling
        )
        scores = jnp.where(causal_mask(first_row, block_rows, last_row), raw_scores, -1e30)
        probs = jnp.exp(scores - log_totals[:, first_row:last_row])
        probs_low = probs.astype(jnp.bfloat16)
        grad_probs = jnp.einsum(
            "qhd,khd->hqk", grad_block, value_rows[:last_row], preferred_element_type=jnp.float32
        )
        grad_values = grad_values.at[:last_row].add(
            jnp.einsum("hqk,qhd->khd", probs_low, grad_block, preferred_element_type=jnp.float32)
        )
        centre = jnp.sum(probs * grad_probs, axis=-1, keepdims=True)
        grad_scores = (probs * (grad_probs - centre)).astype(jnp.bfloat16)
        query_parts.append(
            jnp.einsum("hqk,khd->qhd", grad_scores, key_part, preferred_element_type=jnp.float32)
            * scaling
        )
        grad_keys = grad_keys.at[:last_row].add(
            jnp.einsum("hqk,qhd->khd", grad_scores, query_block, preferred_element_type=jnp.float32)
            * scaling
        )
    return (jnp.concatenate(query_parts, axis=0), grad_keys, grad_values)


def to_sequences(rows):
    return lax.all_to_all(rows, "head", split_axis=0, concat_axis=1, tiled=True)


def to_positions(rows):
    return lax.all_to_all(rows, "head", split_axis=1, concat_axis=0, tiled=True)


def gather(shard, splits):
    share = shard.shape[0] // splits
    mine = lax.dynamic_slice_in_dim(shard, lax.axis_index("head") * share, share, 0)
    return lax.all_gather(mine.astype(jnp.bfloat16), BOTH, axis=0, tiled=True)


def scatter(total):
    part = lax.psum_scatter(total.astype(jnp.bfloat16), BOTH, scatter_dimension=0, tiled=True)
    return lax.all_gather(part, "head", axis=0, tiled=True).astype(jnp.float32)


def local(
    tokens,
    qkv_weight,
    proj_weight,
    up_weight,
    down_weight,
    attn_gain,
    attn_bias,
    ffn_gain,
    ffn_bias,
    cotangent,
):
    splits = lax.axis_size("head")
    model_width = tokens.shape[-1]
    norm_table = jnp.stack([attn_gain, attn_bias, ffn_gain, ffn_bias], axis=1)
    first = gather(jnp.concatenate([qkv_weight, norm_table], axis=1), splits)
    full_qkv = first[:, : 3 * model_width]
    table = first[:, 3 * model_width :].astype(jnp.float32)
    own_tokens = to_sequences(tokens)
    own_cot = to_sequences(cotangent)
    full_proj = gather(proj_weight, splits)
    full_up = gather(up_weight, splits)
    full_down = gather(down_weight, splits)
    seq_count = own_tokens.shape[0]
    tok_rows = seq_count * SEQ
    inputs = own_tokens.astype(jnp.float32).reshape(tok_rows, model_width)
    normed, norm_pull = jax.vjp(layer_norm, inputs, table[:, 0], table[:, 1])
    normed_low = normed.astype(jnp.bfloat16)
    mixed = jnp.dot(normed_low, full_qkv, preferred_element_type=jnp.float32).astype(jnp.bfloat16)
    mixed = mixed.reshape(seq_count, SEQ, 3, HEADS, HEAD_DIM)
    queries, key_rows, value_rows = mixed[:, :, 0], mixed[:, :, 1], mixed[:, :, 2]
    attended, log_totals = lax.map(attend_sequence, (queries, key_rows, value_rows))
    token_heads = attended.astype(jnp.bfloat16).reshape(tok_rows, model_width)
    middle = inputs + jnp.dot(token_heads, full_proj, preferred_element_type=jnp.float32)
    normed_two, norm_pull_two = jax.vjp(layer_norm, middle, table[:, 2], table[:, 3])
    second_low = normed_two.astype(jnp.bfloat16)
    hidden = jnp.dot(second_low, full_up, preferred_element_type=jnp.float32)
    active, gelu_pull = jax.vjp(gelu_tanh, hidden)
    active_low = active.astype(jnp.bfloat16)
    output = (middle + jnp.dot(active_low, full_down, preferred_element_type=jnp.float32)).astype(
        jnp.bfloat16
    )
    out_home = to_positions(output.reshape(seq_count, SEQ, model_width))
    flat_cot = own_cot.reshape(tok_rows, model_width)
    grad_down = contract_rows(active_low, flat_cot)
    (grad_active,) = gelu_pull(contract_cols(flat_cot, full_down))
    grad_hidden = grad_active.astype(jnp.bfloat16)
    grad_up = contract_rows(second_low, grad_hidden)
    grad_second, grad_ffn_gain, grad_ffn_bias = norm_pull_two(contract_cols(grad_hidden, full_up))
    grad_middle = flat_cot.astype(jnp.float32) + grad_second
    grad_branch = grad_middle.astype(jnp.bfloat16)
    grad_proj = contract_rows(token_heads, grad_branch)
    grad_heads = contract_cols(grad_branch, full_proj).astype(jnp.bfloat16)
    grad_attended = grad_heads.reshape(seq_count, SEQ, HEADS, HEAD_DIM)
    grad_query, grad_keys, grad_values = lax.map(
        sequence_grads, (queries, key_rows, value_rows, log_totals, grad_attended)
    )
    back_mixed = (
        jnp.stack([grad_query, grad_keys, grad_values], axis=2)
        .astype(jnp.bfloat16)
        .reshape(tok_rows, 3 * model_width)
    )
    grad_qkv = contract_rows(normed_low, back_mixed)
    grad_normed, grad_attn_gain, grad_attn_bias = norm_pull(contract_cols(back_mixed, full_qkv))
    grad_tokens = (grad_middle + grad_normed).reshape(seq_count, SEQ, model_width)
    grad_home = to_positions(grad_tokens.astype(jnp.bfloat16)).astype(jnp.float32)
    grad_table = jnp.stack([grad_attn_gain, grad_attn_bias, grad_ffn_gain, grad_ffn_bias], axis=1)
    shard_down = scatter(grad_down)
    shard_up = scatter(grad_up)
    shard_proj = scatter(grad_proj)
    shard_first = scatter(jnp.concatenate([grad_qkv, grad_table], axis=1))
    shard_table = shard_first[:, 3 * model_width :]
    return (
        out_home,
        grad_home,
        shard_first[:, : 3 * model_width],
        shard_proj,
        shard_up,
        shard_down,
        shard_table[:, 0],
        shard_table[:, 1],
        shard_table[:, 2],
        shard_table[:, 3],
    )


def solution(mesh):
    rows = P("dp", "head", None)
    placed = (rows,) + (P("dp", None),) * 4 + (P("dp"),) * 4 + (rows,)
    return jax.shard_map(
        local,
        mesh=mesh,
        in_specs=placed,
        out_specs=(rows, rows) + (P("dp", None),) * 4 + (P("dp"),) * 4,
        check_vma=False,
    )
```

time: 1000 us -> 789 us (0.79)
  waiting for transfers between devices: 515 us -> 337 us
  local copies, waits for them, and re-layouts: 120 us -> 88.8 us
  blocking collectives: 58.5 us -> 28.2 us
  other arithmetic: 68.4 us -> 92.7 us
    all_to_all x3 -> x4, waiting for transfers between devices: 129 us -> 54.6 us  [the longest x2 42.3 us: to_sequences(): return lax.all_to_all(rows, 'head', split_axis=0, concat_axis=1, tiled=True)]
    reduce_scatter x4 -> x3, waiting for transfers between devices: 245 us -> 178 us  [scatter(): lax.psum_scatter(total.astype(jnp.bfloat16), BOTH, scatter_dimension=0, t...]
    all_gather x4, waiting for transfers between devices: 41.9 us -> 104 us  [gather(): return lax.all_gather(mine.astype(jnp.bfloat16), BOTH, axis=0, tiled=True)]
    unnamed x11 -> x9, waiting for transfers between devices: 57.5 us -> 0.14 us
    all_to_all x7 -> x0, local copies, waits for them, and re-layouts: 43.5 us -> none  [the longest x2 17.2 us: local(): lax.all_to_all(grad_mixed.reshape(seq_count, SEQ, 3, 1, head_cols), 'head...]
    psum x1 -> x0, waiting for transfers between devices: 41.8 us -> none  [local(): lax.psum(summed[0].astype(jnp.bfloat16), 'head').astype(jnp.float32)]
    all_to_all x1 -> x0, blocking collectives: 30.5 us -> none  [local(): lax.all_to_all(attended_low, 'head', split_axis=1, concat_axis=2, tiled=T...]
    reshape x5 -> x2, local copies, waits for them, and re-layouts: 34.4 us -> 8.52 us  [the longest x1 5.95 us: local(): out_home = to_positions(output.reshape(seq_count, SEQ, model_width))]
  transfers between devices with their start and end apart: 13 -> 12, of which waited for: 8 -> 8; matrix products, arithmetic and copies ran while one was open for 33% -> 38% of each run, Pallas kernels for 0% -> 0%
where the time goes in v1:
time: 789 us; the launch traced here: 778 us
  waiting for transfers between devices  337 us (43%)
  matrix products  199 us (25%)
  other arithmetic  92.7 us (12%)
  local copies, waits for them, and re-layouts  88.8 us (11%)
  blocking collectives  28.2 us (4%)
  starting transfers between devices  17.4 us (2%)
  between operations  15.3 us (2%)
    reduce_scatter x3, waiting for transfers between devices, scatter(): lax.psum_scatter(total.astype(jnp.bfloat16), BOTH, scatter_dimension=0, t...  178 us
    all_gather x4, waiting for transfers between devices, gather(): return lax.all_gather(mine.astype(jnp.bfloat16), BOTH, axis=0, tiled=True)  104 us
    all_to_all x2, waiting for transfers between devices, to_sequences(): return lax.all_to_all(rows, 'head', split_axis=0, concat_axis=1, tiled=True)  42.3 us
    unnamed x81, local copies, waits for them, and re-layouts  36.5 us
    dot_general x4, matrix products, contract_cols(): lax.dot_general(left, right, (((1,), (1,)), ((), ())), preferred_element_...  30.7 us
    dot_general x4, matrix products, contract_rows(): lax.dot_general(left, right, (((0,), (0,)), ((), ())), preferred_element_...  30.1 us
    convert_element_type x2, other arithmetic, sequence_grads(): grad_scores = (probs * (grad_probs - centre)).astype(jnp.bfloat16)  29.2 us
    all_gather x4, blocking collectives, scatter(): return lax.all_gather(part, 'head', axis=0, tiled=True).astype(jnp.float32)  28.2 us
  transfers between devices with their start and end apart: 12, of which 8 were waited for; matrix products, arithmetic and copies ran while one was open for 38% of the time, Pallas kernels for 0%

profile of v1, /device:TPU:0, one launch (start us, length us, event | category | flops | bytes accessed | tf_op | source)
XLA Modules:
  0.0 778.2 jit_solution(7582826896106223531)
XLA Ops:
  20.7 19.2 %all-to-all-done = bf16[4,256,768]{2,1,0:T(8,128)(2,1)S(1)} async-done(((bf16[4,256,768]{2,1,0:T(8,128)(2,1)}), bf16[4,256,768]{2,1,0:T(8,128)(2,1)S(1)}, u32[]{:S(2)}, u32[]{:S(2)}) %all-to-all-start) | async-done | bytes 1572896 | tf_op jit(solution)/shard_map/all_to_all | solution.py:116
  45.6 23.1 %all-to-all-done.2 = bf16[4,256,768]{2,1,0:T(8,128)(2,1)} async-done(((bf16[4,256,768]{2,1,0:T(8,128)(2,1)}), bf16[4,256,768]{2,1,0:T(8,128)(2,1)}, u32[]{:S(2)}, u32[]{:S(2)}) %all-to-all-start.2) | async-done | bytes 1572896 | tf_op jit(solution)/shard_map/all_to_all | solution.py:116
  73.4 7.1 all-gather.5.cloned.1.call-done
  82.3 9.2 %convolution_convert_fusion = bf16[1024,2304]{1,0:T(8,128)(2,1)} fusion(bf16[768,2308]{1,0:T(8,128)(2,1)} %all-gather.5.cloned.1.call-done, f32[1024,768]{0,1:T(8,128)} %copy.119, f32[768]{0:T(1024)S(1)} %get-tuple-element.169, f32[768]{0:T(1024)S(1)} %get-tuple-element.170, f32[1024]{0:T(1024)S(1)} %rsqrt.23, f32[1024]{0:T(1024)S(1)} %bitcast.156), kind=kOutput, calls=%fused_computation.39 | convolution fusion | flops 3630170112 | bytes 11417600 | tf_op jit(solution)/shard_map/dot_general | solution.py:162
  111.8 14.4 %fusion.18 = (f32[12,512]{1,0:T(8,128)S(1)}, f32[12,512,1024]{2,1,0:T(8,128)}) fusion(pred[512,1024]{1,0:T(8,128)(4,1)S(1)} %iota_compare_fusion, bf16[1,1024,3,12,64]{1,4,3,2,0:T(8,128)(2,1)} %bitcast.132), kind=kOutput, calls=%fused_computation.35 | convolution fusion | flops 824174592 | bytes 28073984 | tf_op jit(solution)/shard_map/while/body/eval_jaxpr/qhd,khd->hqk/dot_general | solution.py:53
  126.3 12.4 %fusion = f32[12,512]{1,0:T(8,128)S(1)} fusion(f32[12,512]{1,0:T(8,128)S(1)} %get-tuple-element.179, f32[12,512,1024]{2,1,0:T(8,128)} %get-tuple-element.180, pred[512,1024]{1,0:T(8,128)(4,1)S(1)} %iota_compare_fusion), kind=kLoop, calls=%fused_computation.6 | loop fusion | flops 25159680 | bytes 25739264 | tf_op jit(solution)/shard_map/while/body/eval_jaxpr/reduce_sum | solution.py:64
  141.8 10.3 %fusion.42 = bf16[12,64,512]{2,1,0:T(8,128)(2,1)} fusion(f32[12,512]{1,0:T(8,128)S(1)} %fusion, f32[12,512]{1,0:T(8,128)S(1)} %get-tuple-element.179, f32[12,512,1024]{2,1,0:T(8,128)S(1)} %copy-done.2, pred[512,1024]{1,0:T(8,128)(4,1)S(1)} %iota_compare_fusion, bf16[1,1024,3,12,64]{1,4,3,2,0:T(8,128)(2,1)} %bitcast.133), kind=kOutput, calls=%fused_computation.86 | convolution fusion | flops 837156864 | bytes 28098560 | tf_op jit(solution)/shard_map/while/body/eval_jaxpr/hqk,khd->qhd/dot_general | solution.py:67
  160.5 42.4 %all-gather.9.cloned.1.call-done = bf16[768,3072]{1,0:T(8,128)(2,1)} async-done(((bf16[24,3072]{1,0:T(8,128)(2,1)}), bf16[768,3072]{1,0:T(8,128)(2,1)}) %all-gather.9.cloned.1.call-update) | async-done | bytes 4718608 | tf_op jit(solution)/shard_map/all_gather | solution.py:126
  202.9 11.0 %fusion.62 = f32[1024,3072]{1,0:T(8,128)} fusion(bf16[768,3072]{1,0:T(8,128)(2,1)} %all-gather.9.cloned.1.call-done, f32[1024,768]{0,1:T(8,128)} %copy-done.4, f32[768]{0:T(1024)S(1)} %get-tuple-element.168, f32[768]{0:T(1024)S(1)} %get-tuple-element.167, f32[1024]{0:T(1024)S(1)} %fusion.47, f32[1024]{0:T(1024)S(1)} %broadcast_multiply_fusion), kind=kOutput, calls=%fused_computation.135 | convolution fusion | flops 4835770368 | bytes 20461568 | tf_op jit(solution)/shard_map/dot_general | solution.py:170
  214.0 54.8 %all-gather.11.cloned.1.call-done = bf16[3072,768]{1,0:T(8,128)(2,1)} async-done(((bf16[96,768]{1,0:T(8,128)(2,1)}), bf16[3072,768]{1,0:T(8,128)(2,1)}) %all-gather.11.cloned.1.call-update) | async-done | bytes 4718608 | tf_op jit(solution)/shard_map/all_gather | solution.py:126
  268.7 15.6 %fusion.8 = bf16[1024,3072]{1,0:T(8,128)(2,1)S(1)} fusion(f32[1024,3072]{1,0:T(8,128)} %fusion.62, bf16[3072,768]{1,0:T(8,128)(2,1)} %all-gather.11.cloned.1.call-done, bf16[1024,768]{1,0:T(8,128)(2,1)} %bitcast.17), kind=kOutput, calls=%fused_computation.16 | convolution fusion | flops 4894752768 | bytes 25165824 | tf_op jit(solution)/shard_map/dot_general | solution.py:31
  284.4 6.7 fusion.67
  309.1 7.9 %fusion.38 = f32[512,12,64]{0,2,1:T(8,128)} fusion(bf16[512,12,64]{0,2,1:T(8,128)(2,1)S(1)} %bitcast.149, f32[12,512]{1,0:T(8,128)S(1)} %log_add_fusion.1, f32[12,512,512]{1,2,0:T(8,128)} %copy-done.3, pred[512,512]{0,1:T(8,128)(4,1)S(1)} %iota_compare_fusion.1), kind=kOutput, calls=%fused_computation.84 | convolution fusion | flops 415236096 | bytes 15228928 | tf_op jit(solution)/shard_map/while/body/eval_jaxpr/hqk,qhd->khd/dot_general | solution.py:100
  317.0 8.0 %multiply_reduce_fusion.1 = (f32[12,512]{1,0:T(8,128)S(1)}, f32[12,512,512]{1,2,0:T(8,128)}) fusion(f32[12,512]{1,0:T(8,128)S(1)} %log_add_fusion.1, f32[12,512,512]{1,2,0:T(8,128)S(1)} %bitcast.129, pred[512,512]{0,1:T(8,128)(4,1)S(1)} %iota_compare_fusion.1, bf16[512,12,64]{0,2,1:T(8,128)(2,1)S(1)} %bitcast.150, bf16[1,1024,3,12,64]{1,4,3,2,0:T(8,128)(2,1)} %bitcast.134), kind=kOutput, calls=%fused_computation.25 | convolution fusion | flops 418375680 | bytes 27049984 | tf_op jit(solution)/shard_map/while/body/eval_jaxpr/qhd,khd->hqk/dot_general | solution.py:96
  325.0 7.2 multiply_convert_fusion.1
  337.7 18.1 %multiply_reduce_fusion = (f32[12,512]{1,0:T(8,128)S(1)}, f32[12,512,1024]{2,1,0:T(8,128)}) fusion(f32[12,512]{1,0:T(8,128)S(1)} %log_add_fusion, f32[12,512,1024]{2,1,0:T(8,128)} %get-tuple-element.180, pred[512,1024]{1,0:T(8,128)(4,1)S(1)} %iota_compare_fusion, bf16[512,12,64]{0,2,1:T(8,128)(2,1)} %bitcast.152, bf16[1,1024,3,12,64]{1,4,3,2,0:T(8,128)(2,1)} %bitcast.137), kind=kOutput, calls=%fused_computation.1 | convolution fusion | flops 836757504 | bytes 53264384 | tf_op jit(solution)/shard_map/while/body/eval_jaxpr/qhd,khd->hqk/dot_general | solution.py:96
  355.8 13.8 %fusion.24 = bf16[1,1024,1,12,64]{1,4,3,2,0:T(8,128)(2,1)} fusion(f32[512,12,64]{0,2,1:T(8,128)} %fusion.38, bf16[512,12,64]{0,2,1:T(8,128)(2,1)} %bitcast.153, f32[12,512]{1,0:T(8,128)S(1)} %log_add_fusion, f32[12,512,1024]{2,1,0:T(8,128)} %get-tuple-element.180, pred[512,1024]{1,0:T(8,128)(4,1)S(1)} %iota_compare_fusion), kind=kOutput, calls=%fused_computation.48 | convolution fusion | flops 832045056 | bytes 29646848 | tf_op jit(solution)/shard_map/while/body/eval_jaxpr/hqk,qhd->khd/dot_general | solution.py:100
  369.6 22.0 %multiply_convert_fusion = bf16[12,512,1024]{2,1,0:T(8,128)(2,1)} fusion(f32[12,512,1024]{2,1,0:T(8,128)} %get-tuple-element.188, f32[12,512]{1,0:T(8,128)S(1)} %get-tuple-element.187, f32[12,512]{1,0:T(8,128)S(1)} %log_add_fusion, f32[12,512,1024]{2,1,0:T(8,128)} %get-tuple-element.180, pred[512,1024]{1,0:T(8,128)(4,1)S(1)} %iota_compare_fusion), kind=kLoop, calls=%fused_computation | loop fusion | flops 37748736 | bytes 63488000 | tf_op jit(solution)/shard_map/while/body/eval_jaxpr/convert_element_type | solution.py:103
  391.6 8.6 %multiply_bitcast_fusion.1 = bf16[512,12,64]{0,2,1:T(8,128)(2,1)S(1)} fusion(bf16[12,512,1024]{2,1,0:T(8,128)(2,1)} %multiply_convert_fusion, bf16[1,1024,3,12,64]{1,4,3,2,0:T(8,128)(2,1)S(1)} %bitcast.140), kind=kOutput, calls=%fused_computation.76 | convolution fusion | flops 806092800 | bytes 14942208 | tf_op jit(solution)/shard_map/while/body/eval_jaxpr/hqk,khd->qhd/dot_general | solution.py:105
  400.3 7.0 fusion.25
  440.8 9.8 %convolution_convert_fusion.2 = bf16[768,3072]{1,0:T(8,128)(2,1)} fusion(bf16[1024,3072]{1,0:T(8,128)(2,1)} %copy-done.30, f32[1024,768]{0,1:T(8,128)} %copy-done.4, f32[768]{0:T(1024)S(1)} %copy-done.18, f32[768]{0:T(1024)S(1)} %get-tuple-element.167, f32[1024]{0:T(1024)S(1)} %fusion.47, f32[1024]{0:T(1024)S(1)} %broadcast_multiply_fusion), kind=kOutput, calls=%fused_computation.41 | convolution fusion | flops 4838129664 | bytes 14170112 | tf_op jit(solution)/shard_map/dot_general | solution.py:25
  450.7 12.3 %convolution_convert_fusion.1 = bf16[3072,768]{1,0:T(8,128)(2,1)} fusion(bf16[1024,768]{1,0:T(8,128)(2,1)} %bitcast.17, f32[1024,3072]{1,0:T(8,128)} %fusion.62), kind=kOutput, calls=%fused_computation.40 | convolution fusion | flops 4862509056 | bytes 18874368 | tf_op jit(solution)/shard_map/dot_general | solution.py:25
  463.0 11.1 %fusion.37 = bf16[1,1024,768]{1,2,0:T(8,128)(2,1)S(1)} fusion(f32[1024,768]{0,1:T(8,128)} %copy-done.4, bf16[3072,768]{1,0:T(8,128)(2,1)} %all-gather.11.cloned.1.call-done, f32[1024,3072]{1,0:T(8,128)} %fusion.62), kind=kOutput, calls=%fused_computation.83 | convolution fusion | flops 4861722624 | bytes 22020096 | tf_op jit(solution)/shard_map/dot_general | solution.py:173
  480.6 12.6 %reduce.34 = bf16[1024,768]{1,0:T(8,128)(2,1)} reduce(bf16[1024,1,768]{2,1,0:T(2,128)(2,1)} %bitcast.143, bf16[]{:T(256)} %broadcast.386), dimensions={1}, to_apply=%bitcast.91.reduce_sub_computation | reduce | bytes 3145730
  508.2 8.3 %copy.106 = bf16[1,1024,768]{2,0,1:T(2,128)(2,1)} copy(bf16[1,1024,768]{1,2,0:T(8,128)(2,1)} %fusion.32) | data formatting | bytes 3145728 | tf_op jit(solution)/shard_map/convert_element_type | solution.py:199
  516.5 11.2 %reduce.35 = bf16[1024,768]{1,0:T(8,128)(2,1)S(1)} reduce(bf16[1024,1,768]{2,1,0:T(2,128)(2,1)} %bitcast.144, bf16[]{:T(256)} %broadcast.386), dimensions={1}, to_apply=%bitcast.89.reduce_sub_computation | reduce | bytes 3145730
  541.2 12.3 %all-to-all-done.3 = bf16[4,2,98304]{2,1,0:T(2,128)(2,1)S(1)} async-done(((bf16[4,2,98304]{2,1,0:T(2,128)(2,1)}), bf16[4,2,98304]{2,1,0:T(2,128)(2,1)S(1)}, u32[]{:S(2)}, u32[]{:S(2)}) %all-to-all-start.3) | async-done | bytes 1572896 | tf_op jit(solution)/shard_map/all_to_all | solution.py:120
  566.6 7.2 all_gather.28
  575.5 74.1 %reduce-scatter.9.cloned.1.call-done = bf16[24,3072]{1,0:T(8,128)(2,1)} async-done(((bf16[768,3072]{1,0:T(8,128)(2,1)}), bf16[24,3072]{1,0:T(8,128)(2,1)}) %reduce-scatter.9.cloned.1.call-update) | async-done | bytes 147472 | tf_op jit(solution)/shard_map/reduce_scatter | solution.py:130
  649.6 7.7 all_gather.30
  658.4 103.7 %reduce-scatter.11.cloned.1.call-done = bf16[96,768]{1,0:T(8,128)(2,1)} async-done(((bf16[3072,768]{1,0:T(8,128)(2,1)}), bf16[96,768]{1,0:T(8,128)(2,1)}) %reduce-scatter.11.cloned.1.call-update) | async-done | bytes 147472 | tf_op jit(solution)/shard_map/reduce_scatter | solution.py:130
  762.1 7.7 all_gather.31
  (173 shorter events, 166.0 us)
Async XLA Ops:
  7.2 6.8 copy-start
  7.2 73.3 %all-gather.5.cloned.1.call-start = ((), (), s32[]{:S(2)}) async-start(), calls=%async_computation.8 | async-start | bytes 3852288 | tf_op jit(solution)/shard_map/all_gather | solution.py:126
  12.4 139.7 %all-gather.7.cloned.1.call-start = ((), (), s32[]{:S(2)}) async-start(), calls=%async_computation.9 | async-start | bytes 1216512 | tf_op jit(solution)/shard_map/all_gather | solution.py:126
  14.0 188.9 %all-gather.9.cloned.1.call-start = ((), (), s32[]{:S(2)}) async-start(), calls=%async_computation.10 | async-start | bytes 4866048 | tf_op jit(solution)/shard_map/all_gather | solution.py:126
  14.7 25.1 %all-to-all-start = ((bf16[4,256,768]{2,1,0:T(8,128)(2,1)}), bf16[4,256,768]{2,1,0:T(8,128)(2,1)S(1)}, u32[]{:S(2)}, u32[]{:S(2)}) async-start(bf16[4,256,768]{2,1,0:T(8,128)(2,1)} %param.22), calls=%async_computation | async-start | bytes 3145728 | tf_op jit(solution)/shard_map/all_to_all | solution.py:116
  18.9 249.8 %all-gather.11.cloned.1.call-start = ((), (), s32[]{:S(2)}) async-start(), calls=%async_computation.11 | async-start | bytes 4866048 | tf_op jit(solution)/shard_map/all_gather | solution.py:126
  39.9 28.9 %all-to-all-start.2 = ((bf16[4,256,768]{2,1,0:T(8,128)(2,1)}), bf16[4,256,768]{2,1,0:T(8,128)(2,1)}, u32[]{:S(2)}, u32[]{:S(2)}) async-start(bf16[4,256,768]{2,1,0:T(8,128)(2,1)} %param.31), calls=%async_computation.2 | async-start | bytes 3145728 | tf_op jit(solution)/shard_map/all_to_all | solution.py:116
  44.2 515.9 %reduce-scatter.7.cloned.1.call-start = ((), (), s32[]{:S(2)}) async-start(), calls=%async_computation.12 | async-start | bytes 1216512 | tf_op jit(solution)/shard_map/reduce_scatter | solution.py:130
  45.0 37.3 %copy-start.19 = (f32[1,2,4,128]{3,1,2,0:T(2,128)}, f32[1,2,4,128]{3,1,2,0:T(2,128)S(1)}, u32[]{:S(2)}) copy-start(f32[1,2,4,128]{3,1,2,0:T(2,128)S(1)} %copy.123) | copy-start | bytes 12292
  45.6 27.8 %copy-start.23 = (f32[1,2,4,128]{3,1,2,0:T(2,128)}, f32[1,2,4,128]{3,1,2,0:T(2,128)S(1)}, u32[]{:S(2)}) copy-start(f32[1,2,4,128]{3,1,2,0:T(2,128)S(1)} %copy.124) | copy-start | bytes 12292
  45.6 36.7 %copy-start.21 = (f32[1024]{0:T(1024)}, f32[1024]{0:T(1024)S(1)}, u32[]{:S(2)}) copy-start(f32[1024]{0:T(1024)S(1)} %rsqrt.23) | copy-start | bytes 12292
  82.3 120.6 %copy-start.17 = (f32[768]{0:T(1024)}, f32[768]{0:T(1024)S(1)}, u32[]{:S(2)}) copy-start(f32[768]{0:T(1024)S(1)} %get-tuple-element.168) | copy-start | bytes 9220
  126.3 15.5 %copy-start.2 = (f32[12,512,1024]{2,1,0:T(8,128)S(1)}, f32[12,512,1024]{2,1,0:T(8,128)}, u32[]{:S(2)}) copy-start(f32[12,512,1024]{2,1,0:T(8,128)} %get-tuple-element.180) | copy-start | bytes 75497472
  268.7 15.7 %copy-start.12 = (bf16[768,3072]{1,0:T(8,128)(2,1)S(1)}, bf16[768,3072]{1,0:T(8,128)(2,1)}, u32[]{:S(2)}) copy-start(bf16[768,3072]{1,0:T(8,128)(2,1)} %all-gather.9.cloned.1.call-done) | copy-start | bytes 14155780
  284.4 6.7 copy-start.30
  300.2 5.0 copy-start.25
  305.3 11.7 %slice-start = ((s8[12582912]{0:T(1024)(128)(4,1)}), s8[4194304]{0:T(1024)(128)(4,1)S(1)}, s32[]{:S(2)}) async-start(s8[12582912]{0:T(1024)(128)(4,1)} %bitcast.128), calls=%async_computation.16 | async-start | bytes 8388608
  308.1 8.9 %slice-start.1 = ((s8[12582912]{0:T(1024)(128)(4,1)}), s8[4194304]{0:T(1024)(128)(4,1)S(1)}, s32[]{:S(2)}) async-start(s8[12582912]{0:T(1024)(128)(4,1)} %bitcast.128), calls=%async_computation.17 | async-start | bytes 8388608
  309.1 7.9 %slice-start.2 = ((s8[12582912]{0:T(1024)(128)(4,1)}), s8[4194304]{0:T(1024)(128)(4,1)S(1)}, s32[]{:S(2)}) async-start(s8[12582912]{0:T(1024)(128)(4,1)} %bitcast.128), calls=%async_computation.18 | async-start | bytes 8388608
  337.6 229.0 %reduce-scatter.13.cloned.1.call-start = ((), (), s32[]{:S(2)}) async-start(), calls=%async_computation.15 | async-start | bytes 3852288
  355.8 35.8 %slice-start.3 = ((s8[4718592]{0:T(1024)(128)(4,1)}), s8[4194304]{0:T(1024)(128)(4,1)S(1)}, s32[]{:S(2)}) async-start(s8[4718592]{0:T(1024)(128)(4,1)} %bitcast.138), calls=%async_computation.19 | async-start | bytes 8388608
  369.6 22.0 %slice-start.4 = ((s8[4718592]{0:T(1024)(128)(4,1)}), s8[524288]{0:T(1024)(128)(4,1)S(1)}, s32[]{:S(2)}) async-start(s8[4718592]{0:T(1024)(128)(4,1)} %bitcast.138), calls=%async_computation.20 | async-start | bytes 1048576
  409.2 8.5 %copy-start.13 = (bf16[1,1024,3,12,64]{1,4,3,2,0:T(8,128)(2,1)}, bf16[1,1024,3,12,64]{1,4,3,2,0:T(8,128)(2,1)S(1)}, u32[]{:S(2)}) copy-start(bf16[1,1024,3,12,64]{1,4,3,2,0:T(8,128)(2,1)S(1)} %maximum_convert_fusion) | copy-start | bytes 14155780
  421.3 4.7 copy-start.7
  421.3 4.7 copy-start.22
  440.2 209.4 %reduce-scatter.9.cloned.1.call-start = ((), (), s32[]{:S(2)}) async-start(), calls=%async_computation.13 | async-start | bytes 4866048 | tf_op jit(solution)/shard_map/reduce_scatter | solution.py:130
  450.6 311.5 %reduce-scatter.11.cloned.1.call-start = ((), (), s32[]{:S(2)}) async-start(), calls=%async_computation.14 | async-start | bytes 4866048 | tf_op jit(solution)/shard_map/reduce_scatter | solution.py:130
  493.2 8.5 %copy-start.11 = (bf16[1024,768]{0,1:T(8,128)(2,1)S(1)}, bf16[1024,768]{0,1:T(8,128)(2,1)}, u32[]{:S(2)}) copy-start(bf16[1024,768]{0,1:T(8,128)(2,1)} %copy.120) | copy-start | bytes 4718596
  493.2 8.5 %copy-start.26 = (f32[1024]{0:T(1024)S(1)}, f32[1024]{0:T(1024)}, u32[]{:S(2)}) copy-start(f32[1024]{0:T(1024)} %copy-done.25) | copy-start | bytes 12292
  497.1 32.6 %all-to-all-start.1 = ((bf16[4,2,98304]{2,1,0:T(2,128)(2,1)}), bf16[4,2,98304]{2,1,0:T(2,128)(2,1)}, u32[]{:S(2)}, u32[]{:S(2)}) async-start(bf16[4,2,98304]{2,1,0:T(2,128)(2,1)} %reshape.460), calls=%async_computation.1 | async-start | bytes 3145728 | tf_op jit(solution)/shard_map/all_to_all | solution.py:120
  529.6 23.9 %all-to-all-start.3 = ((bf16[4,2,98304]{2,1,0:T(2,128)(2,1)}), bf16[4,2,98304]{2,1,0:T(2,128)(2,1)S(1)}, u32[]{:S(2)}, u32[]{:S(2)}) async-start(bf16[4,2,98304]{2,1,0:T(2,128)(2,1)} %reshape.458), calls=%async_computation.3 | async-start | bytes 3145728 | tf_op jit(solution)/shard_map/all_to_all | solution.py:120
  573.8 197.1 %copy-start.1 = (f32[96,3072]{1,0:T(8,128)S(1)}, f32[96,3072]{1,0:T(8,128)}, u32[]{:S(2)}) copy-start(f32[96,3072]{1,0:T(8,128)} %param.25) | copy-start | bytes 3538948
  (16 other events, 47.3 us)
Sparse Core Ops, SparseCore 0:
  12.5 67.9 all-gather.4
  84.0 52.7 all-gather.6
  140.3 62.5 all-gather.8
  206.2 62.4 all-gather.10
  337.7 95.0 reduce-scatter.6
  440.3 97.7 reduce-scatter.12
  543.6 106.0 reduce-scatter.8
  656.0 106.0 reduce-scatter.10

commit v2 on v1

v2 whole, which is shorter than its diff:
```python
import functools

import jax
import jax.numpy as jnp
from jax import lax
from jax.experimental import pallas as pl
from jax.experimental.pallas import tpu as pltpu
from jax.sharding import PartitionSpec as P

HEADS = 12
HEAD_DIM = 64
SEQ = 1024
EPSILON = 1e-05
BOTH = ("dp", "head")
BLOCK = 256
GELU_A = 0.7978845608028654
GELU_B = 0.044715
F32 = jnp.float32
BF16 = jnp.bfloat16


def params(mebi):
    return pltpu.CompilerParams(vmem_limit_bytes=mebi * 2**20)


def dot_nn(left, right):
    return lax.dot_general(left, right, (((1,), (0,)), ((), ())), preferred_element_type=F32)


def dot_nt(left, right):
    return lax.dot_general(left, right, (((1,), (1,)), ((), ())), preferred_element_type=F32)


def dot_tn(left, right):
    return lax.dot_general(left, right, (((0,), (0,)), ((), ())), preferred_element_type=F32)


def cost(micros):
    return pl.CostEstimate(
        flops=int(micros * 1.1e9), bytes_accessed=int(micros * 3e6), transcendentals=0
    )


def whole(*shape):
    return pl.BlockSpec(shape, lambda *_: (0,) * len(shape))


def part_of(pair, which):
    parts, _, count, dim = pair.shape
    return pl.BlockSpec((parts, 1, count, dim), lambda *_: (0, which, 0, 0))


def part_rows(pair, which):
    _, _, count, dim = pair.shape
    return pl.BlockSpec((1, 1, count, dim), lambda i, *_: (i, which, 0, 0))


def rows(count, width):
    return pl.BlockSpec((count, width), lambda i, *_: (i, 0))


def shaped(shape, dtype):
    return jax.ShapeDtypeStruct(shape, dtype)


def normalise(vector):
    centred = vector - jnp.mean(vector, axis=-1, keepdims=True)
    inverse = lax.rsqrt(jnp.mean(centred * centred, axis=-1, keepdims=True) + EPSILON)
    return centred * inverse, inverse


def norm_back(unit, inverse, gain, grad):
    scaled = grad * gain
    return inverse * (
        scaled
        - jnp.mean(scaled, axis=-1, keepdims=True)
        - unit * jnp.mean(scaled * unit, axis=-1, keepdims=True)
    )


def proj_kernel(core_ref, x_ref, am_ref, at_ref, pm_ref, pt_ref, table_ref, mid_ref, low_ref, total):
    half = am_ref.shape[1]
    mine = pl.multiple_of(core_ref[0] * half, half)
    theirs = pl.multiple_of((1 - core_ref[0]) * half, half)
    a_mine, a_theirs = am_ref[...], at_ref[...]
    for place, weight in ((mine, pm_ref), (theirs, pt_ref)):
        total[:, pl.ds(place, half)] = (
            x_ref[0, 0, :, pl.ds(place, half)].astype(F32)
            + dot_nn(a_mine, weight[pl.ds(mine, half), :])
            + dot_nn(a_theirs, weight[pl.ds(theirs, half), :])
        )
    mid_ref[...] = total[...].astype(BF16)
    unit, _ = normalise(total[...])
    low_ref[...] = (unit * table_ref[2:3] + table_ref[3:4]).astype(BF16)


def proj_spec(dim):
    half = dim // 2
    return pl.BlockSpec((dim, half), lambda i, *_: (0, 4))


def project(core, x, a_mine, a_theirs, w_mine, w_theirs, table):
    tok, dim = SEQ, x.shape[-1]
    half = dim // 2
    return pl.pallas_call(
        proj_kernel,
        grid_spec=pltpu.PrefetchScalarGridSpec(
            num_scalar_prefetch=1,
            grid=(tok // BLOCK,),
            in_specs=[part_rows(x, 0), rows(BLOCK, half), rows(BLOCK, half)]
            + [proj_spec(dim), proj_spec(dim), whole(8, dim)],
            out_specs=[rows(BLOCK, dim), rows(BLOCK, dim)],
            scratch_shapes=[pltpu.VMEM((BLOCK, dim), F32)],
        ),
        out_shape=[shaped((tok, dim), BF16), shaped((tok, dim), BF16)],
        compiler_params=params(58),
        cost_estimate=cost(0.01),
    )(core, x, a_mine, a_theirs, w_mine, w_theirs, table)


def middle_kernel(
    core_ref, mid_ref, back_ref, cot_ref, table_ref, pm_ref, pt_ref, am_ref, at_ref,
    grad_ref, gm_ref, gt_ref, wm_ref, wt_ref, norm_ref, heads, branch,
):
    half = am_ref.shape[1]
    step = pl.program_id(0)
    mine = pl.multiple_of(core_ref[0] * half, half)
    theirs = pl.multiple_of((1 - core_ref[0]) * half, half)
    here = pl.ds(pl.multiple_of(step * BLOCK, BLOCK), BLOCK)

    @pl.when(step == 0)
    def _():
        norm_ref[...] = jnp.zeros_like(norm_ref)

    unit, inverse = normalise(mid_ref[...].astype(F32))
    grad = back_ref[...].astype(F32)
    norm_ref[0:1] += jnp.sum(grad * unit, axis=0, keepdims=True)
    norm_ref[1:2] += jnp.sum(grad, axis=0, keepdims=True)
    back = norm_back(unit, inverse, table_ref[2:3], grad)
    grad_ref[...] = (cot_ref[0, 0].astype(F32) + back).astype(BF16)
    branch[here, :half] = grad_ref[:, pl.ds(mine, half)]
    branch[here, half:] = grad_ref[:, pl.ds(theirs, half)]
    heads[here, :half] = am_ref[...]
    heads[here, half:] = at_ref[...]
    for place, out in ((mine, gm_ref), (theirs, gt_ref)):
        out[...] = (
            dot_nt(branch[here, :half], pm_ref[pl.ds(place, half), :])
            + dot_nt(branch[here, half:], pt_ref[pl.ds(place, half), :])
        ).astype(BF16)

    @pl.when(step == pl.num_programs(0) - 1)
    def _():
        for place, start in ((mine, 0), (theirs, half)):
            total = dot_tn(heads[:, start : start + half], branch[...]).astype(BF16)
            wm_ref[pl.ds(place, half), :] = total[:, :half]
            wt_ref[pl.ds(place, half), :] = total[:, half:]


def middle_back(core, middle, back, cot, table, w_mine, w_theirs, a_mine, a_theirs):
    tok, dim = middle.shape
    half = dim // 2
    return pl.pallas_call(
        middle_kernel,
        grid_spec=pltpu.PrefetchScalarGridSpec(
            num_scalar_prefetch=1,
            grid=(tok // BLOCK,),
            in_specs=[rows(BLOCK, dim), rows(BLOCK, dim), part_rows(cot, 1)]
            + [whole(8, dim), proj_spec(dim), proj_spec(dim)]
            + [rows(BLOCK, half)] * 2,
            out_specs=[rows(BLOCK, dim), rows(BLOCK, half), rows(BLOCK, half)]
            + [whole(dim, half), whole(dim, half), whole(8, dim)],
            scratch_shapes=[pltpu.VMEM((tok, dim), BF16)] * 2,
        ),
        out_shape=[shaped((tok, dim), BF16)]
        + [shaped((tok, half), BF16)] * 2
        + [shaped((dim, half), BF16)] * 2
        + [shaped((8, dim), F32)],
        compiler_params=params(58),
        cost_estimate=cost(0.01),
    )(core, middle, back, cot, table, w_mine, w_theirs, a_mine, a_theirs)


def lane_low(count):
    return lax.broadcasted_iota(jnp.int32, (count, 128), 1) < HEAD_DIM


def upper():
    return lax.broadcasted_iota(jnp.int32, (BLOCK, BLOCK), 0) <= lax.broadcasted_iota(
        jnp.int32, (BLOCK, BLOCK), 1
    )


def keep_head(low_lanes, head, value):
    zero = jnp.zeros((), value.dtype)
    return jnp.where(low_lanes, value, zero) if head == 0 else jnp.where(low_lanes, zero, value)


def attend_kernel(first, *refs):
    if first:
        x_ref, w_ref, tail_ref, low_ref, mixed_ref, o_ref, l_ref, table_ref = refs
    else:
        low_ref, w_ref, mixed_ref, o_ref, l_ref = refs
    seq = mixed_ref.shape[0]

    if first:

        @pl.when(pl.program_id(0) == 0)
        def _():
            table_ref[...] = tail_ref[...].astype(F32).T[:8]
            for start in range(0, seq, BLOCK):
                here = pl.ds(start, BLOCK)
                unit, _ = normalise(x_ref[start // BLOCK, 0].astype(F32))
                low_ref[here, :] = (unit * table_ref[0:1] + table_ref[1:2]).astype(BF16)

    mixed_ref[...] = dot_nn(low_ref[...], w_ref[...]).astype(BF16)
    q_ref, k_ref, v_ref = (mixed_ref.at[:, 128 * i : 128 * (i + 1)] for i in range(3))
    low_lanes = lane_low(BLOCK)
    allowed = upper()
    scaling = jnp.asarray(HEAD_DIM**-0.5, BF16)
    tiles = [(block, head) for block in range(seq // BLOCK) for head in range(2)]
    with_ones = jnp.concatenate([v_ref[...], jnp.ones((seq, 128), BF16)], axis=1)

    def score(block, head):
        end = (block + 1) * BLOCK
        queries = keep_head(low_lanes, head, q_ref[block * BLOCK : end, :] * scaling)
        raw = dot_nt(k_ref[:end, :], queries)
        last = jnp.where(allowed, raw[end - BLOCK :, :], -1e30)
        return jnp.concatenate([raw[: end - BLOCK, :], last], axis=0) if block else last

    ahead = 3
    waiting = [score(*tile) for tile in tiles[:ahead]]
    parts = []
    for step, (block, head) in enumerate(tiles):
        end = (block + 1) * BLOCK
        if step + ahead < len(tiles):
            waiting.append(score(*tiles[step + ahead]))
        scores = waiting.pop(0)
        row_max = jnp.max(scores, axis=0, keepdims=True)
        weights = jnp.exp(scores - row_max).astype(BF16)
        summed = dot_tn(weights, with_ones[:end])
        totals = summed[:, 128:]
        parts.append(summed[:, :128] / totals)
        l_ref[0, head : head + 1, block * BLOCK : end] = row_max + jnp.log(totals.T[0:1, :])
        if head == 1:
            o_ref[block * BLOCK : end, :] = jnp.where(low_lanes, parts[-2], parts[-1]).astype(BF16)


def columns(count, width):
    return pl.BlockSpec((count, width), lambda i, *_: (0, i))


def attend(value, weight, pairs, first):
    seq, dim = SEQ, value.shape[-1]
    group = 3 * 128
    tail = pl.BlockSpec((dim, 128), lambda i: (0, 3 * pairs))
    return pl.pallas_call(
        functools.partial(attend_kernel, first),
        grid=(pairs,),
        in_specs=[part_of(value, 0) if first else whole(seq, dim), columns(dim, group)]
        + ([tail] if first else []),
        out_specs=([whole(seq, dim)] if first else [])
        + [columns(seq, group), columns(seq, 128), pl.BlockSpec((1, 2, seq), lambda i: (i, 0, 0))]
        + ([whole(8, dim)] if first else []),
        out_shape=([shaped((seq, dim), BF16)] if first else [])
        + [shaped((seq, pairs * group), BF16), shaped((seq, pairs * 128), BF16)]
        + [shaped((pairs, 2, seq), F32)]
        + ([shaped((8, dim), F32)] if first else []),
        compiler_params=params(58),
        cost_estimate=cost(0.01),
    )(value, weight, *((weight,) if first else ()))


def attend_back_kernel(carry, final, *refs):
    mixed_ref, do_ref, o_ref, l_ref, low_ref, w_ref, *refs = refs
    if carry:
        grad_in, *refs = refs
    if final:
        x_ref, mid_ref, table_ref, norm_two, *refs = refs
    gq_ref, more_ref, *refs = refs
    if final:
        out_ref, norm_ref, *refs = refs
    else:
        grad_ref, *refs = refs
    sum_k, sum_v, both, every = refs
    q_ref, k_ref, v_ref = (mixed_ref.at[:, 128 * i : 128 * (i + 1)] for i in range(3))
    dq_ref, dk_ref, dv_ref = (both.at[:, 128 * i : 128 * (i + 1)] for i in range(3))
    seq = mixed_ref.shape[0]
    step = pl.program_id(0)
    low_lanes = lane_low(BLOCK)
    low_all = lane_low(seq)
    allowed = upper()
    scaling = jnp.asarray(HEAD_DIM**-0.5, BF16)
    head_keys = [keep_head(low_all, head, k_ref[...]) for head in range(2)]
    for block in reversed(range(seq // BLOCK)):
        start, end = block * BLOCK, (block + 1) * BLOCK
        queries = q_ref[start:end, :] * scaling
        grads = do_ref[start:end, :]
        dots = (grads.astype(F32) * o_ref[start:end, :].astype(F32)).T
        add_q = add_k = add_v = None
        for head in range(2):
            q_head = keep_head(low_lanes, head, queries)
            g_head = keep_head(low_lanes, head, grads)
            centre = jnp.sum(dots[HEAD_DIM * head : HEAD_DIM * (head + 1)], axis=0, keepdims=True)
            scores = dot_nt(k_ref[:end, :], q_head)
            probs = jnp.exp(scores - l_ref[0, head : head + 1, start:end])
            last = jnp.where(allowed, probs[start:, :], 0.0)
            probs = jnp.concatenate([probs[:start, :], last], axis=0) if block else last
            grad_probs = dot_nt(v_ref[:end, :], g_head)
            grad_scores = (probs * (grad_probs - centre)).astype(BF16)
            terms = (
                dot_tn(grad_scores, head_keys[head][:end]),
                dot_nn(grad_scores, q_head),
                dot_nn(probs.astype(BF16), g_head),
            )
            if head == 0:
                add_q, add_k, add_v = terms
            else:
                add_q, add_k, add_v = add_q + terms[0], add_k + terms[1], add_v + terms[2]
        dq_ref[start:end, :] = (add_q * HEAD_DIM**-0.5).astype(BF16)
        if end == seq:
            sum_k[...] = add_k
            sum_v[...] = add_v
        else:
            sum_k[:end, :] += add_k
            sum_v[:end, :] += add_v
    dk_ref[...] = sum_k[...].astype(BF16)
    dv_ref[...] = sum_v[...].astype(BF16)

    here = pl.ds(pl.multiple_of(step * 384, 384), 384)
    grad_qkv = dot_tn(low_ref[...], both[...]).astype(BF16)
    every[:, here] = both[...]

    @pl.when(step < pl.num_programs(0) - 1)
    def _():
        gq_ref[:, here] = grad_qkv

    @pl.when(step == pl.num_programs(0) - 1)
    def _():
        more_ref[:, :384] = grad_qkv


    @pl.when(step == pl.num_programs(0) - 1)
    def _():
        if final:
            norm_ref[...] = jnp.zeros_like(norm_ref)
        for start in range(0, seq, BLOCK):
            here = pl.ds(start, BLOCK)
            grad = dot_nt(every[here, :], w_ref[...])
            if carry:
                grad = grad + grad_in[here, :].astype(F32)
            if not final:
                grad_ref[here, :] = grad.astype(BF16)
                continue
            unit, inverse = normalise(x_ref[start // BLOCK, 0].astype(F32))
            norm_ref[0:1] += jnp.sum(grad * unit, axis=0, keepdims=True)
            norm_ref[1:2] += jnp.sum(grad, axis=0, keepdims=True)
            back = norm_back(unit, inverse, table_ref[0:1], grad)
            out_ref[here, :] = (mid_ref[here, :].astype(F32) + back).astype(BF16)
        tail = jnp.zeros((128, low_ref.shape[1]), F32)
        if final:
            tail = jnp.concatenate([norm_ref[:2], norm_two[:2], tail[4:]], axis=0)
        more_ref[:, 384:] = tail.T.astype(BF16)


def attend_back(mixed, grad, attended, logs, low, weight, start, pairs, carry=None, final=()):
    seq, dim = low.shape
    group = 3 * 128

    def column(width):
        return pl.BlockSpec((seq, width), lambda i: (0, start + i))

    more = [whole(seq, dim)] if carry is not None else []
    more += [part_of(final[0], 0), whole(seq, dim), whole(8, dim), whole(8, dim)] if final else []
    wide = pairs * group
    widths = [wide - group, group + 128]
    return pl.pallas_call(
        functools.partial(attend_back_kernel, carry is not None, bool(final)),
        grid=(pairs,),
        in_specs=[column(group), column(128), column(128)]
        + [pl.BlockSpec((1, 2, seq), lambda i: (start + i, 0, 0)), whole(seq, dim)]
        + [pl.BlockSpec((dim, wide), lambda i: (0, start // pairs))]
        + more,
        out_specs=[whole(dim, width) for width in widths]
        + [whole(seq, dim)]
        + ([whole(8, dim)] if final else []),
        out_shape=[shaped((dim, width), BF16) for width in widths]
        + [shaped((seq, dim), BF16)]
        + ([shaped((8, dim), F32)] if final else []),
        scratch_shapes=[pltpu.VMEM((seq, 128), F32)] * 2
        + [pltpu.VMEM((seq, group), BF16), pltpu.VMEM((seq, wide), BF16)],
        compiler_params=params(58),
        cost_estimate=cost(0.01),
    )(mixed, grad, attended, logs, low, weight, *(() if carry is None else (carry,)), *final)


def ffn_kernel(final, paired, *refs):
    low_ref, cot_ref, up_ref, down_ref, out_in = refs[:5]
    back_in = refs[5] if final else None
    out_ref, back_ref, gu_ref, gd_ref, out_sum, back_sum, act, hid = refs[5 + final :]

    def chunk(first):
        up, down = up_ref[...], down_ref[...]
        for start in range(0, low_ref.shape[0], BLOCK):
            here = pl.ds(start, BLOCK)
            hidden = dot_nn(low_ref[here, :], up)
            grad_active = dot_nt(cot_ref[start // BLOCK, 0], down)
            square = hidden * hidden
            bend = jnp.tanh(hidden * (GELU_A + (GELU_A * GELU_B) * square))
            gate = 0.5 + 0.5 * bend
            active = (hidden * gate).astype(BF16)
            slope = gate + hidden * (0.5 - 0.5 * bend * bend) * (
                GELU_A + (3 * GELU_A * GELU_B) * square
            )
            grad_hidden = (grad_active * slope).astype(BF16)
            act[here, :] = active
            hid[here, :] = grad_hidden
            add_out, add_back = dot_nn(active, down), dot_nt(grad_hidden, up)
            if first:
                out_sum[here, :] = add_out
                back_sum[here, :] = add_back
            else:
                total = out_sum[here, :] + add_out + out_in[here, :].astype(F32)
                out_ref[here, :] = total.astype(out_ref.dtype)
                total = back_sum[here, :] + add_back
                if final:
                    total = total + back_in[here, :].astype(F32)
                back_ref[here, :] = total.astype(BF16)
        gu_ref[...] = dot_tn(low_ref[...], hid[...]).astype(BF16)
        cot = cot_ref[...].reshape(act.shape[0], -1)
        grad_down = dot_tn(act[...], cot).astype(BF16)
        if paired:
            dim = grad_down.shape[1]
            grad_down = grad_down.reshape(-1, 2 * paired, dim)
            for side in range(2):
                gd_ref[:, side * dim : (side + 1) * dim] = grad_down[
                    :, side * paired : (side + 1) * paired
                ].reshape(-1, dim)
        else:
            gd_ref[...] = grad_down

    for place in range(2):

        @pl.when(pl.program_id(0) == place)
        def _(place=place):
            chunk(place == 0)


def feed_forward(low, pair, up, down, out_in, part, back_in=None):
    tok, dim = low.shape
    final = back_in is not None
    wide = down.shape[0]
    chunk = wide // 2
    paired = part if part % 16 == 0 else 0
    tall, long = (chunk // 2, 2 * dim) if paired else (chunk, dim)
    outs = pl.pallas_call(
        functools.partial(ffn_kernel, int(final), paired),
        grid=(2,),
        in_specs=[whole(tok, dim), part_of(pair, 1), columns(dim, chunk), rows(chunk, dim)]
        + [whole(tok, dim)] * (2 if final else 1),
        out_specs=[whole(tok, dim), whole(tok, dim), columns(dim, chunk), rows(tall, long)],
        out_shape=[shaped((tok, dim), BF16 if final else F32), shaped((tok, dim), BF16)]
        + [shaped((dim, wide), BF16), shaped((2 * tall, long), BF16)],
        scratch_shapes=[pltpu.VMEM((tok, dim), F32)] * 2 + [pltpu.VMEM((tok, chunk), BF16)] * 2,
        compiler_params=params(58),
        cost_estimate=cost(0.01),
    )(low, pair, up, down, out_in, *((back_in,) if final else ()))
    if paired:
        return outs
    grad_down = outs[3].reshape(-1, 2, part, dim).transpose(0, 2, 1, 3).reshape(-1, 2 * dim)
    return list(outs[:3]) + [grad_down]


def by_place(where_ref, refs):
    x, c = where_ref[0], where_ref[1]
    own, other_x, other_c, other_both = (ref[...].astype(F32) for ref in refs)
    low_x = [jnp.where(x == 0, own, other_x), jnp.where(x == 0, other_c, other_both)]
    high_x = [jnp.where(x == 0, other_x, own), jnp.where(x == 0, other_both, other_c)]
    return [
        [jnp.where(c == 0, side[0], side[1]) for side in (low_x, high_x)],
        [jnp.where(c == 0, side[1], side[0]) for side in (low_x, high_x)],
    ]


def finish_ffn(fan, where_ref, all_ref, up_ref, down_ref):
    part, dim = all_ref.shape[2], down_ref.shape[1]
    count = up_ref.shape[1] // fan // 2
    for core in range(2):
        for side in range(2):
            here = slice(side * part, (side + 1) * part)
            for block in range(count):
                place = (2 * block + core) * fan
                up_ref[here, place : place + fan] = all_ref[
                    core, side, :, block * fan : (block + 1) * fan
                ].astype(F32)
            start = count * fan
            for half in range(2):
                place = core * fan + side * fan // 2 + half * part
                down_ref[place : place + part, :] = all_ref[
                    core, side, :, start + half * dim : start + (half + 1) * dim
                ].astype(F32)


def finish_qkv(pairs, where_ref, *refs):
    pieces, (qkv_ref, proj_ref, *norm_refs) = by_place(where_ref, refs[:4]), refs[4:]
    part, dim = refs[0].shape[0], qkv_ref.shape[1] // 3
    sums = []
    for side in range(2):
        here = slice(side * part, (side + 1) * part)
        for core in range(2):
            piece = pieces[core][side]
            for pair in range(pairs):
                for which in range(3):
                    place = which * dim + core * dim // 2 + pair * 128
                    start = (pair * 3 + which) * 128
                    qkv_ref[here, place : place + 128] = piece[:, start : start + 128]
            start = pairs * 384 + 128
            proj_ref[here, core * dim // 2 : (core + 1) * dim // 2] = piece[:, start:]
        norms = slice(pairs * 384, pairs * 384 + 128)
        sums.append(pieces[0][side][:, norms] + pieces[1][side][:, norms])
    sums = jnp.concatenate(sums, axis=0).T
    for place, norm_ref in enumerate(norm_refs):
        norm_ref[...] = sums[place : place + 1].reshape(norm_ref.shape)


def finish(kernel, where, pieces, *shapes):
    return pl.pallas_call(
        kernel,
        grid_spec=pltpu.PrefetchScalarGridSpec(
            num_scalar_prefetch=1,
            grid=(1,),
            in_specs=[whole(*piece.shape) for piece in pieces],
            out_specs=[whole(*shape) for shape in shapes],
        ),
        out_shape=[shaped(shape, F32) for shape in shapes],
        compiler_params=params(58),
        cost_estimate=cost(0.01),
    )(where, *pieces)


class Grid:
    def __init__(self):
        self.z_count = lax.axis_size("dp") // 2
        self.dp, self.head = lax.axis_index("dp"), lax.axis_index("head")
        self.z, self.y, self.x, self.c = self.dp // 2, self.dp % 2, self.head // 2, self.head % 2
        assert lax.axis_size("head") == 4 and lax.axis_size("dp") % 2 == 0

    def send(self, value, z=0, y=0, x=0, c=0):
        pairs = []
        for source in range(self.z_count * 8):
            zi, yi, xi, ci = source // 8, source // 4 % 2, source // 2 % 2, source % 2
            zt, yt, xt, ct = (zi + z) % self.z_count, yi ^ y, xi ^ x, ci ^ c
            pairs.append((source, ((zt * 2 + yt) * 2 + xt) * 2 + ct))
        return lax.ppermute(value, BOTH, pairs)

    def pick(self, value, axis, index):
        return lax.dynamic_index_in_dim(value, index, axis, keepdims=False)

    def join(self, mine, other, index, axis):
        shape = mine.shape[:axis] + (2,) + mine.shape[axis:]
        here = lax.broadcasted_iota(jnp.int32, shape, axis) == index
        mine, other = (jnp.broadcast_to(jnp.expand_dims(v, axis), shape) for v in (mine, other))
        return jnp.where(here, mine, other)

    def to_z(self, piece):
        return [piece] + [self.send(piece, z=step) for step in range(1, self.z_count)]

    def by_z(self, got):
        shape = (self.z_count,) + got[0].shape
        steps = (self.z - lax.broadcasted_iota(jnp.int32, shape, 0)) % self.z_count
        out = jnp.broadcast_to(got[0], shape)
        for step in range(1, self.z_count):
            out = jnp.where(steps == step, jnp.broadcast_to(got[step], shape), out)
        return out

    def over_y(self, value, got):
        return self.join(value, got, self.y, 1)

    def over_x(self, value, got, axis):
        return self.join(value, got, self.x, axis)

    def halves(self, name, values):
        axis, index = (1, self.y) if name == "y" else (values[0].ndim - 3, self.x)
        low, high = (
            sum(lax.index_in_dim(v, place, axis, False).astype(F32) for v in values).astype(BF16)
            for place in range(2)
        )
        return jnp.where(index == 0, high, low), jnp.where(index == 0, low, high)

    def by_block(self, *values):
        totals = [keep.astype(F32) + got.astype(F32) for keep, got in values]
        return [
            jnp.concatenate(
                [self.pick(total, 0, (self.z + step) % self.z_count) for total in totals], axis=-1
            ).astype(BF16)
            for step in range(self.z_count)
        ]

    def end(self, parts):
        return self.total(
            [parts[0]] + [self.send(part, z=step) for step, part in enumerate(parts) if step]
        )

    def total(self, parts):
        return sum(value.astype(F32) for value in parts).astype(BF16)

    def share(self, piece):
        return [piece, self.send(piece, x=1), self.send(piece, c=1), self.send(piece, x=1, c=1)]

    def share_all(self, piece):
        both = self.join(piece, self.send(piece, x=1), self.x, 0)
        return self.join(both, self.send(both, c=1), self.c, 0)


def exchange(value):
    return lax.all_to_all(value, "head", split_axis=0, concat_axis=0, tiled=True)


def after(value, *done):
    return lax.optimization_barrier((value, done))[0]


def flat(value):
    return value.reshape(-1, value.shape[-1])


def local(
    tokens,
    qkv_weight,
    proj_weight,
    up_weight,
    down_weight,
    attn_gain,
    attn_bias,
    ffn_gain,
    ffn_bias,
    cotangent,
):
    grid = Grid()
    dim = tokens.shape[-1]
    share = qkv_weight.shape[0]
    part = share // 2
    half = dim // 2
    pairs = half // 128
    hidden = up_weight.shape[1]
    dp_count = lax.axis_size("dp")
    fan = hidden // dp_count // 2
    core = grid.c.reshape(1).astype(jnp.int32)
    assert tokens.shape[0] == 4 and tokens.shape[1] * 4 == SEQ
    assert fan == 4 * part

    def row_half(value):
        return lax.dynamic_slice_in_dim(value, grid.x * part, part, 0)

    qkv = grid.pick(qkv_weight.reshape(share, 3, 2, pairs, 128), 2, grid.c)
    qkv = qkv.transpose(0, 2, 1, 3).reshape(share, -1)
    table = jnp.stack([attn_gain, attn_bias, ffn_gain, ffn_bias], axis=1)
    table = jnp.pad(table, ((0, 0), (0, 124)))
    piece = jnp.concatenate([qkv, table], axis=1).astype(BF16)
    up = grid.pick(row_half(up_weight).reshape(part, dp_count, 2, fan), 2, grid.c)
    proj = grid.pick(row_half(proj_weight).reshape(part, 2, half), 1, grid.c)
    up_piece = jnp.concatenate([up.reshape(part, -1), proj], axis=1).astype(BF16)
    down_piece = grid.pick(down_weight.reshape(2, fan, dim), 0, grid.c).astype(BF16)
    where_head = jnp.stack([grid.x, grid.c]).astype(jnp.int32)

    both = exchange(after(jnp.stack([tokens, cotangent], axis=1), piece))
    first_z = grid.by_z(after(grid.to_z(piece), up_piece, down_piece))
    up_got = grid.to_z(after(up_piece, first_z))
    w_mine = flat(grid.over_y(first_z, after(grid.send(first_z, y=1), up_got)))
    w_theirs = grid.send(w_mine, c=1)
    up_z = grid.by_z(after(up_got, w_mine))
    up_y = grid.send(up_z, y=1)
    down_got = grid.to_z(after(down_piece, w_mine, both))

    up_x = grid.send(up_z, x=1)
    up_xy = grid.send(after(up_y, down_got), x=1)
    down_z = grid.by_z(after(down_got, up_z))
    down_y = grid.send(down_z, y=1)
    low, mixed_mine, att_mine, log_mine, table = attend(
        after(both, up_x, down_z), w_mine, pairs, True
    )
    mixed_theirs, att_theirs, log_theirs = attend(low, w_theirs, pairs, False)
    up_y = grid.over_y(up_z, up_y)
    up_x = grid.over_y(up_x, after(up_xy, att_theirs))
    up_mine = flat(grid.over_x(up_y, up_x, 2))
    up_theirs = grid.send(up_mine, c=1)
    down_mine = flat(grid.over_y(down_z, after(down_y, att_theirs)))
    down_theirs = grid.send(down_mine, c=1)
    middle, low_two = project(core, both, att_mine, att_theirs, up_mine, up_theirs, table)
    out, back, gu_mine, gd_mine = feed_forward(
        low_two, both, up_mine, after(down_mine, low_two), middle, part
    )
    out, back, gu_theirs, gd_theirs = feed_forward(
        low_two, both, up_theirs, after(down_theirs, back), out, part, back
    )

    def blocks(value):
        return value.reshape(grid.z_count, 2, 2, -1, value.shape[-1])

    gd_core, gu_core = grid.send(gd_theirs, c=1), grid.send(gu_theirs, c=1)
    gd_out, gd_keep = grid.halves("y", [blocks(gd_mine), blocks(gd_core)])
    gd_got = grid.send(gd_out, y=1)
    gu_out, gu_keep = grid.halves("x", [blocks(gu_mine), blocks(after(gu_core, gd_out))])
    gu_got = grid.send(gu_out, x=1)
    grad_middle, ga_mine, ga_theirs, gp_mine, gp_theirs, norm_two = middle_back(
        core, middle, after(back, gd_out, gu_out), both, table, up_mine, up_theirs, att_mine,
        att_theirs,
    )
    gp_core = grid.send(gp_theirs, c=1)
    gq_theirs, gq_rest, grad_low = attend_back(
        mixed_theirs, ga_theirs, att_theirs, log_theirs, low, w_theirs, 0, pairs
    )
    gq_core = [grid.send(value, c=1) for value in (gq_theirs, gq_rest)]
    gd_got, gu_got, gp_core = after((gd_got, gu_got, gp_core), grad_low)
    gd_out, gd_keep = grid.halves("x", [gd_keep, gd_got])
    gd_got = grid.send(gd_out, x=1)
    gu_out, gu_keep = grid.halves("y", [gu_keep, gu_got])
    gu_got = grid.send(gu_out, y=1)
    out_home = exchange(after(out.reshape(4, SEQ // 4, dim), gd_out, gu_out))
    gq_mine, gq_more, grad_x, _ = attend_back(
        mixed_mine, after(ga_mine, gd_out, gu_out, gq_core, gp_core), att_mine, log_mine, low,
        w_mine, 0, pairs, carry=grad_low, final=(both, grad_middle, table, norm_two),
    )
    gq_core, gd_got, gu_got = after((gq_core, gd_got, gu_got), gq_mine)
    left_out, left_keep = grid.halves(
        "x", [blocks(gq_mine), blocks(gq_core[0])]
    )
    left_got = grid.send(left_out, x=1)
    right_out, right_keep = grid.halves(
        "y",
        [
            jnp.concatenate([blocks(gq_more), blocks(gp_mine)], axis=-1),
            jnp.concatenate([blocks(gq_core[1]), blocks(gp_core)], axis=-1),
        ],
    )
    right_got = grid.send(right_out, y=1)
    gd_got, gu_got, out_home = after((gd_got, gu_got, out_home), left_out, right_out)
    ffn_parts = grid.by_block((gu_keep, gu_got), (gd_keep, gd_got))
    left_got, right_got = after((left_got, right_got), ffn_parts)
    ffn_got = [grid.send(part, z=step) for step, part in enumerate(ffn_parts) if step]
    left_out, left_keep = grid.halves("y", [left_keep, left_got])
    left_got = grid.send(left_out, y=1)
    right_out, right_keep = grid.halves("x", [right_keep, right_got])
    right_got = grid.send(right_out, x=1)
    grad_home = exchange(after(grad_x.reshape(4, SEQ // 4, dim), left_got))
    left_got, right_got = after((left_got, right_got), ffn_got)
    qkv_parts = grid.by_block((left_keep, left_got), (right_keep, right_got))
    sum_ffn = after(grid.total([ffn_parts[0], *ffn_got]), qkv_parts)
    ffn_x = grid.send(sum_ffn, x=1)
    qkv_got = [grid.send(part, z=step) for step, part in enumerate(qkv_parts) if step]
    qkv_got, grad_home = after((qkv_got, grad_home), grad_home)
    sum_qkv = grid.total([qkv_parts[0], *qkv_got])
    ffn_x = grid.join(sum_ffn, ffn_x, grid.x, 0)
    all_ffn = grid.join(ffn_x, grid.send(ffn_x, c=1), grid.c, 0)
    shares = grid.share(sum_qkv)
    grad_home = after(grad_home, sum_qkv).astype(F32)
    shard_up, shard_down = finish(
        functools.partial(finish_ffn, fan), where_head, [after(all_ffn, sum_qkv)],
        (share, hidden), (2 * fan, dim),
    )
    shard_qkv, shard_proj, *norms = finish(
        functools.partial(finish_qkv, pairs), where_head, after(shares, shard_up),
        (share, 3 * dim), (share, dim), *[(share,)] * 4,
    )
    return (
        out_home,
        grad_home,
        shard_qkv,
        shard_proj,
        shard_up,
        shard_down,
        norms[0],
        norms[1],
        norms[2],
        norms[3],
    )


def solution(mesh):
    spread = P("dp", "head", None)
    placed = (spread,) + (P("dp", None),) * 4 + (P("dp"),) * 4 + (spread,)
    return jax.shard_map(
        local,
        mesh=mesh,
        in_specs=placed,
        out_specs=(spread, spread) + (P("dp", None),) * 4 + (P("dp"),) * 4,
        check_vma=False,
    )
```

time: 789 us -> 357 us (0.45)
  waiting for transfers between devices: 337 us -> 84.5 us
  matrix products: 199 us -> 0 us
  Pallas kernels: 0 us -> 141 us
  local copies, waits for them, and re-layouts: 88.8 us -> 20.5 us
  other arithmetic: 92.7 us -> 40.3 us
  starting transfers between devices: 17.4 us -> 63 us
  blocking collectives: 28.2 us -> 0 us
  between operations: 15.3 us -> 1.68 us
    dot_general x24 -> x0, matrix products: 199 us -> none  [the longest x4 30.7 us: contract_cols(): lax.dot_general(left, right, (((1,), (1,)), ((), ())), preferred_element_...]
    reduce_scatter x3 -> x0, waiting for transfers between devices: 178 us -> none  [scatter(): lax.psum_scatter(total.astype(jnp.bfloat16), BOTH, scatter_dimension=0, t...]
    pallas_call x0 -> x10, Pallas kernels: none -> 141 us  [the longest x2 47.5 us: attend_back(): pl.pallas_call(functools.partial(attend_back_kernel, carry is not None, b...]
    all_gather x4 -> x0, waiting for transfers between devices: 104 us -> none  [gather(): return lax.all_gather(mine.astype(jnp.bfloat16), BOTH, axis=0, tiled=True)]
    ppermute x0 -> x41, waiting for transfers between devices: none -> 79.3 us  [send(): return lax.ppermute(value, BOTH, pairs)]
    ppermute x0 -> x41, starting transfers between devices: none -> 50.3 us  [send(): return lax.ppermute(value, BOTH, pairs)]
    all_to_all x4 -> x3, waiting for transfers between devices: 54.6 us -> 5.15 us  [exchange(): lax.all_to_all(value, 'head', split_axis=0, concat_axis=0, tiled=True)]
    convert_element_type x11 -> x4, other arithmetic: 42.5 us -> 4.72 us  [the longest x1 1.93 us: local(): grad_home = after(grad_home, sum_qkv).astype(F32)]
  transfers between devices with their start and end apart: 12 -> 44, of which waited for: 8 -> 18; matrix products, arithmetic and copies ran while one was open for 38% -> 12% of each run, Pallas kernels for 0% -> 33%
where the time goes in v2:
time: 357 us; the launch traced here: 351 us
  Pallas kernels  141 us (39%)
  waiting for transfers between devices  84.5 us (24%)
  starting transfers between devices  63 us (18%)
  other arithmetic  40.3 us (11%)
  local copies, waits for them, and re-layouts  20.5 us (6%)
    ppermute x41, waiting for transfers between devices, send(): return lax.ppermute(value, BOTH, pairs)  79.3 us
    ppermute x41, starting transfers between devices, send(): return lax.ppermute(value, BOTH, pairs)  50.3 us
    pallas_call x2, Pallas kernels, attend_back(): pl.pallas_call(functools.partial(attend_back_kernel, carry is not None, b...  47.5 us
    pallas_call x2, Pallas kernels, feed_forward(): pl.pallas_call(functools.partial(ffn_kernel, int(final), paired), grid=(2...  46.2 us
    pallas_call x2, Pallas kernels, attend(): pl.pallas_call(functools.partial(attend_kernel, first), grid=(pairs,), in...  23.7 us
    all_to_all x3, starting transfers between devices, exchange(): lax.all_to_all(value, 'head', split_axis=0, concat_axis=0, tiled=True)  12.7 us
    pallas_call x1, Pallas kernels, middle_back(): pl.pallas_call(middle_kernel, grid_spec=pltpu.PrefetchScalarGridSpec(num_...  10.3 us
    select_n x9, other arithmetic, halves(): return (jnp.where(index == 0, high, low), jnp.where(index == 0, low, high))  9.37 us
  transfers between devices with their start and end apart: 44, of which 18 were waited for; matrix products, arithmetic and copies ran while one was open for 12% of the time, Pallas kernels for 33%

profile of v2, /device:TPU:0, one launch (start us, length us, event | category | flops | bytes accessed | tf_op | source)
XLA Modules:
  0.0 350.7 jit_solution(12492224181810158153)
XLA Ops:
  4.7 3.1 collective-permute-start
  7.8 2.6 collective-permute-start.1
  11.7 3.4 pad_maximum_fusion
  15.1 4.6 %all-to-all-start = ((bf16[4,2,256,768]{3,2,1,0:T(8,128)(2,1)}), bf16[4,2,256,768]{3,2,1,0:T(8,128)(2,1)}, u32[]{:S(2)}, u32[]{:S(2)}) async-start(bf16[4,2,256,768]{3,2,1,0:T(8,128)(2,1)} %pad_maximum_fusion), calls=%async_computation | async-start | bytes 6291456 | tf_op jit(solution)/shard_map/all_to_all | solution.py:615
  24.0 2.6 collective-permute-done.1
  29.6 5.7 %collective-permute-start.3 = (bf16[48,1920]{1,0:T(8,128)(2,1)S(1)}, bf16[48,1920]{1,0:T(8,128)(2,1)S(1)}, u32[]{:S(2)}, u32[]{:S(2)}) collective-permute-start(bf16[48,1920]{1,0:T(8,128)(2,1)S(1)} %pad_maximum_fusion.7), channel_id=1, source_target_pairs={{0,8},{1,9},{2,10},{3,11},{4,12},{5,13},{6,14},{7,15},{8,16},{9,17... | collective-permute-start | bytes 552968 | tf_op jit(solution)/shard_map/ppermute | solution.py:553
  37.9 4.0 %collective-permute-done.3 = bf16[48,1920]{1,0:T(8,128)(2,1)S(1)} collective-permute-done((bf16[48,1920]{1,0:T(8,128)(2,1)S(1)}, bf16[48,1920]{1,0:T(8,128)(2,1)S(1)}, u32[]{:S(2)}, u32[]{:S(2)}) %collective-permute-start.3) | collective-permute-done | bytes 184352 | tf_op jit(solution)/shard_map/ppermute | solution.py:553
  41.9 6.0 %collective-permute-done.4 = bf16[48,1920]{1,0:T(8,128)(2,1)S(1)} collective-permute-done((bf16[48,1920]{1,0:T(8,128)(2,1)S(1)}, bf16[48,1920]{1,0:T(8,128)(2,1)S(1)}, u32[]{:S(2)}, u32[]{:S(2)}) %collective-permute-start.4) | collective-permute-done | bytes 184352 | tf_op jit(solution)/shard_map/ppermute | solution.py:553
  49.3 2.6 collective-permute-done.6
  56.7 4.4 %collective-permute-start.10 = (bf16[192,768]{1,0:T(8,128)(2,1)S(1)}, bf16[192,768]{1,0:T(8,128)(2,1)S(1)}, u32[]{:S(2)}, u32[]{:S(2)}) collective-permute-start(bf16[192,768]{1,0:T(8,128)(2,1)S(1)} %fusion.18), channel_id=1, source_target_pairs={{0,24},{1,25},{2,26},{3,27},{4,28},{5,29},{6,30},{7,31},{8,0},{9,1... | collective-permute-start | bytes 884744 | tf_op jit(solution)/shard_map/ppermute | solution.py:553
  62.8 9.9 %collective-permute-done.12 = bf16[4,48,1920]{2,1,0:T(8,128)(2,1)} collective-permute-done((bf16[4,48,1920]{2,1,0:T(8,128)(2,1)S(1)}, bf16[4,48,1920]{2,1,0:T(8,128)(2,1)}, u32[]{:S(2)}, u32[]{:S(2)}) %collective-permute-start.12) | collective-permute-done | bytes 737312 | tf_op jit(solution)/shard_map/ppermute | solution.py:553
  75.7 12.9 %collective-permute-done.9 = bf16[192,768]{1,0:T(8,128)(2,1)S(1)} collective-permute-done((bf16[192,768]{1,0:T(8,128)(2,1)S(1)}, bf16[192,768]{1,0:T(8,128)(2,1)S(1)}, u32[]{:S(2)}, u32[]{:S(2)}) %collective-permute-start.9) | collective-permute-done | bytes 294944 | tf_op jit(solution)/shard_map/ppermute | solution.py:553
  94.6 12.5 %shard_map.177 = (bf16[1024,768]{1,0:T(8,128)(2,1)}, bf16[1024,1152]{1,0:T(8,128)(2,1)}, bf16[1024,384]{1,0:T(8,128)(2,1)}, f32[3,2,1024]{2,1,0:T(2,128)}, f32[8,768]{1,0:T(8,128)}) custom-call(bf16[4,2,256,768]{3,2,1,0:T(8,128)(2,1)} %all-to-all-done.refs_0_.x_ref.refs_1_.cot_ref.refs_7_, bf16[768,1280]{1,0:T(8,128)(2,1)} %copy-done.3, ...), custom_call_target="tpu_custom_call" | custom-call | flops 11000000 | bytes 30000 | tf_op jit(solution)/shard_map/pallas_call | solution.py:256
  107.0 11.2 %shard_map.178 = (bf16[1024,1152]{1,0:T(8,128)(2,1)}, bf16[1024,384]{1,0:T(8,128)(2,1)}, f32[3,2,1024]{2,1,0:T(2,128)}) custom-call(bf16[1024,768]{1,0:T(8,128)(2,1)} %get-tuple-element.117.refs_0_.refs_4_, bf16[768,1280]{1,0:T(8,128)(2,1)} %collective-permute-done.11.refs_1_.refs_5_), custom_call_target="tpu_custom_call" | custom-call | flops 11000000 | bytes 30000 | tf_op jit(solution)/shard_map/pallas_call | solution.py:256
  126.2 6.5 %shard_map.179 = (bf16[1024,768]{1,0:T(8,128)(2,1)}, bf16[1024,768]{1,0:T(8,128)(2,1)}) custom-call(s32[1]{0:T(128)} %bitcast.12.core_ref, bf16[4,2,256,768]{3,2,1,0:T(8,128)(2,1)} %all-to-all-done.refs_0_.x_ref.refs_1_.cot_ref.refs_7_, bf16[1024,384]{1,0:T(8,128)(2,1)} %get-tuple-element.119.am_ref.refs_2_, ...), custom_call_target="tpu_custom_call" | custom-call | flops 11000000 | bytes 30000 | tf_op jit(solution)/shard_map/pallas_call | solution.py:105
  132.8 22.7 %shard_map.180 = (f32[1024,768]{1,0:T(8,128)}, bf16[1024,768]{1,0:T(8,128)(2,1)}, bf16[768,1536]{1,0:T(8,128)(2,1)}, bf16[768,1536]{1,0:T(8,128)(2,1)}) custom-call(bf16[1024,768]{1,0:T(8,128)(2,1)} %get-tuple-element.125.refs_0_, bf16[4,2,256,768]{3,2,1,0:T(8,128)(2,1)} %all-to-all-done.refs_0_.x_ref.refs_1_.cot_ref.refs_7_, bf16[768,1920]{1,0:T(8,128)(2,1)} %copy-done.2, ...), custom_call_target="tpu_custom_call" | custom-call | flops 11000000 | bytes 30000 | tf_op jit(solution)/shard_map/pallas_call | solution.py:455
  155.5 23.5 %shard_map.181 = (bf16[1024,768]{1,0:T(8,128)(2,1)}, bf16[1024,768]{1,0:T(8,128)(2,1)}, bf16[768,1536]{1,0:T(8,128)(2,1)}, bf16[768,1536]{1,0:T(8,128)(2,1)}) custom-call(bf16[1024,768]{1,0:T(8,128)(2,1)} %get-tuple-element.125.refs_0_, bf16[4,2,256,768]{3,2,1,0:T(8,128)(2,1)} %all-to-all-done.refs_0_.x_ref.refs_1_.cot_ref.refs_7_, ...), custom_call_target="tpu_custom_call" | custom-call | flops 11000000 | bytes 30000 | tf_op jit(solution)/shard_map/pallas_call | solution.py:455
  179.7 4.2 %collective-permute-done.17 = bf16[768,1536]{1,0:T(8,128)(2,1)} collective-permute-done((bf16[768,1536]{1,0:T(8,128)(2,1)}, bf16[768,1536]{1,0:T(8,128)(2,1)}, u32[]{:S(2)}, u32[]{:S(2)}) %collective-permute-start.17) | collective-permute-done | bytes 2359328 | tf_op jit(solution)/shard_map/ppermute | solution.py:553
  193.1 10.3 %shard_map.182 = (bf16[1024,768]{1,0:T(8,128)(2,1)}, bf16[1024,384]{1,0:T(8,128)(2,1)}, bf16[1024,384]{1,0:T(8,128)(2,1)}, bf16[768,384]{1,0:T(8,128)(2,1)}, bf16[768,384]{1,0:T(8,128)(2,1)}, /*index=5*/f32[8,768]{1,0:T(8,128)}) custom-call(s32[1]{0:T(128)} %bitcast.12.core_ref, bf16[1024,768]{1,0:T(8,128)(2,1)} %get-tuple-element.124.refs_4_.mid_ref, ...), custom_call_target="tpu_custom_call" | custom-call | flops 11000000 | bytes 30000 | tf_op jit(solution)/shard_map/pallas_call | solution.py:162
  203.5 22.5 %shard_map.183 = (bf16[768,768]{1,0:T(8,128)(2,1)}, bf16[768,512]{1,0:T(8,128)(2,1)}, bf16[1024,768]{1,0:T(8,128)(2,1)}) custom-call(bf16[1024,1152]{1,0:T(8,128)(2,1)} %get-tuple-element.118.refs_0_, bf16[1024,384]{1,0:T(8,128)(2,1)} %get-tuple-element.138.refs_1_, bf16[1024,384]{1,0:T(8,128)(2,1)} %get-tuple-element.120.at_ref.refs_2_, ...), custom_call_target="tpu_custom_call" | custom-call | flops 11000000 | bytes 30000 | tf_op jit(solution)/shard_map/pallas_call | solution.py:376
  230.5 4.4 %all-to-all-start.1 = ((bf16[4,256,768]{2,1,0:T(8,128)(2,1)}), bf16[4,256,768]{2,1,0:T(8,128)(2,1)}, u32[]{:S(2)}, u32[]{:S(2)}) async-start(bf16[4,256,768]{2,1,0:T(8,128)(2,1)} %bitcast.147), calls=%async_computation.1 | async-start | bytes 3145728 | tf_op jit(solution)/shard_map/all_to_all | solution.py:615
  234.9 25.0 %shard_map.184 = (bf16[768,768]{1,0:T(8,128)(2,1)}, bf16[768,512]{1,0:T(8,128)(2,1)}, bf16[1024,768]{1,0:T(8,128)(2,1)}, f32[8,768]{1,0:T(8,128)}) custom-call(bf16[1024,1152]{1,0:T(8,128)(2,1)} %get-tuple-element.146.refs_0_, bf16[1024,384]{1,0:T(8,128)(2,1)} %get-tuple-element.149.refs_1_, bf16[1024,384]{1,0:T(8,128)(2,1)} %get-tuple-element.119.am_ref.refs_2_, ...), custom_call_target="tpu_custom_call" | custom-call | flops 11000000 | bytes 30000 | tf_op jit(solution)/shard_map/pallas_call | solution.py:376
  274.0 3.8 %collective-permute-start.32 = (bf16[48,3072]{1,0:T(8,128)(2,1)S(1)}, bf16[48,3072]{1,0:T(8,128)(2,1)S(1)}, u32[]{:S(2)}, u32[]{:S(2)}) collective-permute-start(bf16[48,3072]{1,0:T(8,128)(2,1)S(1)} %pad_maximum_fusion.6), channel_id=1, source_target_pairs={{0,24},{1,25},{2,26},{3,27},{4,28},{5,29},{6,30},{7,31},{8,0},{9,1... | collective-permute-start | bytes 884744 | tf_op jit(solution)/shard_map/ppermute | solution.py:553
  279.4 4.8 %collective-permute-done.26 = bf16[4,2,48,768]{3,2,0,1:T(8,128)(2,1)} collective-permute-done((bf16[4,2,48,768]{3,2,0,1:T(8,128)(2,1)}, bf16[4,2,48,768]{3,2,0,1:T(8,128)(2,1)}, u32[]{:S(2)}, u32[]{:S(2)}) %collective-permute-start.26) | collective-permute-done | bytes 589856 | tf_op jit(solution)/shard_map/ppermute | solution.py:553
  289.1 15.6 %collective-permute-done.31 = bf16[48,3072]{1,0:T(8,128)(2,1)S(1)} collective-permute-done((bf16[48,3072]{1,0:T(8,128)(2,1)S(1)}, bf16[48,3072]{1,0:T(8,128)(2,1)S(1)}, u32[]{:S(2)}, u32[]{:S(2)}) %collective-permute-start.31) | collective-permute-done | bytes 294944 | tf_op jit(solution)/shard_map/ppermute | solution.py:553
  309.9 3.7 %all-to-all-start.2 = ((bf16[4,256,768]{2,1,0:T(8,128)(2,1)}), bf16[4,256,768]{2,1,0:T(8,128)(2,1)S(1)}, u32[]{:S(2)}, u32[]{:S(2)}) async-start(bf16[4,256,768]{2,1,0:T(8,128)(2,1)} %bitcast.62), calls=%async_computation.2 | async-start | bytes 3145728 | tf_op jit(solution)/shard_map/all_to_all | solution.py:615
  318.3 3.3 collective-permute-done.35
  321.6 8.0 %collective-permute-done.34 = bf16[48,1664]{1,0:T(8,128)(2,1)S(1)} collective-permute-done((bf16[48,1664]{1,0:T(8,128)(2,1)}, bf16[48,1664]{1,0:T(8,128)(2,1)S(1)}, u32[]{:S(2)}, u32[]{:S(2)}) %collective-permute-start.34) | collective-permute-done | bytes 159776 | tf_op jit(solution)/shard_map/ppermute | solution.py:553
  330.2 3.7 %all-to-all-done.2 = bf16[4,256,768]{2,1,0:T(8,128)(2,1)S(1)} async-done(((bf16[4,256,768]{2,1,0:T(8,128)(2,1)}), bf16[4,256,768]{2,1,0:T(8,128)(2,1)S(1)}, u32[]{:S(2)}, u32[]{:S(2)}) %all-to-all-start.2) | async-done | bytes 1572896 | tf_op jit(solution)/shard_map/all_to_all | solution.py:615
  340.4 3.6 %shard_map.185 = (f32[96,3072]{1,0:T(8,128)}, f32[384,768]{1,0:T(8,128)}) custom-call(s32[2]{0:T(128)} %pad_add_fusion.where_ref, bf16[2,2,48,3072]{3,2,1,0:T(8,128)(2,1)} %broadcast_select_fusion.2.all_ref), custom_call_target="tpu_custom_call" | custom-call | flops 11000000 | bytes 30000 | tf_op jit(solution)/shard_map/pallas_call | solution.py:526
  344.8 3.0 shard_map.186
  347.8 2.7 copy.202
  (209 shorter events, 92.4 us)
Async XLA Ops:
  4.7 19.3 %collective-permute-start = (bf16[96,1280]{1,0:T(8,128)(2,1)S(1)}, bf16[96,1280]{1,0:T(8,128)(2,1)}, u32[]{:S(2)}, u32[]{:S(2)}) collective-permute-start(bf16[96,1280]{1,0:T(8,128)(2,1)S(1)} %fusion.19), channel_id=1, source_target_pairs={{0,8},{1,9},{2,10},{3,11},{4,12},{5,13},{6,14},{7,15},{8,16},{9,17... | collective-permute-start | bytes 737288 | tf_op jit(solution)/shard_map/ppermute | solution.py:553
  7.8 18.8 %collective-permute-start.1 = (bf16[96,1280]{1,0:T(8,128)(2,1)S(1)}, bf16[96,1280]{1,0:T(8,128)(2,1)}, u32[]{:S(2)}, u32[]{:S(2)}) collective-permute-start(bf16[96,1280]{1,0:T(8,128)(2,1)S(1)} %fusion.19), channel_id=1, source_target_pairs={{0,16},{1,17},{2,18},{3,19},{4,20},{5,21},{6,22},{7,23},{8,24},{9,... | collective-permute-start | bytes 737288 | tf_op jit(solution)/shard_map/ppermute | solution.py:553
  10.4 16.2 %collective-permute-start.2 = (bf16[96,1280]{1,0:T(8,128)(2,1)S(1)}, bf16[96,1280]{1,0:T(8,128)(2,1)}, u32[]{:S(2)}, u32[]{:S(2)}) collective-permute-start(bf16[96,1280]{1,0:T(8,128)(2,1)S(1)} %fusion.19), channel_id=1, source_target_pairs={{0,24},{1,25},{2,26},{3,27},{4,28},{5,29},{6,30},{7,31},{8,0},{9,1... | collective-permute-start | bytes 737288 | tf_op jit(solution)/shard_map/ppermute | solution.py:553
  15.1 41.6 %all-to-all-start = ((bf16[4,2,256,768]{3,2,1,0:T(8,128)(2,1)}), bf16[4,2,256,768]{3,2,1,0:T(8,128)(2,1)}, u32[]{:S(2)}, u32[]{:S(2)}) async-start(bf16[4,2,256,768]{3,2,1,0:T(8,128)(2,1)} %pad_maximum_fusion), calls=%async_computation | async-start | bytes 6291456 | tf_op jit(solution)/shard_map/all_to_all | solution.py:615
  28.1 23.8 %collective-permute-start.6 = (bf16[4,96,1280]{2,1,0:T(8,128)(2,1)S(1)}, bf16[4,96,1280]{2,1,0:T(8,128)(2,1)}, u32[]{:S(2)}, u32[]{:S(2)}) collective-permute-start(bf16[4,96,1280]{2,1,0:T(8,128)(2,1)S(1)} %fusion.3), channel_id=1, source_target_pairs={{0,4},{1,5},{2,6},{3,7},{4,0},{5,1},{6,2},{7,3},{8,12},{9,13},{10,... | collective-permute-start | bytes 2949128 | tf_op jit(solution)/shard_map/ppermute | solution.py:553
  35.4 12.5 %collective-permute-start.4 = (bf16[48,1920]{1,0:T(8,128)(2,1)S(1)}, bf16[48,1920]{1,0:T(8,128)(2,1)S(1)}, u32[]{:S(2)}, u32[]{:S(2)}) collective-permute-start(bf16[48,1920]{1,0:T(8,128)(2,1)S(1)} %pad_maximum_fusion.7), channel_id=1, source_target_pairs={{0,16},{1,17},{2,18},{3,19},{4,20},{5,21},{6,22},{7,23},{8,24},{9,... | collective-permute-start | bytes 552968 | tf_op jit(solution)/shard_map/ppermute | solution.py:553
  53.3 53.7 %collective-permute-start.11 = (bf16[768,1280]{1,0:T(8,128)(2,1)S(1)}, bf16[768,1280]{1,0:T(8,128)(2,1)}, u32[]{:S(2)}, u32[]{:S(2)}) collective-permute-start(bf16[768,1280]{1,0:T(8,128)(2,1)S(1)} %bitcast_select_fusion.2.refs_1_.refs_2_.refs_5_), channel_id=1, source_target_pairs={{0,1},{1,0},{2,3},{3,2},{4,5},{5,4},{6,7},{7,6},{8,9},{9,8},{10,11... | collective-permute-start | bytes 5898248 | tf_op jit(solution)/shard_map/ppermute | solution.py:553
  53.7 19.0 %collective-permute-start.12 = (bf16[4,48,1920]{2,1,0:T(8,128)(2,1)S(1)}, bf16[4,48,1920]{2,1,0:T(8,128)(2,1)}, u32[]{:S(2)}, u32[]{:S(2)}) collective-permute-start(bf16[4,48,1920]{2,1,0:T(8,128)(2,1)S(1)} %fusion.6), channel_id=1, source_target_pairs={{0,4},{1,5},{2,6},{3,7},{4,0},{5,1},{6,2},{7,3},{8,12},{9,13},{10,... | collective-permute-start | bytes 2211848 | tf_op jit(solution)/shard_map/ppermute | solution.py:553
  56.7 17.5 %collective-permute-start.10 = (bf16[192,768]{1,0:T(8,128)(2,1)S(1)}, bf16[192,768]{1,0:T(8,128)(2,1)S(1)}, u32[]{:S(2)}, u32[]{:S(2)}) collective-permute-start(bf16[192,768]{1,0:T(8,128)(2,1)S(1)} %fusion.18), channel_id=1, source_target_pairs={{0,24},{1,25},{2,26},{3,27},{4,28},{5,29},{6,30},{7,31},{8,0},{9,1... | collective-permute-start | bytes 884744 | tf_op jit(solution)/shard_map/ppermute | solution.py:553
  61.1 14.6 %collective-permute-start.8 = (bf16[192,768]{1,0:T(8,128)(2,1)S(1)}, bf16[192,768]{1,0:T(8,128)(2,1)S(1)}, u32[]{:S(2)}, u32[]{:S(2)}) collective-permute-start(bf16[192,768]{1,0:T(8,128)(2,1)S(1)} %fusion.18), channel_id=1, source_target_pairs={{0,8},{1,9},{2,10},{3,11},{4,12},{5,13},{6,14},{7,15},{8,16},{9,17... | collective-permute-start | bytes 884744 | tf_op jit(solution)/shard_map/ppermute | solution.py:553
  61.3 27.3 %collective-permute-start.9 = (bf16[192,768]{1,0:T(8,128)(2,1)S(1)}, bf16[192,768]{1,0:T(8,128)(2,1)S(1)}, u32[]{:S(2)}, u32[]{:S(2)}) collective-permute-start(bf16[192,768]{1,0:T(8,128)(2,1)S(1)} %fusion.18), channel_id=1, source_target_pairs={{0,16},{1,17},{2,18},{3,19},{4,20},{5,21},{6,22},{7,23},{8,24},{9,... | collective-permute-start | bytes 884744 | tf_op jit(solution)/shard_map/ppermute | solution.py:553
  72.8 21.8 %collective-permute-start.7 = (bf16[4,48,1920]{2,1,0:T(8,128)(2,1)S(1)}, bf16[4,48,1920]{2,1,0:T(8,128)(2,1)}, u32[]{:S(2)}, u32[]{:S(2)}) collective-permute-start(bf16[4,48,1920]{2,1,0:T(8,128)(2,1)S(1)} %fusion.6), channel_id=1, source_target_pairs={{0,2},{1,3},{2,0},{3,1},{4,6},{5,7},{6,4},{7,5},{8,10},{9,11},{10,... | collective-permute-start | bytes 2211848 | tf_op jit(solution)/shard_map/ppermute | solution.py:553
  89.4 28.9 %collective-permute-start.13 = (bf16[4,48,1920]{2,1,0:T(8,128)(2,1)}, bf16[4,48,1920]{2,1,0:T(8,128)(2,1)}, u32[]{:S(2)}, u32[]{:S(2)}) collective-permute-start(bf16[4,48,1920]{2,1,0:T(8,128)(2,1)} %collective-permute-done.12), channel_id=1, source_target_pairs={{0,2},{1,3},{2,0},{3,1},{4,6},{5,7},{6,4},{7,5},{8,10},{9,11},{10,... | collective-permute-start | bytes 2211848 | tf_op jit(solution)/shard_map/ppermute | solution.py:553
  94.1 27.3 %collective-permute-start.15 = (bf16[4,192,768]{2,1,0:T(8,128)(2,1)}, bf16[4,192,768]{2,1,0:T(8,128)(2,1)}, u32[]{:S(2)}, u32[]{:S(2)}) collective-permute-start(bf16[4,192,768]{2,1,0:T(8,128)(2,1)} %fusion), channel_id=1, source_target_pairs={{0,4},{1,5},{2,6},{3,7},{4,0},{5,1},{6,2},{7,3},{8,12},{9,13},{10,... | collective-permute-start | bytes 3538952 | tf_op jit(solution)/shard_map/ppermute | solution.py:553
  123.6 31.8 %collective-permute-start.16 = (bf16[1536,768]{1,0:T(8,128)(2,1)S(1)}, bf16[1536,768]{1,0:T(8,128)(2,1)}, u32[]{:S(2)}, u32[]{:S(2)}) collective-permute-start(bf16[1536,768]{1,0:T(8,128)(2,1)S(1)} %bitcast_select_fusion.1.refs_3_), channel_id=1, source_target_pairs={{0,1},{1,0},{2,3},{3,2},{4,5},{5,4},{6,7},{7,6},{8,9},{9,8},{10,11... | collective-permute-start | bytes 7077896 | tf_op jit(solution)/shard_map/ppermute | solution.py:553
  191.0 35.7 %collective-permute-start.22 = (bf16[4,2,48,1536]{3,2,0,1:T(8,128)(2,1)S(1)}, bf16[4,2,48,1536]{3,2,0,1:T(8,128)(2,1)S(1)}, u32[]{:S(2)}, u32[]{:S(2)}) collective-permute-start(bf16[4,2,48,1536]{3,2,0,1:T(8,128)(2,1)S(1)} %get-tuple-element.193), channel_id=1, source_target_pairs={{0,2},{1,3},{2,0},{3,1},{4,6},{5,7},{6,4},{7,5},{8,10},{9,11},{10,... | collective-permute-start | bytes 3538952 | tf_op jit(solution)/shard_map/ppermute | solution.py:553
  191.6 35.1 %collective-permute-start.21 = (bf16[4,2,48,1536]{3,2,0,1:T(8,128)(2,1)}, bf16[4,2,48,1536]{3,2,0,1:T(8,128)(2,1)S(1)}, u32[]{:S(2)}, u32[]{:S(2)}) collective-permute-start(bf16[4,2,48,1536]{3,2,0,1:T(8,128)(2,1)} %fusion.11), channel_id=1, source_target_pairs={{0,4},{1,5},{2,6},{3,7},{4,0},{5,1},{6,2},{7,3},{8,12},{9,13},{10,... | collective-permute-start | bytes 3538952 | tf_op jit(solution)/shard_map/ppermute | solution.py:553
  203.5 23.2 %collective-permute-start.23 = (bf16[768,384]{1,0:T(8,128)(2,1)}, bf16[768,384]{1,0:T(8,128)(2,1)}, u32[]{:S(2)}, u32[]{:S(2)}) collective-permute-start(bf16[768,384]{1,0:T(8,128)(2,1)} %get-tuple-element.142), channel_id=1, source_target_pairs={{0,1},{1,0},{2,3},{3,2},{4,5},{5,4},{6,7},{7,6},{8,9},{9,8},{10,11... | collective-permute-start | bytes 1769480 | tf_op jit(solution)/shard_map/ppermute | solution.py:553
  228.0 33.7 %collective-permute-start.25 = (bf16[4,48,1536]{2,1,0:T(8,128)(2,1)S(1)}, bf16[4,48,1536]{2,1,0:T(8,128)(2,1)}, u32[]{:S(2)}, u32[]{:S(2)}) collective-permute-start(bf16[4,48,1536]{2,1,0:T(8,128)(2,1)S(1)} %select_bitcast_fusion.6), channel_id=1, source_target_pairs={{0,4},{1,5},{2,6},{3,7},{4,0},{5,1},{6,2},{7,3},{8,12},{9,13},{10,... | collective-permute-start | bytes 1769480 | tf_op jit(solution)/shard_map/ppermute | solution.py:553
  228.8 32.8 %collective-permute-start.24 = (bf16[4,48,1536]{2,1,0:T(8,128)(2,1)S(1)}, bf16[4,48,1536]{2,1,0:T(8,128)(2,1)}, u32[]{:S(2)}, u32[]{:S(2)}) collective-permute-start(bf16[4,48,1536]{2,1,0:T(8,128)(2,1)S(1)} %fusion.15), channel_id=1, source_target_pairs={{0,2},{1,3},{2,0},{3,1},{4,6},{5,7},{6,4},{7,5},{8,10},{9,11},{10,... | collective-permute-start | bytes 1769480 | tf_op jit(solution)/shard_map/ppermute | solution.py:553
  230.5 40.0 %all-to-all-start.1 = ((bf16[4,256,768]{2,1,0:T(8,128)(2,1)}), bf16[4,256,768]{2,1,0:T(8,128)(2,1)}, u32[]{:S(2)}, u32[]{:S(2)}) async-start(bf16[4,256,768]{2,1,0:T(8,128)(2,1)} %bitcast.147), calls=%async_computation.1 | async-start | bytes 3145728 | tf_op jit(solution)/shard_map/all_to_all | solution.py:615
  264.4 19.8 %collective-permute-start.27 = (bf16[4,2,48,896]{3,2,0,1:T(8,128)(2,1)}, bf16[4,2,48,896]{3,2,0,1:T(8,128)(2,1)}, u32[]{:S(2)}, u32[]{:S(2)}) collective-permute-start(bf16[4,2,48,896]{3,2,0,1:T(8,128)(2,1)} %get-tuple-element.195), channel_id=1, source_target_pairs={{0,4},{1,5},{2,6},{3,7},{4,0},{5,1},{6,2},{7,3},{8,12},{9,13},{10,... | collective-permute-start | bytes 2064392 | tf_op jit(solution)/shard_map/ppermute | solution.py:553
  268.5 15.7 %collective-permute-start.26 = (bf16[4,2,48,768]{3,2,0,1:T(8,128)(2,1)}, bf16[4,2,48,768]{3,2,0,1:T(8,128)(2,1)}, u32[]{:S(2)}, u32[]{:S(2)}) collective-permute-start(bf16[4,2,48,768]{3,2,0,1:T(8,128)(2,1)} %get-tuple-element.197), channel_id=1, source_target_pairs={{0,2},{1,3},{2,0},{3,1},{4,6},{5,7},{6,4},{7,5},{8,10},{9,11},{10,... | collective-permute-start | bytes 1769480 | tf_op jit(solution)/shard_map/ppermute | solution.py:553
  274.0 15.2 %collective-permute-start.32 = (bf16[48,3072]{1,0:T(8,128)(2,1)S(1)}, bf16[48,3072]{1,0:T(8,128)(2,1)S(1)}, u32[]{:S(2)}, u32[]{:S(2)}) collective-permute-start(bf16[48,3072]{1,0:T(8,128)(2,1)S(1)} %pad_maximum_fusion.6), channel_id=1, source_target_pairs={{0,24},{1,25},{2,26},{3,27},{4,28},{5,29},{6,30},{7,31},{8,0},{9,1... | collective-permute-start | bytes 884744 | tf_op jit(solution)/shard_map/ppermute | solution.py:553
  277.8 26.9 %collective-permute-start.31 = (bf16[48,3072]{1,0:T(8,128)(2,1)S(1)}, bf16[48,3072]{1,0:T(8,128)(2,1)S(1)}, u32[]{:S(2)}, u32[]{:S(2)}) collective-permute-start(bf16[48,3072]{1,0:T(8,128)(2,1)S(1)} %pad_maximum_fusion.5), channel_id=1, source_target_pairs={{0,16},{1,17},{2,18},{3,19},{4,20},{5,21},{6,22},{7,23},{8,24},{9,... | collective-permute-start | bytes 884744 | tf_op jit(solution)/shard_map/ppermute | solution.py:553
  279.3 25.3 %collective-permute-start.30 = (bf16[48,3072]{1,0:T(8,128)(2,1)S(1)}, bf16[48,3072]{1,0:T(8,128)(2,1)S(1)}, u32[]{:S(2)}, u32[]{:S(2)}) collective-permute-start(bf16[48,3072]{1,0:T(8,128)(2,1)S(1)} %pad_maximum_fusion.4), channel_id=1, source_target_pairs={{0,8},{1,9},{2,10},{3,11},{4,12},{5,13},{6,14},{7,15},{8,16},{9,17... | collective-permute-start | bytes 884744 | tf_op jit(solution)/shard_map/ppermute | solution.py:553
  285.5 19.4 %collective-permute-start.29 = (bf16[4,48,896]{2,1,0:T(8,128)(2,1)S(1)}, bf16[4,48,896]{2,1,0:T(8,128)(2,1)S(1)}, u32[]{:S(2)}, u32[]{:S(2)}) collective-permute-start(bf16[4,48,896]{2,1,0:T(8,128)(2,1)S(1)} %select_bitcast_fusion.7), channel_id=1, source_target_pairs={{0,2},{1,3},{2,0},{3,1},{4,6},{5,7},{6,4},{7,5},{8,10},{9,11},{10,... | collective-permute-start | bytes 1032200 | tf_op jit(solution)/shard_map/ppermute | solution.py:553
  288.4 16.4 %collective-permute-start.28 = (bf16[4,48,768]{2,1,0:T(8,128)(2,1)S(1)}, bf16[4,48,768]{2,1,0:T(8,128)(2,1)S(1)}, u32[]{:S(2)}, u32[]{:S(2)}) collective-permute-start(bf16[4,48,768]{2,1,0:T(8,128)(2,1)S(1)} %select_bitcast_fusion.8), channel_id=1, source_target_pairs={{0,4},{1,5},{2,6},{3,7},{4,0},{5,1},{6,2},{7,3},{8,12},{9,13},{10,... | collective-permute-start | bytes 884744 | tf_op jit(solution)/shard_map/ppermute | solution.py:553
  309.9 24.1 %all-to-all-start.2 = ((bf16[4,256,768]{2,1,0:T(8,128)(2,1)}), bf16[4,256,768]{2,1,0:T(8,128)(2,1)S(1)}, u32[]{:S(2)}, u32[]{:S(2)}) async-start(bf16[4,256,768]{2,1,0:T(8,128)(2,1)} %bitcast.62), calls=%async_computation.2 | async-start | bytes 3145728 | tf_op jit(solution)/shard_map/all_to_all | solution.py:615
  313.7 15.9 %collective-permute-start.34 = (bf16[48,1664]{1,0:T(8,128)(2,1)}, bf16[48,1664]{1,0:T(8,128)(2,1)S(1)}, u32[]{:S(2)}, u32[]{:S(2)}) collective-permute-start(bf16[48,1664]{1,0:T(8,128)(2,1)} %pad_maximum_fusion.9), channel_id=1, source_target_pairs={{0,16},{1,17},{2,18},{3,19},{4,20},{5,21},{6,22},{7,23},{8,24},{9,... | collective-permute-start | bytes 479240 | tf_op jit(solution)/shard_map/ppermute | solution.py:553
  314.5 15.8 %collective-permute-start.33 = (bf16[48,1664]{1,0:T(8,128)(2,1)}, bf16[48,1664]{1,0:T(8,128)(2,1)}, u32[]{:S(2)}, u32[]{:S(2)}) collective-permute-start(bf16[48,1664]{1,0:T(8,128)(2,1)} %pad_maximum_fusion.8), channel_id=1, source_target_pairs={{0,8},{1,9},{2,10},{3,11},{4,12},{5,13},{6,14},{7,15},{8,16},{9,17... | collective-permute-start | bytes 479240 | tf_op jit(solution)/shard_map/ppermute | solution.py:553
  317.5 19.7 %collective-permute-start.40 = (bf16[2,48,3072]{2,1,0:T(8,128)(2,1)S(1)}, bf16[2,48,3072]{2,1,0:T(8,128)(2,1)S(1)}, u32[]{:S(2)}, u32[]{:S(2)}) collective-permute-start(bf16[2,48,3072]{2,1,0:T(8,128)(2,1)S(1)} %broadcast_select_fusion.3), channel_id=1, source_target_pairs={{0,1},{1,0},{2,3},{3,2},{4,5},{5,4},{6,7},{7,6},{8,9},{9,8},{10,11... | collective-permute-start | bytes 1769480 | tf_op jit(solution)/shard_map/ppermute | solution.py:553
  (46 other events, 313.9 us)

commit v3 on v2

--- a/solution.py
+++ b/solution.py
@@ -270,18 +270,24 @@
     )(value, weight, *((weight,) if first else ()))
 
 
-def attend_back_kernel(carry, final, *refs):
+def attend_back_kernel(carry, final, part, *refs):
+    if part:
+        where_ref, *refs = refs
     mixed_ref, do_ref, o_ref, l_ref, low_ref, w_ref, *refs = refs
     if carry:
         grad_in, *refs = refs
     if final:
         x_ref, mid_ref, table_ref, norm_two, *refs = refs
-    gq_ref, more_ref, *refs = refs
+    if part:
+        core_ref, core_more, gp_ref, gp_core, *refs = refs
+        left_out, left_keep, right_out, right_keep, *refs = refs
+    else:
+        gq_ref, more_ref, *refs = refs
     if final:
         out_ref, norm_ref, *refs = refs
     else:
         grad_ref, *refs = refs
-    sum_k, sum_v, both, every = refs
+    sum_k, sum_v, both, every, *sums = refs
     q_ref, k_ref, v_ref = (mixed_ref.at[:, 128 * i : 128 * (i + 1)] for i in range(3))
     dq_ref, dk_ref, dv_ref = (both.at[:, 128 * i : 128 * (i + 1)] for i in range(3))
     seq = mixed_ref.shape[0]
@@ -330,13 +336,29 @@
     grad_qkv = dot_tn(low_ref[...], both[...]).astype(BF16)
     every[:, here] = both[...]
 
+    def cut(out, keep, columns, source, size, index):
+        for block in range(source.shape[0] // (2 * size)):
+            to = pl.ds(block * size, size)
+            for ref, side in ((out, 1 - index), (keep, index)):
+                start = pl.multiple_of(block * 2 * size + side * size, 16)
+                ref[to, columns] = source[pl.ds(start, size), :]
+
     @pl.when(step < pl.num_programs(0) - 1)
     def _():
-        gq_ref[:, here] = grad_qkv
+        if part:
+            sums[0][...] = (grad_qkv.astype(F32) + core_ref[:, here].astype(F32)).astype(BF16)
+            cut(left_out, left_keep, here, sums[0], part, where_ref[0])
+        else:
+            gq_ref[:, here] = grad_qkv
 
     @pl.when(step == pl.num_programs(0) - 1)
     def _():
-        more_ref[:, :384] = grad_qkv
+        if part:
+            sums[1][:, :384] = (
+                grad_qkv.astype(F32) + core_more[:, :384].astype(F32)
+            ).astype(BF16)
+        else:
+            more_ref[:, :384] = grad_qkv
 
 
     @pl.when(step == pl.num_programs(0) - 1)
@@ -359,38 +381,66 @@
         tail = jnp.zeros((128, low_ref.shape[1]), F32)
         if final:
             tail = jnp.concatenate([norm_ref[:2], norm_two[:2], tail[4:]], axis=0)
-        more_ref[:, 384:] = tail.T.astype(BF16)
-
-
-def attend_back(mixed, grad, attended, logs, low, weight, start, pairs, carry=None, final=()):
+        if part:
+            sums[1][:, 384:512] = (tail.T + core_more[:, 384:].astype(F32)).astype(BF16)
+            sums[1][:, 512:] = (gp_ref[...].astype(F32) + gp_core[...].astype(F32)).astype(BF16)
+            cut(right_out, right_keep, slice(None), sums[1], 2 * part, where_ref[1])
+        else:
+            more_ref[:, 384:] = tail.T.astype(BF16)
+
+
+def attend_back(
+    mixed, grad, attended, logs, low, weight, pairs, carry=None, final=(), where=None, others=(), part=0
+):
     seq, dim = low.shape
     group = 3 * 128
+    wide = pairs * group
 
     def column(width):
-        return pl.BlockSpec((seq, width), lambda i: (0, start + i))
+        return pl.BlockSpec((seq, width), lambda i, *_: (0, i))
 
     more = [whole(seq, dim)] if carry is not None else []
     more += [part_of(final[0], 0), whole(seq, dim), whole(8, dim), whole(8, dim)] if final else []
-    wide = pairs * group
+    more += [whole(*other.shape) for other in others]
     widths = [wide - group, group + 128]
+    outs = [(dim, width) for width in widths]
+    scratch = [pltpu.VMEM((seq, 128), F32)] * 2
+    scratch += [pltpu.VMEM((seq, group), BF16), pltpu.VMEM((seq, wide), BF16)]
+    if part:
+        widths[1] += others[2].shape[1]
+        outs = [(dim // 2, width) for width in widths for _ in range(2)]
+        scratch += [pltpu.VMEM((dim, group), BF16), pltpu.VMEM((dim, widths[1]), BF16)]
     return pl.pallas_call(
-        functools.partial(attend_back_kernel, carry is not None, bool(final)),
-        grid=(pairs,),
-        in_specs=[column(group), column(128), column(128)]
-        + [pl.BlockSpec((1, 2, seq), lambda i: (start + i, 0, 0)), whole(seq, dim)]
-        + [pl.BlockSpec((dim, wide), lambda i: (0, start // pairs))]
-        + more,
-        out_specs=[whole(dim, width) for width in widths]
-        + [whole(seq, dim)]
-        + ([whole(8, dim)] if final else []),
-        out_shape=[shaped((dim, width), BF16) for width in widths]
+        functools.partial(attend_back_kernel, carry is not None, bool(final), part),
+        grid_spec=pltpu.PrefetchScalarGridSpec(
+            num_scalar_prefetch=1 if part else 0,
+            grid=(pairs,),
+            in_specs=[column(group), column(128), column(128)]
+            + [pl.BlockSpec((1, 2, seq), lambda i, *_: (i, 0, 0)), whole(seq, dim)]
+            + [whole(dim, wide)]
+            + more,
+            out_specs=[whole(*shape) for shape in outs]
+            + [whole(seq, dim)]
+            + ([whole(8, dim)] if final else []),
+            scratch_shapes=scratch,
+        ),
+        out_shape=[shaped(shape, BF16) for shape in outs]
         + [shaped((seq, dim), BF16)]
         + ([shaped((8, dim), F32)] if final else []),
-        scratch_shapes=[pltpu.VMEM((seq, 128), F32)] * 2
-        + [pltpu.VMEM((seq, group), BF16), pltpu.VMEM((seq, wide), BF16)],
         compiler_params=params(58),
         cost_estimate=cost(0.01),
-    )(mixed, grad, attended, logs, low, weight, *(() if carry is None else (carry,)), *final)
+    )(
+        *((where,) if part else ()),
+        mixed,
+        grad,
+        attended,
+        logs,
+        low,
+        weight,
+        *(() if carry is None else (carry,)),
+        *final,
+        *others,
+    )
 
 
 def ffn_kernel(final, paired, *refs):
@@ -522,6 +572,22 @@
         norm_ref[...] = sums[place : place + 1].reshape(norm_ref.shape)
 
 
+def settle_kernel(in_ref, out_ref):
+    out_ref[...] = in_ref[...]
+
+
+def settle(value):
+    spec = pl.BlockSpec((1,) + value.shape[1:], lambda i: (i, 0, 0))
+    return pl.pallas_call(
+        settle_kernel,
+        grid=value.shape[:1],
+        in_specs=[spec],
+        out_specs=spec,
+        out_shape=shaped(value.shape, value.dtype),
+        cost_estimate=cost(0.01),
+    )(value)
+
+
 def finish(kernel, where, pieces, *shapes):
     return pl.pallas_call(
         kernel,
@@ -571,6 +637,13 @@
         for step in range(1, self.z_count):
             out = jnp.where(steps == step, jnp.broadcast_to(got[step], shape), out)
         return out
+
+    def over_z(self, piece):
+        copies = jnp.broadcast_to(piece, (self.z_count,) + piece.shape)
+        groups = [list(range(y, self.z_count * 2, 2)) for y in range(2)]
+        return lax.all_to_all(
+            copies, "dp", split_axis=0, concat_axis=0, tiled=True, axis_index_groups=groups
+        )
 
     def over_y(self, value, got):
         return self.join(value, got, self.y, 1)
@@ -660,6 +733,7 @@
     proj = grid.pick(row_half(proj_weight).reshape(part, 2, half), 1, grid.c)
     up_piece = jnp.concatenate([up.reshape(part, -1), proj], axis=1).astype(BF16)
     down_piece = grid.pick(down_weight.reshape(2, fan, dim), 0, grid.c).astype(BF16)
+    where = jnp.stack([grid.x, grid.y]).astype(jnp.int32)
     where_head = jnp.stack([grid.x, grid.c]).astype(jnp.int32)
 
     both = exchange(after(jnp.stack([tokens, cotangent], axis=1), piece))
@@ -669,34 +743,34 @@
     w_theirs = grid.send(w_mine, c=1)
     up_z = grid.by_z(after(up_got, w_mine))
     up_y = grid.send(up_z, y=1)
-    down_got = grid.to_z(after(down_piece, w_mine, both))
-
     up_x = grid.send(up_z, x=1)
-    up_xy = grid.send(after(up_y, down_got), x=1)
-    down_z = grid.by_z(after(down_got, up_z))
-    down_y = grid.send(down_z, y=1)
+    down_both = grid.join(
+        down_piece, grid.send(after(down_piece, up_got), y=1), grid.y, 0
+    )
+    down_mine = grid.over_z(after(down_both, both))
     low, mixed_mine, att_mine, log_mine, table = attend(
-        after(both, up_x, down_z), w_mine, pairs, True
+        after(both, up_z), w_mine, pairs, True
     )
     mixed_theirs, att_theirs, log_theirs = attend(low, w_theirs, pairs, False)
+    up_y, up_x = after((up_y, up_x), att_mine, att_theirs)
+    up_xy = grid.send(up_y, x=1)
     up_y = grid.over_y(up_z, up_y)
-    up_x = grid.over_y(up_x, after(up_xy, att_theirs))
+    up_x = grid.over_y(up_x, up_xy)
     up_mine = flat(grid.over_x(up_y, up_x, 2))
     up_theirs = grid.send(up_mine, c=1)
-    down_mine = flat(grid.over_y(down_z, after(down_y, att_theirs)))
+    down_mine = flat(after(down_mine, up_xy))
     down_theirs = grid.send(down_mine, c=1)
     middle, low_two = project(core, both, att_mine, att_theirs, up_mine, up_theirs, table)
-    out, back, gu_mine, gd_mine = feed_forward(
-        low_two, both, up_mine, after(down_mine, low_two), middle, part
-    )
     out, back, gu_theirs, gd_theirs = feed_forward(
-        low_two, both, up_theirs, after(down_theirs, back), out, part, back
-    )
+        low_two, both, up_theirs, after(down_theirs, low_two), middle, part
+    )
+    gd_core, gu_core = grid.send(gd_theirs, c=1), grid.send(gu_theirs, c=1)
+    out, back, gu_mine, gd_mine = feed_forward(low_two, both, up_mine, down_mine, out, part, back)
+    gd_core, gu_core = after((gd_core, gu_core), back)
 
     def blocks(value):
         return value.reshape(grid.z_count, 2, 2, -1, value.shape[-1])
 
-    gd_core, gu_core = grid.send(gd_theirs, c=1), grid.send(gu_theirs, c=1)
     gd_out, gd_keep = grid.halves("y", [blocks(gd_mine), blocks(gd_core)])
     gd_got = grid.send(gd_out, y=1)
     gu_out, gu_keep = grid.halves("x", [blocks(gu_mine), blocks(after(gu_core, gd_out))])
@@ -707,7 +781,7 @@
     )
     gp_core = grid.send(gp_theirs, c=1)
     gq_theirs, gq_rest, grad_low = attend_back(
-        mixed_theirs, ga_theirs, att_theirs, log_theirs, low, w_theirs, 0, pairs
+        mixed_theirs, ga_theirs, att_theirs, log_theirs, low, w_theirs, pairs
     )
     gq_core = [grid.send(value, c=1) for value in (gq_theirs, gq_rest)]
     gd_got, gu_got, gp_core = after((gd_got, gu_got, gp_core), grad_low)
@@ -716,26 +790,32 @@
     gu_out, gu_keep = grid.halves("y", [gu_keep, gu_got])
     gu_got = grid.send(gu_out, y=1)
     out_home = exchange(after(out.reshape(4, SEQ // 4, dim), gd_out, gu_out))
-    gq_mine, gq_more, grad_x, _ = attend_back(
-        mixed_mine, after(ga_mine, gd_out, gu_out, gq_core, gp_core), att_mine, log_mine, low,
-        w_mine, 0, pairs, carry=grad_low, final=(both, grad_middle, table, norm_two),
-    )
-    gq_core, gd_got, gu_got = after((gq_core, gd_got, gu_got), gq_mine)
-    left_out, left_keep = grid.halves(
-        "x", [blocks(gq_mine), blocks(gq_core[0])]
-    )
-    left_got = grid.send(left_out, x=1)
-    right_out, right_keep = grid.halves(
-        "y",
-        [
-            jnp.concatenate([blocks(gq_more), blocks(gp_mine)], axis=-1),
-            jnp.concatenate([blocks(gq_core[1]), blocks(gp_core)], axis=-1),
-        ],
-    )
-    right_got = grid.send(right_out, y=1)
+    mine = (mixed_mine, after(ga_mine, gd_out, gu_out), att_mine, log_mine, low, w_mine, pairs)
+    final = (both, grad_middle, table, norm_two)
+    if part % 16 == 0:
+        *cuts, grad_x, _ = attend_back(
+            *mine, grad_low, final, where, (*gq_core, gp_mine, gp_core), part
+        )
+        left_out, left_keep, right_out, right_keep = cuts
+    else:
+        gq_mine, gq_more, grad_x, _ = attend_back(*mine, grad_low, final)
+        left_out, left_keep = grid.halves("x", [blocks(gq_mine), blocks(gq_core[0])])
+        right_out, right_keep = grid.halves(
+            "y",
+            [
+                jnp.concatenate([blocks(gq_more), blocks(gp_mine)], axis=-1),
+                jnp.concatenate([blocks(gq_core[1]), blocks(gp_core)], axis=-1),
+            ],
+        )
+    left_got, right_got = grid.send(left_out, x=1), grid.send(right_out, y=1)
+    left_keep, left_got, right_keep, right_got = (
+        value.reshape(grid.z_count, 2, part, -1)
+        for value in (left_keep, left_got, right_keep, right_got)
+    )
     gd_got, gu_got, out_home = after((gd_got, gu_got, out_home), left_out, right_out)
+    out_home = settle(out_home)
     ffn_parts = grid.by_block((gu_keep, gu_got), (gd_keep, gd_got))
-    left_got, right_got = after((left_got, right_got), ffn_parts)
+    left_got, right_got = after((left_got, right_got), ffn_parts, out_home)
     ffn_got = [grid.send(part, z=step) for step, part in enumerate(ffn_parts) if step]
     left_out, left_keep = grid.halves("y", [left_keep, left_got])
     left_got = grid.send(left_out, y=1)

time: 357 us -> 342 us (0.958)
  waiting for transfers between devices: 84.5 us -> 72.4 us
  other arithmetic: 40.3 us -> 32.8 us
  Pallas kernels: 141 us -> 147 us
    ppermute x41 -> x38, waiting for transfers between devices: 79.3 us -> 63.5 us  [send(): return lax.ppermute(value, BOTH, pairs)]
    all_to_all x0 -> x1, starting transfers between devices: none -> 7.36 us  [over_z(): lax.all_to_all(copies, 'dp', split_axis=0, concat_axis=0, tiled=True, axi...]
    all_to_all x0 -> x1, waiting for transfers between devices: none -> 6.59 us  [over_z(): lax.all_to_all(copies, 'dp', split_axis=0, concat_axis=0, tiled=True, axi...]
    ppermute x41 -> x38, starting transfers between devices: 50.3 us -> 44.3 us  [send(): return lax.ppermute(value, BOTH, pairs)]
    pallas_call x0 -> x1, Pallas kernels: none -> 3.76 us  [settle(): pl.pallas_call(settle_kernel, grid=value.shape[:1], in_specs=[spec], out_...]
    select_n x9 -> x7, other arithmetic: 9.37 us -> 8.47 us  [halves(): return (jnp.where(index == 0, high, low), jnp.where(index == 0, low, high))]
    unnamed x70 -> x65, local copies, waits for them, and re-layouts: 7.54 us -> 6.82 us
  transfers between devices with their start and end apart: 44 -> 42, of which waited for: 18 -> 13; matrix products, arithmetic and copies ran while one was open for 12% -> 9% of each run, Pallas kernels for 33% -> 36%
where the time goes in v3:
time: 342 us; the launch traced here: 336 us
  Pallas kernels  147 us (43%)
  waiting for transfers between devices  72.4 us (21%)
  starting transfers between devices  64.5 us (19%)
  other arithmetic  32.8 us (10%)
  local copies, waits for them, and re-layouts  18.1 us (5%)
    ppermute x38, waiting for transfers between devices, send(): return lax.ppermute(value, BOTH, pairs)  63.5 us
    pallas_call x2, Pallas kernels, attend_back(): pl.pallas_call(functools.partial(attend_back_kernel, carry is not None, b...  49.9 us
    pallas_call x2, Pallas kernels, feed_forward(): pl.pallas_call(functools.partial(ffn_kernel, int(final), paired), grid=(2...  46 us
    ppermute x38, starting transfers between devices, send(): return lax.ppermute(value, BOTH, pairs)  44.3 us
    pallas_call x2, Pallas kernels, attend(): pl.pallas_call(functools.partial(attend_kernel, first), grid=(pairs,), in...  23.6 us
    all_to_all x3, starting transfers between devices, exchange(): lax.all_to_all(value, 'head', split_axis=0, concat_axis=0, tiled=True)  12.8 us
    pallas_call x1, Pallas kernels, middle_back(): pl.pallas_call(middle_kernel, grid_spec=pltpu.PrefetchScalarGridSpec(num_...  10.3 us
    select_n x7, other arithmetic, halves(): return (jnp.where(index == 0, high, low), jnp.where(index == 0, low, high))  8.47 us
  transfers between devices with their start and end apart: 42, of which 13 were waited for; matrix products, arithmetic and copies ran while one was open for 9% of the time, Pallas kernels for 36%

profile of v3, /device:TPU:0, one launch (start us, length us, event | category | flops | bytes accessed | tf_op | source)
XLA Modules:
  0.0 336.2 jit_solution(14824272377979933017)
XLA Ops:
  4.7 3.1 collective-permute-start
  7.8 2.6 collective-permute-start.1
  11.7 3.4 pad_maximum_fusion
  15.1 4.7 %all-to-all-start = ((bf16[4,2,256,768]{3,2,1,0:T(8,128)(2,1)}), bf16[4,2,256,768]{3,2,1,0:T(8,128)(2,1)}, u32[]{:S(2)}, u32[]{:S(2)}) async-start(bf16[4,2,256,768]{3,2,1,0:T(8,128)(2,1)} %pad_maximum_fusion), calls=%async_computation | async-start | bytes 6291456 | tf_op jit(solution)/shard_map/all_to_all | solution.py:688
  24.0 2.5 collective-permute-done.1
  29.7 5.7 %collective-permute-start.3 = (bf16[48,1920]{1,0:T(8,128)(2,1)S(1)}, bf16[48,1920]{1,0:T(8,128)(2,1)S(1)}, u32[]{:S(2)}, u32[]{:S(2)}) collective-permute-start(bf16[48,1920]{1,0:T(8,128)(2,1)S(1)} %pad_maximum_fusion.5), channel_id=1, source_target_pairs={{0,8},{1,9},{2,10},{3,11},{4,12},{5,13},{6,14},{7,15},{8,16},{9,17... | collective-permute-start | bytes 552968 | tf_op jit(solution)/shard_map/ppermute | solution.py:619
  37.8 4.1 %collective-permute-done.3 = bf16[48,1920]{1,0:T(8,128)(2,1)S(1)} collective-permute-done((bf16[48,1920]{1,0:T(8,128)(2,1)S(1)}, bf16[48,1920]{1,0:T(8,128)(2,1)S(1)}, u32[]{:S(2)}, u32[]{:S(2)}) %collective-permute-start.3) | collective-permute-done | bytes 184352 | tf_op jit(solution)/shard_map/ppermute | solution.py:619
  41.9 6.0 %collective-permute-done.4 = bf16[48,1920]{1,0:T(8,128)(2,1)S(1)} collective-permute-done((bf16[48,1920]{1,0:T(8,128)(2,1)S(1)}, bf16[48,1920]{1,0:T(8,128)(2,1)S(1)}, u32[]{:S(2)}, u32[]{:S(2)}) %collective-permute-start.4) | collective-permute-done | bytes 184352 | tf_op jit(solution)/shard_map/ppermute | solution.py:619
  53.4 4.8 %collective-permute-done.12 = bf16[192,768]{1,0:T(8,128)(2,1)S(1)} collective-permute-done((bf16[192,768]{1,0:T(8,128)(2,1)S(1)}, bf16[192,768]{1,0:T(8,128)(2,1)S(1)}, u32[]{:S(2)}, u32[]{:S(2)}) %collective-permute-start.12) | collective-permute-done | bytes 294944 | tf_op jit(solution)/shard_map/ppermute | solution.py:619
  59.9 7.4 %all-to-all-start.1 = ((bf16[4,2,192,768]{3,2,1,0:T(8,128)(2,1)}), bf16[4,2,192,768]{3,2,1,0:T(8,128)(2,1)}, u32[]{:S(2)}, u32[]{:S(2)}) async-start(bf16[4,2,192,768]{3,2,1,0:T(8,128)(2,1)} %broadcast_in_dim.141), calls=%async_computation.1 | async-start | bytes 4718592 | tf_op jit(solution)/shard_map/all_to_all | solution.py:644
  70.6 12.4 %shard_map.177 = (bf16[1024,768]{1,0:T(8,128)(2,1)}, bf16[1024,1152]{1,0:T(8,128)(2,1)}, bf16[1024,384]{1,0:T(8,128)(2,1)}, f32[3,2,1024]{2,1,0:T(2,128)}, f32[8,768]{1,0:T(8,128)}) custom-call(bf16[4,2,256,768]{3,2,1,0:T(8,128)(2,1)} %all-to-all-done.refs_0_.x_ref.refs_1_.cot_ref.refs_8_, bf16[768,1280]{1,0:T(8,128)(2,1)} %copy-done.3, ...), custom_call_target="tpu_custom_call" | custom-call | flops 11000000 | bytes 30000 | tf_op jit(solution)/shard_map/pallas_call | solution.py:256
  83.1 11.2 %shard_map.178 = (bf16[1024,1152]{1,0:T(8,128)(2,1)}, bf16[1024,384]{1,0:T(8,128)(2,1)}, f32[3,2,1024]{2,1,0:T(2,128)}) custom-call(bf16[1024,768]{1,0:T(8,128)(2,1)} %get-tuple-element.109.refs_0_.refs_4_.refs_5_, bf16[768,1280]{1,0:T(8,128)(2,1)} %collective-permute-done.7.refs_1_.refs_5_), custom_call_target="tpu_custom_call" | custom-call | flops 11000000 | bytes 30000 | tf_op jit(solution)/shard_map/pallas_call | solution.py:256
  95.9 16.0 %collective-permute-done.10 = bf16[4,48,1920]{2,1,0:T(8,128)(2,1)S(1)} collective-permute-done((bf16[4,48,1920]{2,1,0:T(8,128)(2,1)S(1)}, bf16[4,48,1920]{2,1,0:T(8,128)(2,1)S(1)}, u32[]{:S(2)}, u32[]{:S(2)}) %collective-permute-start.10) | collective-permute-done | bytes 737312 | tf_op jit(solution)/shard_map/ppermute | solution.py:619
  113.9 6.6 %all-to-all-done.1 = bf16[4,2,192,768]{3,2,1,0:T(8,128)(2,1)} async-done(((bf16[4,2,192,768]{3,2,1,0:T(8,128)(2,1)}), bf16[4,2,192,768]{3,2,1,0:T(8,128)(2,1)}, u32[]{:S(2)}, u32[]{:S(2)}) %all-to-all-start.1) | async-done | bytes 2359328 | tf_op jit(solution)/shard_map/all_to_all | solution.py:644
  120.5 6.6 %shard_map.179 = (bf16[1024,768]{1,0:T(8,128)(2,1)}, bf16[1024,768]{1,0:T(8,128)(2,1)}) custom-call(s32[1]{0:T(128)} %bitcast.core_ref, bf16[4,2,256,768]{3,2,1,0:T(8,128)(2,1)} %all-to-all-done.refs_0_.x_ref.refs_1_.cot_ref.refs_8_, bf16[1024,384]{1,0:T(8,128)(2,1)} %get-tuple-element.108.am_ref.refs_3_, ...), custom_call_target="tpu_custom_call" | custom-call | flops 11000000 | bytes 30000 | tf_op jit(solution)/shard_map/pallas_call | solution.py:105
  128.4 22.7 %shard_map.180 = (f32[1024,768]{1,0:T(8,128)}, bf16[1024,768]{1,0:T(8,128)(2,1)}, bf16[768,1536]{1,0:T(8,128)(2,1)}, bf16[768,1536]{1,0:T(8,128)(2,1)}) custom-call(bf16[1024,768]{1,0:T(8,128)(2,1)} %get-tuple-element.114.refs_0_, bf16[4,2,256,768]{3,2,1,0:T(8,128)(2,1)} %all-to-all-done.refs_0_.x_ref.refs_1_.cot_ref.refs_8_, ...), custom_call_target="tpu_custom_call" | custom-call | flops 11000000 | bytes 30000 | tf_op jit(solution)/shard_map/pallas_call | solution.py:505
  151.7 23.3 %shard_map.181 = (bf16[1024,768]{1,0:T(8,128)(2,1)}, bf16[1024,768]{1,0:T(8,128)(2,1)}, bf16[768,1536]{1,0:T(8,128)(2,1)}, bf16[768,1536]{1,0:T(8,128)(2,1)}) custom-call(bf16[1024,768]{1,0:T(8,128)(2,1)} %get-tuple-element.114.refs_0_, bf16[4,2,256,768]{3,2,1,0:T(8,128)(2,1)} %all-to-all-done.refs_0_.x_ref.refs_1_.cot_ref.refs_8_, ...), custom_call_target="tpu_custom_call" | custom-call | flops 11000000 | bytes 30000 | tf_op jit(solution)/shard_map/pallas_call | solution.py:505
  175.0 2.0 fusion.32
  187.9 10.3 %shard_map.182 = (bf16[1024,768]{1,0:T(8,128)(2,1)}, bf16[1024,384]{1,0:T(8,128)(2,1)}, bf16[1024,384]{1,0:T(8,128)(2,1)}, bf16[768,384]{1,0:T(8,128)(2,1)}, bf16[768,384]{1,0:T(8,128)(2,1)}, /*index=5*/f32[8,768]{1,0:T(8,128)}) custom-call(s32[1]{0:T(128)} %bitcast.core_ref, bf16[1024,768]{1,0:T(8,128)(2,1)} %get-tuple-element.119.refs_4_.mid_ref, ...), custom_call_target="tpu_custom_call" | custom-call | flops 11000000 | bytes 30000 | tf_op jit(solution)/shard_map/pallas_call | solution.py:162
  198.4 22.3 %shard_map.183 = (bf16[768,768]{1,0:T(8,128)(2,1)}, bf16[768,512]{1,0:T(8,128)(2,1)}, bf16[1024,768]{1,0:T(8,128)(2,1)}) custom-call(bf16[1024,1152]{1,0:T(8,128)(2,1)} %get-tuple-element.132.refs_0_, bf16[1024,384]{1,0:T(8,128)(2,1)} %get-tuple-element.133.refs_1_, bf16[1024,384]{1,0:T(8,128)(2,1)} %get-tuple-element.110.at_ref.refs_2_, ...), custom_call_target="tpu_custom_call" | custom-call | flops 11000000 | bytes 30000 | tf_op jit(solution)/shard_map/pallas_call | solution.py:413
  223.5 4.5 %all-to-all-start.2 = ((bf16[4,256,768]{2,1,0:T(8,128)(2,1)}), bf16[4,256,768]{2,1,0:T(8,128)(2,1)}, u32[]{:S(2)}, u32[]{:S(2)}) async-start(bf16[4,256,768]{2,1,0:T(8,128)(2,1)} %bitcast.166), calls=%async_computation.2 | async-start | bytes 3145728 | tf_op jit(solution)/shard_map/all_to_all | solution.py:688
  231.4 27.6 %shard_map.184 = (bf16[384,768]{1,0:T(8,128)(2,1)}, bf16[384,768]{1,0:T(8,128)(2,1)}, bf16[384,896]{1,0:T(8,128)(2,1)}, bf16[384,896]{1,0:T(8,128)(2,1)}, bf16[1024,768]{1,0:T(8,128)(2,1)}, /*index=5*/f32[8,768]{1,0:T(8,128)}) custom-call(s32[2]{0:T(128)} %pad_add_fusion.refs_0_, bf16[1024,1152]{1,0:T(8,128)(2,1)} %get-tuple-element.140.refs_1_, ...), custom_call_target="tpu_custom_call" | custom-call | flops 11000000 | bytes 30000 | tf_op jit(solution)/shard_map/pallas_call | solution.py:413
  264.2 3.3 collective-permute-start.29
  268.3 3.8 %shard_map.185 = bf16[4,256,768]{2,1,0:T(8,128)(2,1)} custom-call(bf16[4,256,768]{2,1,0:T(8,128)(2,1)} %all-to-all-done.2.in_ref), custom_call_target="tpu_custom_call" | custom-call | flops 11000000 | bytes 30000 | tf_op jit(solution)/shard_map/pallas_call | solution.py:581
  272.0 3.6 %collective-permute-done.23 = bf16[384,768]{1,0:T(8,128)(2,1)} collective-permute-done((bf16[384,768]{1,0:T(8,128)(2,1)}, bf16[384,768]{1,0:T(8,128)(2,1)}, u32[]{:S(2)}, u32[]{:S(2)}) %collective-permute-start.23) | collective-permute-done | bytes 589856 | tf_op jit(solution)/shard_map/ppermute | solution.py:619
  281.7 11.1 %collective-permute-done.28 = bf16[48,3072]{1,0:T(8,128)(2,1)S(1)} collective-permute-done((bf16[48,3072]{1,0:T(8,128)(2,1)S(1)}, bf16[48,3072]{1,0:T(8,128)(2,1)S(1)}, u32[]{:S(2)}, u32[]{:S(2)}) %collective-permute-start.28) | collective-permute-done | bytes 294944 | tf_op jit(solution)/shard_map/ppermute | solution.py:619
  297.9 3.6 %all-to-all-start.3 = ((bf16[4,256,768]{2,1,0:T(8,128)(2,1)}), bf16[4,256,768]{2,1,0:T(8,128)(2,1)S(1)}, u32[]{:S(2)}, u32[]{:S(2)}) async-start(bf16[4,256,768]{2,1,0:T(8,128)(2,1)} %bitcast.167), calls=%async_computation.3 | async-start | bytes 3145728 | tf_op jit(solution)/shard_map/all_to_all | solution.py:688
  301.5 3.3 collective-permute-start.31
  308.2 11.8 %collective-permute-done.31 = bf16[48,1664]{1,0:T(8,128)(2,1)S(1)} collective-permute-done((bf16[48,1664]{1,0:T(8,128)(2,1)}, bf16[48,1664]{1,0:T(8,128)(2,1)S(1)}, u32[]{:S(2)}, u32[]{:S(2)}) %collective-permute-start.31) | collective-permute-done | bytes 159776 | tf_op jit(solution)/shard_map/ppermute | solution.py:619
  319.9 2.3 all-to-all-done.3
  328.6 3.6 %shard_map.186 = (f32[96,3072]{1,0:T(8,128)}, f32[384,768]{1,0:T(8,128)}) custom-call(s32[2]{0:T(128)} %pad_add_fusion.1.where_ref, bf16[2,2,48,3072]{3,2,1,0:T(8,128)(2,1)} %broadcast_select_fusion.2.all_ref), custom_call_target="tpu_custom_call" | custom-call | flops 11000000 | bytes 30000 | tf_op jit(solution)/shard_map/pallas_call | solution.py:592
  333.0 3.0 shard_map.187
  (194 shorter events, 75.4 us)
Async XLA Ops:
  4.7 19.3 %collective-permute-start = (bf16[96,1280]{1,0:T(8,128)(2,1)S(1)}, bf16[96,1280]{1,0:T(8,128)(2,1)}, u32[]{:S(2)}, u32[]{:S(2)}) collective-permute-start(bf16[96,1280]{1,0:T(8,128)(2,1)S(1)} %fusion.14), channel_id=1, source_target_pairs={{0,8},{1,9},{2,10},{3,11},{4,12},{5,13},{6,14},{7,15},{8,16},{9,17... | collective-permute-start | bytes 737288 | tf_op jit(solution)/shard_map/ppermute | solution.py:619
  7.8 18.8 %collective-permute-start.1 = (bf16[96,1280]{1,0:T(8,128)(2,1)S(1)}, bf16[96,1280]{1,0:T(8,128)(2,1)}, u32[]{:S(2)}, u32[]{:S(2)}) collective-permute-start(bf16[96,1280]{1,0:T(8,128)(2,1)S(1)} %fusion.14), channel_id=1, source_target_pairs={{0,16},{1,17},{2,18},{3,19},{4,20},{5,21},{6,22},{7,23},{8,24},{9,... | collective-permute-start | bytes 737288 | tf_op jit(solution)/shard_map/ppermute | solution.py:619
  10.4 16.2 %collective-permute-start.2 = (bf16[96,1280]{1,0:T(8,128)(2,1)S(1)}, bf16[96,1280]{1,0:T(8,128)(2,1)}, u32[]{:S(2)}, u32[]{:S(2)}) collective-permute-start(bf16[96,1280]{1,0:T(8,128)(2,1)S(1)} %fusion.14), channel_id=1, source_target_pairs={{0,24},{1,25},{2,26},{3,27},{4,28},{5,29},{6,30},{7,31},{8,0},{9,1... | collective-permute-start | bytes 737288 | tf_op jit(solution)/shard_map/ppermute | solution.py:619
  15.1 43.2 %all-to-all-start = ((bf16[4,2,256,768]{3,2,1,0:T(8,128)(2,1)}), bf16[4,2,256,768]{3,2,1,0:T(8,128)(2,1)}, u32[]{:S(2)}, u32[]{:S(2)}) async-start(bf16[4,2,256,768]{3,2,1,0:T(8,128)(2,1)} %pad_maximum_fusion), calls=%async_computation | async-start | bytes 6291456 | tf_op jit(solution)/shard_map/all_to_all | solution.py:688
  28.1 23.8 %collective-permute-start.6 = (bf16[4,96,1280]{2,1,0:T(8,128)(2,1)S(1)}, bf16[4,96,1280]{2,1,0:T(8,128)(2,1)}, u32[]{:S(2)}, u32[]{:S(2)}) collective-permute-start(bf16[4,96,1280]{2,1,0:T(8,128)(2,1)S(1)} %fusion), channel_id=1, source_target_pairs={{0,4},{1,5},{2,6},{3,7},{4,0},{5,1},{6,2},{7,3},{8,12},{9,13},{10,... | collective-permute-start | bytes 2949128 | tf_op jit(solution)/shard_map/ppermute | solution.py:619
  29.7 12.2 %collective-permute-start.3 = (bf16[48,1920]{1,0:T(8,128)(2,1)S(1)}, bf16[48,1920]{1,0:T(8,128)(2,1)S(1)}, u32[]{:S(2)}, u32[]{:S(2)}) collective-permute-start(bf16[48,1920]{1,0:T(8,128)(2,1)S(1)} %pad_maximum_fusion.5), channel_id=1, source_target_pairs={{0,8},{1,9},{2,10},{3,11},{4,12},{5,13},{6,14},{7,15},{8,16},{9,17... | collective-permute-start | bytes 552968 | tf_op jit(solution)/shard_map/ppermute | solution.py:619
  35.4 12.5 %collective-permute-start.4 = (bf16[48,1920]{1,0:T(8,128)(2,1)S(1)}, bf16[48,1920]{1,0:T(8,128)(2,1)S(1)}, u32[]{:S(2)}, u32[]{:S(2)}) collective-permute-start(bf16[48,1920]{1,0:T(8,128)(2,1)S(1)} %pad_maximum_fusion.5), channel_id=1, source_target_pairs={{0,16},{1,17},{2,18},{3,19},{4,20},{5,21},{6,22},{7,23},{8,24},{9,... | collective-permute-start | bytes 552968 | tf_op jit(solution)/shard_map/ppermute | solution.py:619
  37.0 11.0 %collective-permute-start.5 = (bf16[48,1920]{1,0:T(8,128)(2,1)S(1)}, bf16[48,1920]{1,0:T(8,128)(2,1)S(1)}, u32[]{:S(2)}, u32[]{:S(2)}) collective-permute-start(bf16[48,1920]{1,0:T(8,128)(2,1)S(1)} %pad_maximum_fusion.5), channel_id=1, source_target_pairs={{0,24},{1,25},{2,26},{3,27},{4,28},{5,29},{6,30},{7,31},{8,0},{9,1... | collective-permute-start | bytes 552968 | tf_op jit(solution)/shard_map/ppermute | solution.py:619
  53.3 29.8 %collective-permute-start.7 = (bf16[768,1280]{1,0:T(8,128)(2,1)S(1)}, bf16[768,1280]{1,0:T(8,128)(2,1)}, u32[]{:S(2)}, u32[]{:S(2)}) collective-permute-start(bf16[768,1280]{1,0:T(8,128)(2,1)S(1)} %bitcast_select_fusion.1.refs_1_.refs_2_.refs_6_), channel_id=1, source_target_pairs={{0,1},{1,0},{2,3},{3,2},{4,5},{5,4},{6,7},{7,6},{8,9},{9,8},{10,11... | collective-permute-start | bytes 5898248 | tf_op jit(solution)/shard_map/ppermute | solution.py:619
  59.9 60.6 %all-to-all-start.1 = ((bf16[4,2,192,768]{3,2,1,0:T(8,128)(2,1)}), bf16[4,2,192,768]{3,2,1,0:T(8,128)(2,1)}, u32[]{:S(2)}, u32[]{:S(2)}) async-start(bf16[4,2,192,768]{3,2,1,0:T(8,128)(2,1)} %broadcast_in_dim.141), calls=%async_computation.1 | async-start | bytes 4718592 | tf_op jit(solution)/shard_map/all_to_all | solution.py:644
  67.6 26.7 %collective-permute-start.8 = (bf16[4,48,1920]{2,1,0:T(8,128)(2,1)S(1)}, bf16[4,48,1920]{2,1,0:T(8,128)(2,1)S(1)}, u32[]{:S(2)}, u32[]{:S(2)}) collective-permute-start(bf16[4,48,1920]{2,1,0:T(8,128)(2,1)S(1)} %fusion.3), channel_id=1, source_target_pairs={{0,4},{1,5},{2,6},{3,7},{4,0},{5,1},{6,2},{7,3},{8,12},{9,13},{10,... | collective-permute-start | bytes 2211848 | tf_op jit(solution)/shard_map/ppermute | solution.py:619
  69.1 25.2 %collective-permute-start.9 = (bf16[4,48,1920]{2,1,0:T(8,128)(2,1)S(1)}, bf16[4,48,1920]{2,1,0:T(8,128)(2,1)S(1)}, u32[]{:S(2)}, u32[]{:S(2)}) collective-permute-start(bf16[4,48,1920]{2,1,0:T(8,128)(2,1)S(1)} %fusion.3), channel_id=1, source_target_pairs={{0,2},{1,3},{2,0},{3,1},{4,6},{5,7},{6,4},{7,5},{8,10},{9,11},{10,... | collective-permute-start | bytes 2211848 | tf_op jit(solution)/shard_map/ppermute | solution.py:619
  95.2 16.7 %collective-permute-start.10 = (bf16[4,48,1920]{2,1,0:T(8,128)(2,1)S(1)}, bf16[4,48,1920]{2,1,0:T(8,128)(2,1)S(1)}, u32[]{:S(2)}, u32[]{:S(2)}) collective-permute-start(bf16[4,48,1920]{2,1,0:T(8,128)(2,1)S(1)} %collective-permute-done.8), channel_id=1, source_target_pairs={{0,2},{1,3},{2,0},{3,1},{4,6},{5,7},{6,4},{7,5},{8,10},{9,11},{10,... | collective-permute-start | bytes 2211848 | tf_op jit(solution)/shard_map/ppermute | solution.py:619
  151.1 25.9 %collective-permute-start.14 = (bf16[768,1536]{1,0:T(8,128)(2,1)}, bf16[768,1536]{1,0:T(8,128)(2,1)}, u32[]{:S(2)}, u32[]{:S(2)}) collective-permute-start(bf16[768,1536]{1,0:T(8,128)(2,1)} %get-tuple-element.123), channel_id=1, source_target_pairs={{0,1},{1,0},{2,3},{3,2},{4,5},{5,4},{6,7},{7,6},{8,9},{9,8},{10,11... | collective-permute-start | bytes 7077896 | tf_op jit(solution)/shard_map/ppermute | solution.py:619
  151.6 25.4 %collective-permute-start.15 = (bf16[768,1536]{1,0:T(8,128)(2,1)}, bf16[768,1536]{1,0:T(8,128)(2,1)S(1)}, u32[]{:S(2)}, u32[]{:S(2)}) collective-permute-start(bf16[768,1536]{1,0:T(8,128)(2,1)} %get-tuple-element.124), channel_id=1, source_target_pairs={{0,1},{1,0},{2,3},{3,2},{4,5},{5,4},{6,7},{7,6},{8,9},{9,8},{10,11... | collective-permute-start | bytes 7077896 | tf_op jit(solution)/shard_map/ppermute | solution.py:619
  184.9 36.3 %collective-permute-start.17 = (bf16[4,2,48,1536]{3,2,0,1:T(8,128)(2,1)S(1)}, bf16[4,2,48,1536]{3,2,0,1:T(8,128)(2,1)S(1)}, u32[]{:S(2)}, u32[]{:S(2)}) collective-permute-start(bf16[4,2,48,1536]{3,2,0,1:T(8,128)(2,1)S(1)} %get-tuple-element.185), channel_id=1, source_target_pairs={{0,2},{1,3},{2,0},{3,1},{4,6},{5,7},{6,4},{7,5},{8,10},{9,11},{10,... | collective-permute-start | bytes 3538952 | tf_op jit(solution)/shard_map/ppermute | solution.py:619
  186.4 34.8 %collective-permute-start.16 = (bf16[4,2,48,1536]{3,2,1,0:T(8,128)(2,1)}, bf16[4,2,48,1536]{3,2,1,0:T(8,128)(2,1)S(1)}, u32[]{:S(2)}, u32[]{:S(2)}) collective-permute-start(bf16[4,2,48,1536]{3,2,1,0:T(8,128)(2,1)} %fusion.7), channel_id=1, source_target_pairs={{0,4},{1,5},{2,6},{3,7},{4,0},{5,1},{6,2},{7,3},{8,12},{9,13},{10,... | collective-permute-start | bytes 3538952 | tf_op jit(solution)/shard_map/ppermute | solution.py:619
  198.3 22.9 %collective-permute-start.18 = (bf16[768,384]{1,0:T(8,128)(2,1)}, bf16[768,384]{1,0:T(8,128)(2,1)}, u32[]{:S(2)}, u32[]{:S(2)}) collective-permute-start(bf16[768,384]{1,0:T(8,128)(2,1)} %get-tuple-element.131), channel_id=1, source_target_pairs={{0,1},{1,0},{2,3},{3,2},{4,5},{5,4},{6,7},{7,6},{8,9},{9,8},{10,11... | collective-permute-start | bytes 1769480 | tf_op jit(solution)/shard_map/ppermute | solution.py:619
  223.5 37.5 %all-to-all-start.2 = ((bf16[4,256,768]{2,1,0:T(8,128)(2,1)}), bf16[4,256,768]{2,1,0:T(8,128)(2,1)}, u32[]{:S(2)}, u32[]{:S(2)}) async-start(bf16[4,256,768]{2,1,0:T(8,128)(2,1)} %bitcast.166), calls=%async_computation.2 | async-start | bytes 3145728 | tf_op jit(solution)/shard_map/all_to_all | solution.py:688
  228.6 32.4 %collective-permute-start.20 = (bf16[4,48,1536]{2,1,0:T(8,128)(2,1)}, bf16[4,48,1536]{2,1,0:T(8,128)(2,1)}, u32[]{:S(2)}, u32[]{:S(2)}) collective-permute-start(bf16[4,48,1536]{2,1,0:T(8,128)(2,1)} %select_bitcast_fusion.2), channel_id=1, source_target_pairs={{0,4},{1,5},{2,6},{3,7},{4,0},{5,1},{6,2},{7,3},{8,12},{9,13},{10,... | collective-permute-start | bytes 1769480 | tf_op jit(solution)/shard_map/ppermute | solution.py:619
  229.1 31.9 %collective-permute-start.19 = (bf16[4,48,1536]{2,1,0:T(8,128)(2,1)}, bf16[4,48,1536]{2,1,0:T(8,128)(2,1)}, u32[]{:S(2)}, u32[]{:S(2)}) collective-permute-start(bf16[4,48,1536]{2,1,0:T(8,128)(2,1)} %fusion.10), channel_id=1, source_target_pairs={{0,2},{1,3},{2,0},{3,1},{4,6},{5,7},{6,4},{7,5},{8,10},{9,11},{10,... | collective-permute-start | bytes 1769480 | tf_op jit(solution)/shard_map/ppermute | solution.py:619
  259.0 17.7 %collective-permute-start.24 = (bf16[384,896]{1,0:T(8,128)(2,1)}, bf16[384,896]{1,0:T(8,128)(2,1)}, u32[]{:S(2)}, u32[]{:S(2)}) collective-permute-start(bf16[384,896]{1,0:T(8,128)(2,1)} %get-tuple-element.151), channel_id=1, source_target_pairs={{0,4},{1,5},{2,6},{3,7},{4,0},{5,1},{6,2},{7,3},{8,12},{9,13},{10,... | collective-permute-start | bytes 2064392 | tf_op jit(solution)/shard_map/ppermute | solution.py:619
  260.6 15.1 %collective-permute-start.23 = (bf16[384,768]{1,0:T(8,128)(2,1)}, bf16[384,768]{1,0:T(8,128)(2,1)}, u32[]{:S(2)}, u32[]{:S(2)}) collective-permute-start(bf16[384,768]{1,0:T(8,128)(2,1)} %get-tuple-element.150), channel_id=1, source_target_pairs={{0,2},{1,3},{2,0},{3,1},{4,6},{5,7},{6,4},{7,5},{8,10},{9,11},{10,... | collective-permute-start | bytes 1769480 | tf_op jit(solution)/shard_map/ppermute | solution.py:619
  264.2 17.5 %collective-permute-start.29 = (bf16[48,3072]{1,0:T(8,128)(2,1)S(1)}, bf16[48,3072]{1,0:T(8,128)(2,1)S(1)}, u32[]{:S(2)}, u32[]{:S(2)}) collective-permute-start(bf16[48,3072]{1,0:T(8,128)(2,1)S(1)} %pad_maximum_fusion.4), channel_id=1, source_target_pairs={{0,24},{1,25},{2,26},{3,27},{4,28},{5,29},{6,30},{7,31},{8,0},{9,1... | collective-permute-start | bytes 884744 | tf_op jit(solution)/shard_map/ppermute | solution.py:619
  267.5 25.2 %collective-permute-start.28 = (bf16[48,3072]{1,0:T(8,128)(2,1)S(1)}, bf16[48,3072]{1,0:T(8,128)(2,1)S(1)}, u32[]{:S(2)}, u32[]{:S(2)}) collective-permute-start(bf16[48,3072]{1,0:T(8,128)(2,1)S(1)} %pad_maximum_fusion.3), channel_id=1, source_target_pairs={{0,16},{1,17},{2,18},{3,19},{4,20},{5,21},{6,22},{7,23},{8,24},{9,... | collective-permute-start | bytes 884744 | tf_op jit(solution)/shard_map/ppermute | solution.py:619
  267.6 25.1 %collective-permute-start.27 = (bf16[48,3072]{1,0:T(8,128)(2,1)S(1)}, bf16[48,3072]{1,0:T(8,128)(2,1)S(1)}, u32[]{:S(2)}, u32[]{:S(2)}) collective-permute-start(bf16[48,3072]{1,0:T(8,128)(2,1)S(1)} %pad_maximum_fusion.2), channel_id=1, source_target_pairs={{0,8},{1,9},{2,10},{3,11},{4,12},{5,13},{6,14},{7,15},{8,16},{9,17... | collective-permute-start | bytes 884744 | tf_op jit(solution)/shard_map/ppermute | solution.py:619
  277.9 15.0 %collective-permute-start.26 = (bf16[4,48,896]{2,1,0:T(8,128)(2,1)S(1)}, bf16[4,48,896]{2,1,0:T(8,128)(2,1)S(1)}, u32[]{:S(2)}, u32[]{:S(2)}) collective-permute-start(bf16[4,48,896]{2,1,0:T(8,128)(2,1)S(1)} %select_bitcast_fusion.3), channel_id=1, source_target_pairs={{0,2},{1,3},{2,0},{3,1},{4,6},{5,7},{6,4},{7,5},{8,10},{9,11},{10,... | collective-permute-start | bytes 1032200 | tf_op jit(solution)/shard_map/ppermute | solution.py:619
  281.1 11.8 %collective-permute-start.25 = (bf16[4,48,768]{2,1,0:T(8,128)(2,1)S(1)}, bf16[4,48,768]{2,1,0:T(8,128)(2,1)S(1)}, u32[]{:S(2)}, u32[]{:S(2)}) collective-permute-start(bf16[4,48,768]{2,1,0:T(8,128)(2,1)S(1)} %select_bitcast_fusion.4), channel_id=1, source_target_pairs={{0,4},{1,5},{2,6},{3,7},{4,0},{5,1},{6,2},{7,3},{8,12},{9,13},{10,... | collective-permute-start | bytes 884744 | tf_op jit(solution)/shard_map/ppermute | solution.py:619
  297.9 24.4 %all-to-all-start.3 = ((bf16[4,256,768]{2,1,0:T(8,128)(2,1)}), bf16[4,256,768]{2,1,0:T(8,128)(2,1)S(1)}, u32[]{:S(2)}, u32[]{:S(2)}) async-start(bf16[4,256,768]{2,1,0:T(8,128)(2,1)} %bitcast.167), calls=%async_computation.3 | async-start | bytes 3145728 | tf_op jit(solution)/shard_map/all_to_all | solution.py:688
  301.5 18.4 %collective-permute-start.31 = (bf16[48,1664]{1,0:T(8,128)(2,1)}, bf16[48,1664]{1,0:T(8,128)(2,1)S(1)}, u32[]{:S(2)}, u32[]{:S(2)}) collective-permute-start(bf16[48,1664]{1,0:T(8,128)(2,1)} %pad_maximum_fusion.7), channel_id=1, source_target_pairs={{0,16},{1,17},{2,18},{3,19},{4,20},{5,21},{6,22},{7,23},{8,24},{9,... | collective-permute-start | bytes 479240 | tf_op jit(solution)/shard_map/ppermute | solution.py:619
  304.9 15.1 %collective-permute-start.30 = (bf16[48,1664]{1,0:T(8,128)(2,1)}, bf16[48,1664]{1,0:T(8,128)(2,1)}, u32[]{:S(2)}, u32[]{:S(2)}) collective-permute-start(bf16[48,1664]{1,0:T(8,128)(2,1)} %pad_maximum_fusion.6), channel_id=1, source_target_pairs={{0,8},{1,9},{2,10},{3,11},{4,12},{5,13},{6,14},{7,15},{8,16},{9,17... | collective-permute-start | bytes 479240 | tf_op jit(solution)/shard_map/ppermute | solution.py:619
  306.9 18.6 %collective-permute-start.37 = (bf16[2,48,3072]{2,1,0:T(8,128)(2,1)S(1)}, bf16[2,48,3072]{2,1,0:T(8,128)(2,1)S(1)}, u32[]{:S(2)}, u32[]{:S(2)}) collective-permute-start(bf16[2,48,3072]{2,1,0:T(8,128)(2,1)S(1)} %broadcast_select_fusion.3), channel_id=1, source_target_pairs={{0,1},{1,0},{2,3},{3,2},{4,5},{5,4},{6,7},{7,6},{8,9},{9,8},{10,11... | collective-permute-start | bytes 1769480 | tf_op jit(solution)/shard_map/ppermute | solution.py:619
  (42 other events, 244.9 us)

commit v4 on v3

--- a/solution.py
+++ b/solution.py
@@ -297,31 +297,37 @@
     allowed = upper()
     scaling = jnp.asarray(HEAD_DIM**-0.5, BF16)
     head_keys = [keep_head(low_all, head, k_ref[...]) for head in range(2)]
-    for block in reversed(range(seq // BLOCK)):
+    tiles = [(block, head) for block in reversed(range(seq // BLOCK)) for head in range(2)]
+
+    def scored(block, head):
         start, end = block * BLOCK, (block + 1) * BLOCK
-        queries = q_ref[start:end, :] * scaling
-        grads = do_ref[start:end, :]
-        dots = (grads.astype(F32) * o_ref[start:end, :].astype(F32)).T
-        add_q = add_k = add_v = None
-        for head in range(2):
-            q_head = keep_head(low_lanes, head, queries)
-            g_head = keep_head(low_lanes, head, grads)
-            centre = jnp.sum(dots[HEAD_DIM * head : HEAD_DIM * (head + 1)], axis=0, keepdims=True)
-            scores = dot_nt(k_ref[:end, :], q_head)
-            probs = jnp.exp(scores - l_ref[0, head : head + 1, start:end])
-            last = jnp.where(allowed, probs[start:, :], 0.0)
-            probs = jnp.concatenate([probs[:start, :], last], axis=0) if block else last
-            grad_probs = dot_nt(v_ref[:end, :], g_head)
-            grad_scores = (probs * (grad_probs - centre)).astype(BF16)
-            terms = (
-                dot_tn(grad_scores, head_keys[head][:end]),
-                dot_nn(grad_scores, q_head),
-                dot_nn(probs.astype(BF16), g_head),
-            )
-            if head == 0:
-                add_q, add_k, add_v = terms
-            else:
-                add_q, add_k, add_v = add_q + terms[0], add_k + terms[1], add_v + terms[2]
+        q_head = keep_head(low_lanes, head, q_ref[start:end, :] * scaling)
+        g_head = keep_head(low_lanes, head, do_ref[start:end, :])
+        return q_head, g_head, dot_nt(k_ref[:end, :], q_head), dot_nt(v_ref[:end, :], g_head)
+
+    ahead = 2
+    waiting = [scored(*tile) for tile in tiles[:ahead]]
+    for number, (block, head) in enumerate(tiles):
+        start, end = block * BLOCK, (block + 1) * BLOCK
+        if number + ahead < len(tiles):
+            waiting.append(scored(*tiles[number + ahead]))
+        q_head, g_head, scores, grad_probs = waiting.pop(0)
+        if head == 0:
+            dots = (do_ref[start:end, :].astype(F32) * o_ref[start:end, :].astype(F32)).T
+        centre = jnp.sum(dots[HEAD_DIM * head : HEAD_DIM * (head + 1)], axis=0, keepdims=True)
+        probs = jnp.exp(scores - l_ref[0, head : head + 1, start:end])
+        last = jnp.where(allowed, probs[start:, :], 0.0)
+        probs = jnp.concatenate([probs[:start, :], last], axis=0) if block else last
+        grad_scores = (probs * (grad_probs - centre)).astype(BF16)
+        terms = (
+            dot_tn(grad_scores, head_keys[head][:end]),
+            dot_nn(grad_scores, q_head),
+            dot_nn(probs.astype(BF16), g_head),
+        )
+        if head == 0:
+            add_q, add_k, add_v = terms
+            continue
+        add_q, add_k, add_v = add_q + terms[0], add_k + terms[1], add_v + terms[2]
         dq_ref[start:end, :] = (add_q * HEAD_DIM**-0.5).astype(BF16)
         if end == seq:
             sum_k[...] = add_k

time: 342 us -> 339 us (level)
  transfers between devices with their start and end apart: 42 -> 42, of which waited for: 13 -> 14; matrix products, arithmetic and copies ran while one was open for 9% -> 9% of each run, Pallas kernels for 36% -> 35%
where the time goes in v4:
time: 339 us; the launch traced here: 333 us
  Pallas kernels  144 us (42%)
  waiting for transfers between devices  71.7 us (21%)
  starting transfers between devices  65 us (19%)
  other arithmetic  32.8 us (10%)
  local copies, waits for them, and re-layouts  18.1 us (5%)
    ppermute x38, waiting for transfers between devices, send(): return lax.ppermute(value, BOTH, pairs)  63.5 us
    pallas_call x2, Pallas kernels, attend_back(): pl.pallas_call(functools.partial(attend_back_kernel, carry is not None, b...  47.2 us
    pallas_call x2, Pallas kernels, feed_forward(): pl.pallas_call(functools.partial(ffn_kernel, int(final), paired), grid=(2...  46 us
    ppermute x38, starting transfers between devices, send(): return lax.ppermute(value, BOTH, pairs)  44.9 us
    pallas_call x2, Pallas kernels, attend(): pl.pallas_call(functools.partial(attend_kernel, first), grid=(pairs,), in...  23.6 us
    all_to_all x3, starting transfers between devices, exchange(): lax.all_to_all(value, 'head', split_axis=0, concat_axis=0, tiled=True)  12.8 us
    pallas_call x1, Pallas kernels, middle_back(): pl.pallas_call(middle_kernel, grid_spec=pltpu.PrefetchScalarGridSpec(num_...  10.3 us
    select_n x7, other arithmetic, halves(): return (jnp.where(index == 0, high, low), jnp.where(index == 0, low, high))  8.47 us
  transfers between devices with their start and end apart: 42, of which 14 were waited for; matrix products, arithmetic and copies ran while one was open for 9% of the time, Pallas kernels for 35%

profile of v4, /device:TPU:0, one launch (start us, length us, event | category | flops | bytes accessed | tf_op | source)
XLA Modules:
  0.0 333.3 jit_solution(3211788162909383980)
XLA Ops:
  4.7 3.1 collective-permute-start
  7.8 2.6 collective-permute-start.1
  11.7 3.4 %pad_maximum_fusion = bf16[4,2,256,768]{3,2,1,0:T(8,128)(2,1)} fusion(bf16[4,1,256,768]{3,2,1,0:T(8,128)(2,1)S(1)} %bitcast.168, bf16[4,1,256,768]{3,2,1,0:T(8,128)(2,1)} %bitcast.169), kind=kLoop, calls=%fused_computation.3 | loop fusion | flops 1572864 | bytes 6291456 | tf_op jit(solution)/shard_map/stack | solution.py:745
  15.1 4.7 %all-to-all-start = ((bf16[4,2,256,768]{3,2,1,0:T(8,128)(2,1)}), bf16[4,2,256,768]{3,2,1,0:T(8,128)(2,1)}, u32[]{:S(2)}, u32[]{:S(2)}) async-start(bf16[4,2,256,768]{3,2,1,0:T(8,128)(2,1)} %pad_maximum_fusion), calls=%async_computation | async-start | bytes 6291456 | tf_op jit(solution)/shard_map/all_to_all | solution.py:694
  24.0 2.5 collective-permute-done.1
  29.7 5.7 %collective-permute-start.3 = (bf16[48,1920]{1,0:T(8,128)(2,1)S(1)}, bf16[48,1920]{1,0:T(8,128)(2,1)S(1)}, u32[]{:S(2)}, u32[]{:S(2)}) collective-permute-start(bf16[48,1920]{1,0:T(8,128)(2,1)S(1)} %pad_maximum_fusion.5), channel_id=1, source_target_pairs={{0,8},{1,9},{2,10},{3,11},{4,12},{5,13},{6,14},{7,15},{8,16},{9,17... | collective-permute-start | bytes 552968 | tf_op jit(solution)/shard_map/ppermute | solution.py:625
  37.8 4.1 %collective-permute-done.3 = bf16[48,1920]{1,0:T(8,128)(2,1)S(1)} collective-permute-done((bf16[48,1920]{1,0:T(8,128)(2,1)S(1)}, bf16[48,1920]{1,0:T(8,128)(2,1)S(1)}, u32[]{:S(2)}, u32[]{:S(2)}) %collective-permute-start.3) | collective-permute-done | bytes 184352 | tf_op jit(solution)/shard_map/ppermute | solution.py:625
  41.9 6.0 %collective-permute-done.4 = bf16[48,1920]{1,0:T(8,128)(2,1)S(1)} collective-permute-done((bf16[48,1920]{1,0:T(8,128)(2,1)S(1)}, bf16[48,1920]{1,0:T(8,128)(2,1)S(1)}, u32[]{:S(2)}, u32[]{:S(2)}) %collective-permute-start.4) | collective-permute-done | bytes 184352 | tf_op jit(solution)/shard_map/ppermute | solution.py:625
  53.4 4.8 %collective-permute-done.12 = bf16[192,768]{1,0:T(8,128)(2,1)S(1)} collective-permute-done((bf16[192,768]{1,0:T(8,128)(2,1)S(1)}, bf16[192,768]{1,0:T(8,128)(2,1)S(1)}, u32[]{:S(2)}, u32[]{:S(2)}) %collective-permute-start.12) | collective-permute-done | bytes 294944 | tf_op jit(solution)/shard_map/ppermute | solution.py:625
  59.9 7.4 %all-to-all-start.1 = ((bf16[4,2,192,768]{3,2,1,0:T(8,128)(2,1)}), bf16[4,2,192,768]{3,2,1,0:T(8,128)(2,1)}, u32[]{:S(2)}, u32[]{:S(2)}) async-start(bf16[4,2,192,768]{3,2,1,0:T(8,128)(2,1)} %broadcast_in_dim.141), calls=%async_computation.1 | async-start | bytes 4718592 | tf_op jit(solution)/shard_map/all_to_all | solution.py:650
  70.6 12.4 %shard_map.177 = (bf16[1024,768]{1,0:T(8,128)(2,1)}, bf16[1024,1152]{1,0:T(8,128)(2,1)}, bf16[1024,384]{1,0:T(8,128)(2,1)}, f32[3,2,1024]{2,1,0:T(2,128)}, f32[8,768]{1,0:T(8,128)}) custom-call(bf16[4,2,256,768]{3,2,1,0:T(8,128)(2,1)} %all-to-all-done.refs_0_.x_ref.refs_1_.cot_ref.refs_8_, bf16[768,1280]{1,0:T(8,128)(2,1)} %copy-done.3, ...), custom_call_target="tpu_custom_call" | custom-call | flops 11000000 | bytes 30000 | tf_op jit(solution)/shard_map/pallas_call | solution.py:256
  83.1 11.2 %shard_map.178 = (bf16[1024,1152]{1,0:T(8,128)(2,1)}, bf16[1024,384]{1,0:T(8,128)(2,1)}, f32[3,2,1024]{2,1,0:T(2,128)}) custom-call(bf16[1024,768]{1,0:T(8,128)(2,1)} %get-tuple-element.109.refs_0_.refs_4_.refs_5_, bf16[768,1280]{1,0:T(8,128)(2,1)} %collective-permute-done.7.refs_1_.refs_5_), custom_call_target="tpu_custom_call" | custom-call | flops 11000000 | bytes 30000 | tf_op jit(solution)/shard_map/pallas_call | solution.py:256
  95.9 16.0 %collective-permute-done.10 = bf16[4,48,1920]{2,1,0:T(8,128)(2,1)S(1)} collective-permute-done((bf16[4,48,1920]{2,1,0:T(8,128)(2,1)S(1)}, bf16[4,48,1920]{2,1,0:T(8,128)(2,1)S(1)}, u32[]{:S(2)}, u32[]{:S(2)}) %collective-permute-start.10) | collective-permute-done | bytes 737312 | tf_op jit(solution)/shard_map/ppermute | solution.py:625
  113.9 6.6 %all-to-all-done.1 = bf16[4,2,192,768]{3,2,1,0:T(8,128)(2,1)} async-done(((bf16[4,2,192,768]{3,2,1,0:T(8,128)(2,1)}), bf16[4,2,192,768]{3,2,1,0:T(8,128)(2,1)}, u32[]{:S(2)}, u32[]{:S(2)}) %all-to-all-start.1) | async-done | bytes 2359328 | tf_op jit(solution)/shard_map/all_to_all | solution.py:650
  120.5 6.6 %shard_map.179 = (bf16[1024,768]{1,0:T(8,128)(2,1)}, bf16[1024,768]{1,0:T(8,128)(2,1)}) custom-call(s32[1]{0:T(128)} %bitcast.core_ref, bf16[4,2,256,768]{3,2,1,0:T(8,128)(2,1)} %all-to-all-done.refs_0_.x_ref.refs_1_.cot_ref.refs_8_, bf16[1024,384]{1,0:T(8,128)(2,1)} %get-tuple-element.108.am_ref.refs_3_, ...), custom_call_target="tpu_custom_call" | custom-call | flops 11000000 | bytes 30000 | tf_op jit(solution)/shard_map/pallas_call | solution.py:105
  128.4 22.7 %shard_map.180 = (f32[1024,768]{1,0:T(8,128)}, bf16[1024,768]{1,0:T(8,128)(2,1)}, bf16[768,1536]{1,0:T(8,128)(2,1)}, bf16[768,1536]{1,0:T(8,128)(2,1)}) custom-call(bf16[1024,768]{1,0:T(8,128)(2,1)} %get-tuple-element.114.refs_0_, bf16[4,2,256,768]{3,2,1,0:T(8,128)(2,1)} %all-to-all-done.refs_0_.x_ref.refs_1_.cot_ref.refs_8_, ...), custom_call_target="tpu_custom_call" | custom-call | flops 11000000 | bytes 30000 | tf_op jit(solution)/shard_map/pallas_call | solution.py:511
  151.7 23.3 %shard_map.181 = (bf16[1024,768]{1,0:T(8,128)(2,1)}, bf16[1024,768]{1,0:T(8,128)(2,1)}, bf16[768,1536]{1,0:T(8,128)(2,1)}, bf16[768,1536]{1,0:T(8,128)(2,1)}) custom-call(bf16[1024,768]{1,0:T(8,128)(2,1)} %get-tuple-element.114.refs_0_, bf16[4,2,256,768]{3,2,1,0:T(8,128)(2,1)} %all-to-all-done.refs_0_.x_ref.refs_1_.cot_ref.refs_8_, ...), custom_call_target="tpu_custom_call" | custom-call | flops 11000000 | bytes 30000 | tf_op jit(solution)/shard_map/pallas_call | solution.py:511
  175.0 2.0 fusion.32
  187.9 10.3 %shard_map.182 = (bf16[1024,768]{1,0:T(8,128)(2,1)}, bf16[1024,384]{1,0:T(8,128)(2,1)}, bf16[1024,384]{1,0:T(8,128)(2,1)}, bf16[768,384]{1,0:T(8,128)(2,1)}, bf16[768,384]{1,0:T(8,128)(2,1)}, /*index=5*/f32[8,768]{1,0:T(8,128)}) custom-call(s32[1]{0:T(128)} %bitcast.core_ref, bf16[1024,768]{1,0:T(8,128)(2,1)} %get-tuple-element.119.refs_4_.mid_ref, ...), custom_call_target="tpu_custom_call" | custom-call | flops 11000000 | bytes 30000 | tf_op jit(solution)/shard_map/pallas_call | solution.py:162
  198.4 21.0 %shard_map.183 = (bf16[768,768]{1,0:T(8,128)(2,1)}, bf16[768,512]{1,0:T(8,128)(2,1)}, bf16[1024,768]{1,0:T(8,128)(2,1)}) custom-call(bf16[1024,1152]{1,0:T(8,128)(2,1)} %get-tuple-element.132.refs_0_, bf16[1024,384]{1,0:T(8,128)(2,1)} %get-tuple-element.133.refs_1_, bf16[1024,384]{1,0:T(8,128)(2,1)} %get-tuple-element.110.at_ref.refs_2_, ...), custom_call_target="tpu_custom_call" | custom-call | flops 11000000 | bytes 30000 | tf_op jit(solution)/shard_map/pallas_call | solution.py:419
  222.2 4.5 %all-to-all-start.2 = ((bf16[4,256,768]{2,1,0:T(8,128)(2,1)}), bf16[4,256,768]{2,1,0:T(8,128)(2,1)}, u32[]{:S(2)}, u32[]{:S(2)}) async-start(bf16[4,256,768]{2,1,0:T(8,128)(2,1)} %bitcast.166), calls=%async_computation.2 | async-start | bytes 3145728 | tf_op jit(solution)/shard_map/all_to_all | solution.py:694
  230.0 26.2 %shard_map.184 = (bf16[384,768]{1,0:T(8,128)(2,1)}, bf16[384,768]{1,0:T(8,128)(2,1)}, bf16[384,896]{1,0:T(8,128)(2,1)}, bf16[384,896]{1,0:T(8,128)(2,1)}, bf16[1024,768]{1,0:T(8,128)(2,1)}, /*index=5*/f32[8,768]{1,0:T(8,128)}) custom-call(s32[2]{0:T(128)} %pad_add_fusion.refs_0_, bf16[1024,1152]{1,0:T(8,128)(2,1)} %get-tuple-element.140.refs_1_, ...), custom_call_target="tpu_custom_call" | custom-call | flops 11000000 | bytes 30000 | tf_op jit(solution)/shard_map/pallas_call | solution.py:419
  262.6 3.3 collective-permute-start.29
  266.6 3.8 %shard_map.185 = bf16[4,256,768]{2,1,0:T(8,128)(2,1)} custom-call(bf16[4,256,768]{2,1,0:T(8,128)(2,1)} %all-to-all-done.2.in_ref), custom_call_target="tpu_custom_call" | custom-call | flops 11000000 | bytes 30000 | tf_op jit(solution)/shard_map/pallas_call | solution.py:587
  270.4 2.5 collective-permute-done.23
  278.9 11.1 %collective-permute-done.28 = bf16[48,3072]{1,0:T(8,128)(2,1)S(1)} collective-permute-done((bf16[48,3072]{1,0:T(8,128)(2,1)S(1)}, bf16[48,3072]{1,0:T(8,128)(2,1)S(1)}, u32[]{:S(2)}, u32[]{:S(2)}) %collective-permute-start.28) | collective-permute-done | bytes 294944 | tf_op jit(solution)/shard_map/ppermute | solution.py:625
  295.5 3.6 %all-to-all-start.3 = ((bf16[4,256,768]{2,1,0:T(8,128)(2,1)}), bf16[4,256,768]{2,1,0:T(8,128)(2,1)S(1)}, u32[]{:S(2)}, u32[]{:S(2)}) async-start(bf16[4,256,768]{2,1,0:T(8,128)(2,1)} %bitcast.167), calls=%async_computation.3 | async-start | bytes 3145728 | tf_op jit(solution)/shard_map/all_to_all | solution.py:694
  299.1 3.6 %collective-permute-start.31 = (bf16[48,1664]{1,0:T(8,128)(2,1)}, bf16[48,1664]{1,0:T(8,128)(2,1)S(1)}, u32[]{:S(2)}, u32[]{:S(2)}) collective-permute-start(bf16[48,1664]{1,0:T(8,128)(2,1)} %pad_maximum_fusion.7), channel_id=1, source_target_pairs={{0,16},{1,17},{2,18},{3,19},{4,20},{5,21},{6,22},{7,23},{8,24},{9,... | collective-permute-start | bytes 479240 | tf_op jit(solution)/shard_map/ppermute | solution.py:625
  302.7 1.9 collective-permute-start.30
  305.8 12.0 %collective-permute-done.31 = bf16[48,1664]{1,0:T(8,128)(2,1)S(1)} collective-permute-done((bf16[48,1664]{1,0:T(8,128)(2,1)}, bf16[48,1664]{1,0:T(8,128)(2,1)S(1)}, u32[]{:S(2)}, u32[]{:S(2)}) %collective-permute-start.31) | collective-permute-done | bytes 159776 | tf_op jit(solution)/shard_map/ppermute | solution.py:625
  325.7 3.6 %shard_map.186 = (f32[96,3072]{1,0:T(8,128)}, f32[384,768]{1,0:T(8,128)}) custom-call(s32[2]{0:T(128)} %pad_add_fusion.1.where_ref, bf16[2,2,48,3072]{3,2,1,0:T(8,128)(2,1)} %broadcast_select_fusion.2.all_ref), custom_call_target="tpu_custom_call" | custom-call | flops 11000000 | bytes 30000 | tf_op jit(solution)/shard_map/pallas_call | solution.py:598
  330.1 3.0 shard_map.187
  (194 shorter events, 76.2 us)
Async XLA Ops:
  4.7 19.3 %collective-permute-start = (bf16[96,1280]{1,0:T(8,128)(2,1)S(1)}, bf16[96,1280]{1,0:T(8,128)(2,1)}, u32[]{:S(2)}, u32[]{:S(2)}) collective-permute-start(bf16[96,1280]{1,0:T(8,128)(2,1)S(1)} %fusion.14), channel_id=1, source_target_pairs={{0,8},{1,9},{2,10},{3,11},{4,12},{5,13},{6,14},{7,15},{8,16},{9,17... | collective-permute-start | bytes 737288 | tf_op jit(solution)/shard_map/ppermute | solution.py:625
  7.8 18.8 %collective-permute-start.1 = (bf16[96,1280]{1,0:T(8,128)(2,1)S(1)}, bf16[96,1280]{1,0:T(8,128)(2,1)}, u32[]{:S(2)}, u32[]{:S(2)}) collective-permute-start(bf16[96,1280]{1,0:T(8,128)(2,1)S(1)} %fusion.14), channel_id=1, source_target_pairs={{0,16},{1,17},{2,18},{3,19},{4,20},{5,21},{6,22},{7,23},{8,24},{9,... | collective-permute-start | bytes 737288 | tf_op jit(solution)/shard_map/ppermute | solution.py:625
  10.4 16.2 %collective-permute-start.2 = (bf16[96,1280]{1,0:T(8,128)(2,1)S(1)}, bf16[96,1280]{1,0:T(8,128)(2,1)}, u32[]{:S(2)}, u32[]{:S(2)}) collective-permute-start(bf16[96,1280]{1,0:T(8,128)(2,1)S(1)} %fusion.14), channel_id=1, source_target_pairs={{0,24},{1,25},{2,26},{3,27},{4,28},{5,29},{6,30},{7,31},{8,0},{9,1... | collective-permute-start | bytes 737288 | tf_op jit(solution)/shard_map/ppermute | solution.py:625
  15.1 43.2 %all-to-all-start = ((bf16[4,2,256,768]{3,2,1,0:T(8,128)(2,1)}), bf16[4,2,256,768]{3,2,1,0:T(8,128)(2,1)}, u32[]{:S(2)}, u32[]{:S(2)}) async-start(bf16[4,2,256,768]{3,2,1,0:T(8,128)(2,1)} %pad_maximum_fusion), calls=%async_computation | async-start | bytes 6291456 | tf_op jit(solution)/shard_map/all_to_all | solution.py:694
  28.1 23.8 %collective-permute-start.6 = (bf16[4,96,1280]{2,1,0:T(8,128)(2,1)S(1)}, bf16[4,96,1280]{2,1,0:T(8,128)(2,1)}, u32[]{:S(2)}, u32[]{:S(2)}) collective-permute-start(bf16[4,96,1280]{2,1,0:T(8,128)(2,1)S(1)} %fusion), channel_id=1, source_target_pairs={{0,4},{1,5},{2,6},{3,7},{4,0},{5,1},{6,2},{7,3},{8,12},{9,13},{10,... | collective-permute-start | bytes 2949128 | tf_op jit(solution)/shard_map/ppermute | solution.py:625
  29.7 12.2 %collective-permute-start.3 = (bf16[48,1920]{1,0:T(8,128)(2,1)S(1)}, bf16[48,1920]{1,0:T(8,128)(2,1)S(1)}, u32[]{:S(2)}, u32[]{:S(2)}) collective-permute-start(bf16[48,1920]{1,0:T(8,128)(2,1)S(1)} %pad_maximum_fusion.5), channel_id=1, source_target_pairs={{0,8},{1,9},{2,10},{3,11},{4,12},{5,13},{6,14},{7,15},{8,16},{9,17... | collective-permute-start | bytes 552968 | tf_op jit(solution)/shard_map/ppermute | solution.py:625
  35.4 12.5 %collective-permute-start.4 = (bf16[48,1920]{1,0:T(8,128)(2,1)S(1)}, bf16[48,1920]{1,0:T(8,128)(2,1)S(1)}, u32[]{:S(2)}, u32[]{:S(2)}) collective-permute-start(bf16[48,1920]{1,0:T(8,128)(2,1)S(1)} %pad_maximum_fusion.5), channel_id=1, source_target_pairs={{0,16},{1,17},{2,18},{3,19},{4,20},{5,21},{6,22},{7,23},{8,24},{9,... | collective-permute-start | bytes 552968 | tf_op jit(solution)/shard_map/ppermute | solution.py:625
  37.0 11.0 %collective-permute-start.5 = (bf16[48,1920]{1,0:T(8,128)(2,1)S(1)}, bf16[48,1920]{1,0:T(8,128)(2,1)S(1)}, u32[]{:S(2)}, u32[]{:S(2)}) collective-permute-start(bf16[48,1920]{1,0:T(8,128)(2,1)S(1)} %pad_maximum_fusion.5), channel_id=1, source_target_pairs={{0,24},{1,25},{2,26},{3,27},{4,28},{5,29},{6,30},{7,31},{8,0},{9,1... | collective-permute-start | bytes 552968 | tf_op jit(solution)/shard_map/ppermute | solution.py:625
  53.3 29.8 %collective-permute-start.7 = (bf16[768,1280]{1,0:T(8,128)(2,1)S(1)}, bf16[768,1280]{1,0:T(8,128)(2,1)}, u32[]{:S(2)}, u32[]{:S(2)}) collective-permute-start(bf16[768,1280]{1,0:T(8,128)(2,1)S(1)} %bitcast_select_fusion.1.refs_1_.refs_2_.refs_6_), channel_id=1, source_target_pairs={{0,1},{1,0},{2,3},{3,2},{4,5},{5,4},{6,7},{7,6},{8,9},{9,8},{10,11... | collective-permute-start | bytes 5898248 | tf_op jit(solution)/shard_map/ppermute | solution.py:625
  59.9 60.6 %all-to-all-start.1 = ((bf16[4,2,192,768]{3,2,1,0:T(8,128)(2,1)}), bf16[4,2,192,768]{3,2,1,0:T(8,128)(2,1)}, u32[]{:S(2)}, u32[]{:S(2)}) async-start(bf16[4,2,192,768]{3,2,1,0:T(8,128)(2,1)} %broadcast_in_dim.141), calls=%async_computation.1 | async-start | bytes 4718592 | tf_op jit(solution)/shard_map/all_to_all | solution.py:650
  67.6 26.7 %collective-permute-start.8 = (bf16[4,48,1920]{2,1,0:T(8,128)(2,1)S(1)}, bf16[4,48,1920]{2,1,0:T(8,128)(2,1)S(1)}, u32[]{:S(2)}, u32[]{:S(2)}) collective-permute-start(bf16[4,48,1920]{2,1,0:T(8,128)(2,1)S(1)} %fusion.3), channel_id=1, source_target_pairs={{0,4},{1,5},{2,6},{3,7},{4,0},{5,1},{6,2},{7,3},{8,12},{9,13},{10,... | collective-permute-start | bytes 2211848 | tf_op jit(solution)/shard_map/ppermute | solution.py:625
  69.1 25.2 %collective-permute-start.9 = (bf16[4,48,1920]{2,1,0:T(8,128)(2,1)S(1)}, bf16[4,48,1920]{2,1,0:T(8,128)(2,1)S(1)}, u32[]{:S(2)}, u32[]{:S(2)}) collective-permute-start(bf16[4,48,1920]{2,1,0:T(8,128)(2,1)S(1)} %fusion.3), channel_id=1, source_target_pairs={{0,2},{1,3},{2,0},{3,1},{4,6},{5,7},{6,4},{7,5},{8,10},{9,11},{10,... | collective-permute-start | bytes 2211848 | tf_op jit(solution)/shard_map/ppermute | solution.py:625
  95.2 16.7 %collective-permute-start.10 = (bf16[4,48,1920]{2,1,0:T(8,128)(2,1)S(1)}, bf16[4,48,1920]{2,1,0:T(8,128)(2,1)S(1)}, u32[]{:S(2)}, u32[]{:S(2)}) collective-permute-start(bf16[4,48,1920]{2,1,0:T(8,128)(2,1)S(1)} %collective-permute-done.8), channel_id=1, source_target_pairs={{0,2},{1,3},{2,0},{3,1},{4,6},{5,7},{6,4},{7,5},{8,10},{9,11},{10,... | collective-permute-start | bytes 2211848 | tf_op jit(solution)/shard_map/ppermute | solution.py:625
  151.1 25.9 %collective-permute-start.14 = (bf16[768,1536]{1,0:T(8,128)(2,1)}, bf16[768,1536]{1,0:T(8,128)(2,1)}, u32[]{:S(2)}, u32[]{:S(2)}) collective-permute-start(bf16[768,1536]{1,0:T(8,128)(2,1)} %get-tuple-element.123), channel_id=1, source_target_pairs={{0,1},{1,0},{2,3},{3,2},{4,5},{5,4},{6,7},{7,6},{8,9},{9,8},{10,11... | collective-permute-start | bytes 7077896 | tf_op jit(solution)/shard_map/ppermute | solution.py:625
  151.6 25.4 %collective-permute-start.15 = (bf16[768,1536]{1,0:T(8,128)(2,1)}, bf16[768,1536]{1,0:T(8,128)(2,1)S(1)}, u32[]{:S(2)}, u32[]{:S(2)}) collective-permute-start(bf16[768,1536]{1,0:T(8,128)(2,1)} %get-tuple-element.124), channel_id=1, source_target_pairs={{0,1},{1,0},{2,3},{3,2},{4,5},{5,4},{6,7},{7,6},{8,9},{9,8},{10,11... | collective-permute-start | bytes 7077896 | tf_op jit(solution)/shard_map/ppermute | solution.py:625
  184.9 34.9 %collective-permute-start.17 = (bf16[4,2,48,1536]{3,2,0,1:T(8,128)(2,1)S(1)}, bf16[4,2,48,1536]{3,2,0,1:T(8,128)(2,1)S(1)}, u32[]{:S(2)}, u32[]{:S(2)}) collective-permute-start(bf16[4,2,48,1536]{3,2,0,1:T(8,128)(2,1)S(1)} %get-tuple-element.185), channel_id=1, source_target_pairs={{0,2},{1,3},{2,0},{3,1},{4,6},{5,7},{6,4},{7,5},{8,10},{9,11},{10,... | collective-permute-start | bytes 3538952 | tf_op jit(solution)/shard_map/ppermute | solution.py:625
  186.4 33.4 %collective-permute-start.16 = (bf16[4,2,48,1536]{3,2,1,0:T(8,128)(2,1)}, bf16[4,2,48,1536]{3,2,1,0:T(8,128)(2,1)S(1)}, u32[]{:S(2)}, u32[]{:S(2)}) collective-permute-start(bf16[4,2,48,1536]{3,2,1,0:T(8,128)(2,1)} %fusion.7), channel_id=1, source_target_pairs={{0,4},{1,5},{2,6},{3,7},{4,0},{5,1},{6,2},{7,3},{8,12},{9,13},{10,... | collective-permute-start | bytes 3538952 | tf_op jit(solution)/shard_map/ppermute | solution.py:625
  198.3 21.5 %collective-permute-start.18 = (bf16[768,384]{1,0:T(8,128)(2,1)}, bf16[768,384]{1,0:T(8,128)(2,1)}, u32[]{:S(2)}, u32[]{:S(2)}) collective-permute-start(bf16[768,384]{1,0:T(8,128)(2,1)} %get-tuple-element.131), channel_id=1, source_target_pairs={{0,1},{1,0},{2,3},{3,2},{4,5},{5,4},{6,7},{7,6},{8,9},{9,8},{10,11... | collective-permute-start | bytes 1769480 | tf_op jit(solution)/shard_map/ppermute | solution.py:625
  222.2 37.3 %all-to-all-start.2 = ((bf16[4,256,768]{2,1,0:T(8,128)(2,1)}), bf16[4,256,768]{2,1,0:T(8,128)(2,1)}, u32[]{:S(2)}, u32[]{:S(2)}) async-start(bf16[4,256,768]{2,1,0:T(8,128)(2,1)} %bitcast.166), calls=%async_computation.2 | async-start | bytes 3145728 | tf_op jit(solution)/shard_map/all_to_all | solution.py:694
  227.2 31.0 %collective-permute-start.20 = (bf16[4,48,1536]{2,1,0:T(8,128)(2,1)}, bf16[4,48,1536]{2,1,0:T(8,128)(2,1)}, u32[]{:S(2)}, u32[]{:S(2)}) collective-permute-start(bf16[4,48,1536]{2,1,0:T(8,128)(2,1)} %select_bitcast_fusion.2), channel_id=1, source_target_pairs={{0,4},{1,5},{2,6},{3,7},{4,0},{5,1},{6,2},{7,3},{8,12},{9,13},{10,... | collective-permute-start | bytes 1769480 | tf_op jit(solution)/shard_map/ppermute | solution.py:625
  227.7 31.7 %collective-permute-start.19 = (bf16[4,48,1536]{2,1,0:T(8,128)(2,1)}, bf16[4,48,1536]{2,1,0:T(8,128)(2,1)}, u32[]{:S(2)}, u32[]{:S(2)}) collective-permute-start(bf16[4,48,1536]{2,1,0:T(8,128)(2,1)} %fusion.10), channel_id=1, source_target_pairs={{0,2},{1,3},{2,0},{3,1},{4,6},{5,7},{6,4},{7,5},{8,10},{9,11},{10,... | collective-permute-start | bytes 1769480 | tf_op jit(solution)/shard_map/ppermute | solution.py:625
  256.2 17.7 %collective-permute-start.24 = (bf16[384,896]{1,0:T(8,128)(2,1)}, bf16[384,896]{1,0:T(8,128)(2,1)}, u32[]{:S(2)}, u32[]{:S(2)}) collective-permute-start(bf16[384,896]{1,0:T(8,128)(2,1)} %get-tuple-element.151), channel_id=1, source_target_pairs={{0,4},{1,5},{2,6},{3,7},{4,0},{5,1},{6,2},{7,3},{8,12},{9,13},{10,... | collective-permute-start | bytes 2064392 | tf_op jit(solution)/shard_map/ppermute | solution.py:625
  257.8 15.1 %collective-permute-start.23 = (bf16[384,768]{1,0:T(8,128)(2,1)}, bf16[384,768]{1,0:T(8,128)(2,1)}, u32[]{:S(2)}, u32[]{:S(2)}) collective-permute-start(bf16[384,768]{1,0:T(8,128)(2,1)} %get-tuple-element.150), channel_id=1, source_target_pairs={{0,2},{1,3},{2,0},{3,1},{4,6},{5,7},{6,4},{7,5},{8,10},{9,11},{10,... | collective-permute-start | bytes 1769480 | tf_op jit(solution)/shard_map/ppermute | solution.py:625
  262.6 16.3 %collective-permute-start.29 = (bf16[48,3072]{1,0:T(8,128)(2,1)S(1)}, bf16[48,3072]{1,0:T(8,128)(2,1)S(1)}, u32[]{:S(2)}, u32[]{:S(2)}) collective-permute-start(bf16[48,3072]{1,0:T(8,128)(2,1)S(1)} %pad_maximum_fusion.4), channel_id=1, source_target_pairs={{0,24},{1,25},{2,26},{3,27},{4,28},{5,29},{6,30},{7,31},{8,0},{9,1... | collective-permute-start | bytes 884744 | tf_op jit(solution)/shard_map/ppermute | solution.py:625
  265.9 24.1 %collective-permute-start.28 = (bf16[48,3072]{1,0:T(8,128)(2,1)S(1)}, bf16[48,3072]{1,0:T(8,128)(2,1)S(1)}, u32[]{:S(2)}, u32[]{:S(2)}) collective-permute-start(bf16[48,3072]{1,0:T(8,128)(2,1)S(1)} %pad_maximum_fusion.3), channel_id=1, source_target_pairs={{0,16},{1,17},{2,18},{3,19},{4,20},{5,21},{6,22},{7,23},{8,24},{9,... | collective-permute-start | bytes 884744 | tf_op jit(solution)/shard_map/ppermute | solution.py:625
  266.0 24.0 %collective-permute-start.27 = (bf16[48,3072]{1,0:T(8,128)(2,1)S(1)}, bf16[48,3072]{1,0:T(8,128)(2,1)S(1)}, u32[]{:S(2)}, u32[]{:S(2)}) collective-permute-start(bf16[48,3072]{1,0:T(8,128)(2,1)S(1)} %pad_maximum_fusion.2), channel_id=1, source_target_pairs={{0,8},{1,9},{2,10},{3,11},{4,12},{5,13},{6,14},{7,15},{8,16},{9,17... | collective-permute-start | bytes 884744 | tf_op jit(solution)/shard_map/ppermute | solution.py:625
  275.2 15.0 %collective-permute-start.26 = (bf16[4,48,896]{2,1,0:T(8,128)(2,1)S(1)}, bf16[4,48,896]{2,1,0:T(8,128)(2,1)S(1)}, u32[]{:S(2)}, u32[]{:S(2)}) collective-permute-start(bf16[4,48,896]{2,1,0:T(8,128)(2,1)S(1)} %select_bitcast_fusion.3), channel_id=1, source_target_pairs={{0,2},{1,3},{2,0},{3,1},{4,6},{5,7},{6,4},{7,5},{8,10},{9,11},{10,... | collective-permute-start | bytes 1032200 | tf_op jit(solution)/shard_map/ppermute | solution.py:625
  278.3 11.9 %collective-permute-start.25 = (bf16[4,48,768]{2,1,0:T(8,128)(2,1)S(1)}, bf16[4,48,768]{2,1,0:T(8,128)(2,1)S(1)}, u32[]{:S(2)}, u32[]{:S(2)}) collective-permute-start(bf16[4,48,768]{2,1,0:T(8,128)(2,1)S(1)} %select_bitcast_fusion.4), channel_id=1, source_target_pairs={{0,4},{1,5},{2,6},{3,7},{4,0},{5,1},{6,2},{7,3},{8,12},{9,13},{10,... | collective-permute-start | bytes 884744 | tf_op jit(solution)/shard_map/ppermute | solution.py:625
  295.5 23.9 %all-to-all-start.3 = ((bf16[4,256,768]{2,1,0:T(8,128)(2,1)}), bf16[4,256,768]{2,1,0:T(8,128)(2,1)S(1)}, u32[]{:S(2)}, u32[]{:S(2)}) async-start(bf16[4,256,768]{2,1,0:T(8,128)(2,1)} %bitcast.167), calls=%async_computation.3 | async-start | bytes 3145728 | tf_op jit(solution)/shard_map/all_to_all | solution.py:694
  299.1 18.7 %collective-permute-start.31 = (bf16[48,1664]{1,0:T(8,128)(2,1)}, bf16[48,1664]{1,0:T(8,128)(2,1)S(1)}, u32[]{:S(2)}, u32[]{:S(2)}) collective-permute-start(bf16[48,1664]{1,0:T(8,128)(2,1)} %pad_maximum_fusion.7), channel_id=1, source_target_pairs={{0,16},{1,17},{2,18},{3,19},{4,20},{5,21},{6,22},{7,23},{8,24},{9,... | collective-permute-start | bytes 479240 | tf_op jit(solution)/shard_map/ppermute | solution.py:625
  302.7 15.1 %collective-permute-start.30 = (bf16[48,1664]{1,0:T(8,128)(2,1)}, bf16[48,1664]{1,0:T(8,128)(2,1)}, u32[]{:S(2)}, u32[]{:S(2)}) collective-permute-start(bf16[48,1664]{1,0:T(8,128)(2,1)} %pad_maximum_fusion.6), channel_id=1, source_target_pairs={{0,8},{1,9},{2,10},{3,11},{4,12},{5,13},{6,14},{7,15},{8,16},{9,17... | collective-permute-start | bytes 479240 | tf_op jit(solution)/shard_map/ppermute | solution.py:625
  304.8 17.8 %collective-permute-start.37 = (bf16[2,48,3072]{2,1,0:T(8,128)(2,1)S(1)}, bf16[2,48,3072]{2,1,0:T(8,128)(2,1)S(1)}, u32[]{:S(2)}, u32[]{:S(2)}) collective-permute-start(bf16[2,48,3072]{2,1,0:T(8,128)(2,1)S(1)} %broadcast_select_fusion.3), channel_id=1, source_target_pairs={{0,1},{1,0},{2,3},{3,2},{4,5},{5,4},{6,7},{7,6},{8,9},{9,8},{10,11... | collective-permute-start | bytes 1769480 | tf_op jit(solution)/shard_map/ppermute | solution.py:625
  (42 other events, 241.9 us)

commit v5 on v4

--- a/solution.py
+++ b/solution.py
@@ -526,9 +526,49 @@
     return list(outs[:3]) + [grad_down]
 
 
+def spread_kernel(widths, where_ref, *refs):
+    del where_ref
+    count = len(refs) // (2 * len(widths) + 1)
+    ins, outs = refs[: 2 * len(widths) * count], refs[2 * len(widths) * count :]
+    position = 0
+    for out in outs:
+        start = 0
+        for width in widths:
+            total = ins[position][0].astype(F32) + ins[position + 1][0].astype(F32)
+            out[:, start : start + width] = total.astype(BF16)
+            start += width
+            position += 2
+
+
+def spread(where, *items):
+    z_count, part = items[0][0].shape[:2]
+    widths = [item[0].shape[-1] for item in items]
+    arrays, in_specs = [], []
+    for step in range(z_count):
+        for item in items:
+            spec = pl.BlockSpec(
+                (1, part, item[0].shape[-1]),
+                lambda i, where_ref, step=step: ((where_ref[0] + step) % z_count, 0, 0),
+            )
+            arrays += item
+            in_specs += [spec, spec]
+    return pl.pallas_call(
+        functools.partial(spread_kernel, widths),
+        grid_spec=pltpu.PrefetchScalarGridSpec(
+            num_scalar_prefetch=1,
+            grid=(1,),
+            in_specs=in_specs,
+            out_specs=[pl.BlockSpec((part, sum(widths)), lambda i, _: (0, 0))] * z_count,
+        ),
+        out_shape=[shaped((part, sum(widths)), BF16)] * z_count,
+        compiler_params=params(58),
+        cost_estimate=cost(0.01),
+    )(where, *arrays)
+
+
 def by_place(where_ref, refs):
     x, c = where_ref[0], where_ref[1]
-    own, other_x, other_c, other_both = (ref[...].astype(F32) for ref in refs)
+    own, other_x, other_c, other_both = (ref[...] for ref in refs)
     low_x = [jnp.where(x == 0, own, other_x), jnp.where(x == 0, other_c, other_both)]
     high_x = [jnp.where(x == 0, other_x, own), jnp.where(x == 0, other_both, other_c)]
     return [
@@ -568,11 +608,13 @@
                 for which in range(3):
                     place = which * dim + core * dim // 2 + pair * 128
                     start = (pair * 3 + which) * 128
-                    qkv_ref[here, place : place + 128] = piece[:, start : start + 128]
+                    qkv_ref[here, place : place + 128] = piece[:, start : start + 128].astype(F32)
             start = pairs * 384 + 128
-            proj_ref[here, core * dim // 2 : (core + 1) * dim // 2] = piece[:, start:]
+            proj_ref[here, core * dim // 2 : (core + 1) * dim // 2] = piece[:, start:].astype(F32)
         norms = slice(pairs * 384, pairs * 384 + 128)
-        sums.append(pieces[0][side][:, norms] + pieces[1][side][:, norms])
+        sums.append(
+            pieces[0][side][:, norms].astype(F32) + pieces[1][side][:, norms].astype(F32)
+        )
     sums = jnp.concatenate(sums, axis=0).T
     for place, norm_ref in enumerate(norm_refs):
         norm_ref[...] = sums[place : place + 1].reshape(norm_ref.shape)
@@ -829,7 +871,9 @@
     right_got = grid.send(right_out, x=1)
     grad_home = exchange(after(grad_x.reshape(4, SEQ // 4, dim), left_got))
     left_got, right_got = after((left_got, right_got), ffn_got)
-    qkv_parts = grid.by_block((left_keep, left_got), (right_keep, right_got))
+    qkv_parts = spread(
+        grid.z.reshape(1).astype(jnp.int32), (left_keep, left_got), (right_keep, right_got)
+    )
     sum_ffn = after(grid.total([ffn_parts[0], *ffn_got]), qkv_parts)
     ffn_x = grid.send(sum_ffn, x=1)
     qkv_got = [grid.send(part, z=step) for step, part in enumerate(qkv_parts) if step]

time: 339 us -> 337 us (level)
  other arithmetic: 32.8 us -> 28.9 us
    ppermute x38, waiting for transfers between devices: 63.5 us -> 58.1 us  [send(): return lax.ppermute(value, BOTH, pairs)]
    unnamed x65 -> x71, local copies, waits for them, and re-layouts: 6.82 us -> 7.6 us
  transfers between devices with their start and end apart: 42 -> 42, of which waited for: 14 -> 14; matrix products, arithmetic and copies ran while one was open for 9% -> 9% of each run, Pallas kernels for 35% -> 36%
where the time goes in v5:
time: 337 us; the launch traced here: 331 us
  Pallas kernels  146 us (43%)
  waiting for transfers between devices  69.5 us (21%)
  starting transfers between devices  65.8 us (20%)
  other arithmetic  28.9 us (9%)
  local copies, waits for them, and re-layouts  18.8 us (6%)
    ppermute x38, waiting for transfers between devices, send(): return lax.ppermute(value, BOTH, pairs)  58.1 us
    pallas_call x2, Pallas kernels, attend_back(): pl.pallas_call(functools.partial(attend_back_kernel, carry is not None, b...  47.2 us
    pallas_call x2, Pallas kernels, feed_forward(): pl.pallas_call(functools.partial(ffn_kernel, int(final), paired), grid=(2...  46 us
    ppermute x38, starting transfers between devices, send(): return lax.ppermute(value, BOTH, pairs)  45.7 us
    pallas_call x2, Pallas kernels, attend(): pl.pallas_call(functools.partial(attend_kernel, first), grid=(pairs,), in...  23.6 us
    all_to_all x3, starting transfers between devices, exchange(): lax.all_to_all(value, 'head', split_axis=0, concat_axis=0, tiled=True)  12.8 us
    pallas_call x1, Pallas kernels, middle_back(): pl.pallas_call(middle_kernel, grid_spec=pltpu.PrefetchScalarGridSpec(num_...  10.3 us
    select_n x7, other arithmetic, halves(): return (jnp.where(index == 0, high, low), jnp.where(index == 0, low, high))  9.95 us
  transfers between devices with their start and end apart: 42, of which 14 were waited for; matrix products, arithmetic and copies ran while one was open for 9% of the time, Pallas kernels for 36%

profile of v5, /device:TPU:0, one launch (start us, length us, event | category | flops | bytes accessed | tf_op | source)
XLA Modules:
  0.0 330.5 jit_solution(3451941412082774091)
XLA Ops:
  4.7 3.1 collective-permute-start
  7.8 2.6 collective-permute-start.1
  11.7 3.4 %pad_maximum_fusion = bf16[4,2,256,768]{3,2,1,0:T(8,128)(2,1)} fusion(bf16[4,1,256,768]{3,2,1,0:T(8,128)(2,1)S(1)} %bitcast.147, bf16[4,1,256,768]{3,2,1,0:T(8,128)(2,1)} %bitcast.148), kind=kLoop, calls=%fused_computation.3 | loop fusion | flops 1572864 | bytes 6291456 | tf_op jit(solution)/shard_map/stack | solution.py:787
  15.1 4.7 %all-to-all-start = ((bf16[4,2,256,768]{3,2,1,0:T(8,128)(2,1)}), bf16[4,2,256,768]{3,2,1,0:T(8,128)(2,1)}, u32[]{:S(2)}, u32[]{:S(2)}) async-start(bf16[4,2,256,768]{3,2,1,0:T(8,128)(2,1)} %pad_maximum_fusion), calls=%async_computation | async-start | bytes 6291456 | tf_op jit(solution)/shard_map/all_to_all | solution.py:736
  24.0 2.5 collective-permute-done.1
  29.7 5.7 %collective-permute-start.3 = (bf16[48,1920]{1,0:T(8,128)(2,1)S(1)}, bf16[48,1920]{1,0:T(8,128)(2,1)S(1)}, u32[]{:S(2)}, u32[]{:S(2)}) collective-permute-start(bf16[48,1920]{1,0:T(8,128)(2,1)S(1)} %pad_maximum_fusion.5), channel_id=1, source_target_pairs={{0,8},{1,9},{2,10},{3,11},{4,12},{5,13},{6,14},{7,15},{8,16},{9,17... | collective-permute-start | bytes 552968 | tf_op jit(solution)/shard_map/ppermute | solution.py:667
  37.8 4.1 %collective-permute-done.3 = bf16[48,1920]{1,0:T(8,128)(2,1)S(1)} collective-permute-done((bf16[48,1920]{1,0:T(8,128)(2,1)S(1)}, bf16[48,1920]{1,0:T(8,128)(2,1)S(1)}, u32[]{:S(2)}, u32[]{:S(2)}) %collective-permute-start.3) | collective-permute-done | bytes 184352 | tf_op jit(solution)/shard_map/ppermute | solution.py:667
  41.9 6.0 %collective-permute-done.4 = bf16[48,1920]{1,0:T(8,128)(2,1)S(1)} collective-permute-done((bf16[48,1920]{1,0:T(8,128)(2,1)S(1)}, bf16[48,1920]{1,0:T(8,128)(2,1)S(1)}, u32[]{:S(2)}, u32[]{:S(2)}) %collective-permute-start.4) | collective-permute-done | bytes 184352 | tf_op jit(solution)/shard_map/ppermute | solution.py:667
  53.4 4.8 %collective-permute-done.12 = bf16[192,768]{1,0:T(8,128)(2,1)S(1)} collective-permute-done((bf16[192,768]{1,0:T(8,128)(2,1)S(1)}, bf16[192,768]{1,0:T(8,128)(2,1)S(1)}, u32[]{:S(2)}, u32[]{:S(2)}) %collective-permute-start.12) | collective-permute-done | bytes 294944 | tf_op jit(solution)/shard_map/ppermute | solution.py:667
  59.9 7.4 %all-to-all-start.1 = ((bf16[4,2,192,768]{3,2,1,0:T(8,128)(2,1)}), bf16[4,2,192,768]{3,2,1,0:T(8,128)(2,1)}, u32[]{:S(2)}, u32[]{:S(2)}) async-start(bf16[4,2,192,768]{3,2,1,0:T(8,128)(2,1)} %broadcast_in_dim.141), calls=%async_computation.1 | async-start | bytes 4718592 | tf_op jit(solution)/shard_map/all_to_all | solution.py:692
  70.6 12.4 %shard_map.177 = (bf16[1024,768]{1,0:T(8,128)(2,1)}, bf16[1024,1152]{1,0:T(8,128)(2,1)}, bf16[1024,384]{1,0:T(8,128)(2,1)}, f32[3,2,1024]{2,1,0:T(2,128)}, f32[8,768]{1,0:T(8,128)}) custom-call(bf16[4,2,256,768]{3,2,1,0:T(8,128)(2,1)} %all-to-all-done.refs_0_.x_ref.refs_1_.cot_ref.refs_8_, bf16[768,1280]{1,0:T(8,128)(2,1)} %copy-done.3, ...), custom_call_target="tpu_custom_call" | custom-call | flops 11000000 | bytes 30000 | tf_op jit(solution)/shard_map/pallas_call | solution.py:256
  83.0 11.2 %shard_map.178 = (bf16[1024,1152]{1,0:T(8,128)(2,1)}, bf16[1024,384]{1,0:T(8,128)(2,1)}, f32[3,2,1024]{2,1,0:T(2,128)}) custom-call(bf16[1024,768]{1,0:T(8,128)(2,1)} %get-tuple-element.113.refs_0_.refs_4_.refs_5_, bf16[768,1280]{1,0:T(8,128)(2,1)} %collective-permute-done.7.refs_1_.refs_5_), custom_call_target="tpu_custom_call" | custom-call | flops 11000000 | bytes 30000 | tf_op jit(solution)/shard_map/pallas_call | solution.py:256
  95.8 16.0 %collective-permute-done.10 = bf16[4,48,1920]{2,1,0:T(8,128)(2,1)S(1)} collective-permute-done((bf16[4,48,1920]{2,1,0:T(8,128)(2,1)S(1)}, bf16[4,48,1920]{2,1,0:T(8,128)(2,1)S(1)}, u32[]{:S(2)}, u32[]{:S(2)}) %collective-permute-start.10) | collective-permute-done | bytes 737312 | tf_op jit(solution)/shard_map/ppermute | solution.py:667
  113.8 6.6 %all-to-all-done.1 = bf16[4,2,192,768]{3,2,1,0:T(8,128)(2,1)} async-done(((bf16[4,2,192,768]{3,2,1,0:T(8,128)(2,1)}), bf16[4,2,192,768]{3,2,1,0:T(8,128)(2,1)}, u32[]{:S(2)}, u32[]{:S(2)}) %all-to-all-start.1) | async-done | bytes 2359328 | tf_op jit(solution)/shard_map/all_to_all | solution.py:692
  120.5 6.6 %shard_map.179 = (bf16[1024,768]{1,0:T(8,128)(2,1)}, bf16[1024,768]{1,0:T(8,128)(2,1)}) custom-call(s32[1]{0:T(128)} %bitcast.core_ref, bf16[4,2,256,768]{3,2,1,0:T(8,128)(2,1)} %all-to-all-done.refs_0_.x_ref.refs_1_.cot_ref.refs_8_, bf16[1024,384]{1,0:T(8,128)(2,1)} %get-tuple-element.112.am_ref.refs_3_, ...), custom_call_target="tpu_custom_call" | custom-call | flops 11000000 | bytes 30000 | tf_op jit(solution)/shard_map/pallas_call | solution.py:105
  128.4 22.7 %shard_map.180 = (f32[1024,768]{1,0:T(8,128)}, bf16[1024,768]{1,0:T(8,128)(2,1)}, bf16[768,1536]{1,0:T(8,128)(2,1)}, bf16[768,1536]{1,0:T(8,128)(2,1)}) custom-call(bf16[1024,768]{1,0:T(8,128)(2,1)} %get-tuple-element.118.refs_0_, bf16[4,2,256,768]{3,2,1,0:T(8,128)(2,1)} %all-to-all-done.refs_0_.x_ref.refs_1_.cot_ref.refs_8_, ...), custom_call_target="tpu_custom_call" | custom-call | flops 11000000 | bytes 30000 | tf_op jit(solution)/shard_map/pallas_call | solution.py:511
  151.7 23.3 %shard_map.181 = (bf16[1024,768]{1,0:T(8,128)(2,1)}, bf16[1024,768]{1,0:T(8,128)(2,1)}, bf16[768,1536]{1,0:T(8,128)(2,1)}, bf16[768,1536]{1,0:T(8,128)(2,1)}) custom-call(bf16[1024,768]{1,0:T(8,128)(2,1)} %get-tuple-element.118.refs_0_, bf16[4,2,256,768]{3,2,1,0:T(8,128)(2,1)} %all-to-all-done.refs_0_.x_ref.refs_1_.cot_ref.refs_8_, ...), custom_call_target="tpu_custom_call" | custom-call | flops 11000000 | bytes 30000 | tf_op jit(solution)/shard_map/pallas_call | solution.py:511
  187.9 10.3 %shard_map.182 = (bf16[1024,768]{1,0:T(8,128)(2,1)}, bf16[1024,384]{1,0:T(8,128)(2,1)}, bf16[1024,384]{1,0:T(8,128)(2,1)}, bf16[768,384]{1,0:T(8,128)(2,1)}, bf16[768,384]{1,0:T(8,128)(2,1)}, /*index=5*/f32[8,768]{1,0:T(8,128)}) custom-call(s32[1]{0:T(128)} %bitcast.core_ref, bf16[1024,768]{1,0:T(8,128)(2,1)} %get-tuple-element.123.refs_4_.mid_ref, ...), custom_call_target="tpu_custom_call" | custom-call | flops 11000000 | bytes 30000 | tf_op jit(solution)/shard_map/pallas_call | solution.py:162
  198.3 20.9 %shard_map.183 = (bf16[768,768]{1,0:T(8,128)(2,1)}, bf16[768,512]{1,0:T(8,128)(2,1)}, bf16[1024,768]{1,0:T(8,128)(2,1)}) custom-call(bf16[1024,1152]{1,0:T(8,128)(2,1)} %get-tuple-element.136.refs_0_, bf16[1024,384]{1,0:T(8,128)(2,1)} %get-tuple-element.137.refs_1_, bf16[1024,384]{1,0:T(8,128)(2,1)} %get-tuple-element.114.at_ref.refs_2_, ...), custom_call_target="tpu_custom_call" | custom-call | flops 11000000 | bytes 30000 | tf_op jit(solution)/shard_map/pallas_call | solution.py:419
  222.1 4.5 %all-to-all-start.2 = ((bf16[4,256,768]{2,1,0:T(8,128)(2,1)}), bf16[4,256,768]{2,1,0:T(8,128)(2,1)}, u32[]{:S(2)}, u32[]{:S(2)}) async-start(bf16[4,256,768]{2,1,0:T(8,128)(2,1)} %bitcast.145), calls=%async_computation.2 | async-start | bytes 3145728 | tf_op jit(solution)/shard_map/all_to_all | solution.py:736
  229.9 26.2 %shard_map.184 = (bf16[384,768]{1,0:T(8,128)(2,1)}, bf16[384,768]{1,0:T(8,128)(2,1)}, bf16[384,896]{1,0:T(8,128)(2,1)}, bf16[384,896]{1,0:T(8,128)(2,1)}, bf16[1024,768]{1,0:T(8,128)(2,1)}, /*index=5*/f32[8,768]{1,0:T(8,128)}) custom-call(s32[2]{0:T(128)} %pad_add_fusion.refs_0_, bf16[1024,1152]{1,0:T(8,128)(2,1)} %get-tuple-element.144.refs_1_, ...), custom_call_target="tpu_custom_call" | custom-call | flops 11000000 | bytes 30000 | tf_op jit(solution)/shard_map/pallas_call | solution.py:419
  262.5 3.3 collective-permute-start.29
  266.6 3.6 %shard_map.185 = bf16[4,256,768]{2,1,0:T(8,128)(2,1)} custom-call(bf16[4,256,768]{2,1,0:T(8,128)(2,1)} %all-to-all-done.2.in_ref), custom_call_target="tpu_custom_call" | custom-call | flops 11000000 | bytes 30000 | tf_op jit(solution)/shard_map/pallas_call | solution.py:629
  270.1 2.7 collective-permute-done.23
  280.2 9.7 %collective-permute-done.28 = bf16[48,3072]{1,0:T(8,128)(2,1)S(1)} collective-permute-done((bf16[48,3072]{1,0:T(8,128)(2,1)S(1)}, bf16[48,3072]{1,0:T(8,128)(2,1)S(1)}, u32[]{:S(2)}, u32[]{:S(2)}) %collective-permute-start.28) | collective-permute-done | bytes 294944 | tf_op jit(solution)/shard_map/ppermute | solution.py:667
  290.9 2.2 shard_map.186
  293.8 3.6 %all-to-all-start.3 = ((bf16[4,256,768]{2,1,0:T(8,128)(2,1)}), bf16[4,256,768]{2,1,0:T(8,128)(2,1)S(1)}, u32[]{:S(2)}, u32[]{:S(2)}) async-start(bf16[4,256,768]{2,1,0:T(8,128)(2,1)} %bitcast.146), calls=%async_computation.3 | async-start | bytes 3145728 | tf_op jit(solution)/shard_map/all_to_all | solution.py:736
  301.0 2.8 collective-permute-start.32
  306.4 6.3 %collective-permute-done.31 = bf16[48,1664]{1,0:T(8,128)(2,1)S(1)} collective-permute-done((bf16[48,1664]{1,0:T(8,128)(2,1)}, bf16[48,1664]{1,0:T(8,128)(2,1)S(1)}, u32[]{:S(2)}, u32[]{:S(2)}) %collective-permute-start.31) | collective-permute-done | bytes 159776 | tf_op jit(solution)/shard_map/ppermute | solution.py:667
  312.8 4.9 %all-to-all-done.3 = bf16[4,256,768]{2,1,0:T(8,128)(2,1)S(1)} async-done(((bf16[4,256,768]{2,1,0:T(8,128)(2,1)}), bf16[4,256,768]{2,1,0:T(8,128)(2,1)S(1)}, u32[]{:S(2)}, u32[]{:S(2)}) %all-to-all-start.3) | async-done | bytes 1572896 | tf_op jit(solution)/shard_map/all_to_all | solution.py:736
  323.1 3.6 %shard_map.187 = (f32[96,3072]{1,0:T(8,128)}, f32[384,768]{1,0:T(8,128)}) custom-call(s32[2]{0:T(128)} %pad_add_fusion.1.where_ref, bf16[2,2,48,3072]{3,2,1,0:T(8,128)(2,1)} %broadcast_select_fusion.2.all_ref), custom_call_target="tpu_custom_call" | custom-call | flops 11000000 | bytes 30000 | tf_op jit(solution)/shard_map/pallas_call | solution.py:640
  327.4 2.9 shard_map.188
  (194 shorter events, 78.3 us)
Async XLA Ops:
  4.7 19.3 %collective-permute-start = (bf16[96,1280]{1,0:T(8,128)(2,1)S(1)}, bf16[96,1280]{1,0:T(8,128)(2,1)}, u32[]{:S(2)}, u32[]{:S(2)}) collective-permute-start(bf16[96,1280]{1,0:T(8,128)(2,1)S(1)} %fusion.14), channel_id=1, source_target_pairs={{0,8},{1,9},{2,10},{3,11},{4,12},{5,13},{6,14},{7,15},{8,16},{9,17... | collective-permute-start | bytes 737288 | tf_op jit(solution)/shard_map/ppermute | solution.py:667
  7.8 18.8 %collective-permute-start.1 = (bf16[96,1280]{1,0:T(8,128)(2,1)S(1)}, bf16[96,1280]{1,0:T(8,128)(2,1)}, u32[]{:S(2)}, u32[]{:S(2)}) collective-permute-start(bf16[96,1280]{1,0:T(8,128)(2,1)S(1)} %fusion.14), channel_id=1, source_target_pairs={{0,16},{1,17},{2,18},{3,19},{4,20},{5,21},{6,22},{7,23},{8,24},{9,... | collective-permute-start | bytes 737288 | tf_op jit(solution)/shard_map/ppermute | solution.py:667
  10.4 16.2 %collective-permute-start.2 = (bf16[96,1280]{1,0:T(8,128)(2,1)S(1)}, bf16[96,1280]{1,0:T(8,128)(2,1)}, u32[]{:S(2)}, u32[]{:S(2)}) collective-permute-start(bf16[96,1280]{1,0:T(8,128)(2,1)S(1)} %fusion.14), channel_id=1, source_target_pairs={{0,24},{1,25},{2,26},{3,27},{4,28},{5,29},{6,30},{7,31},{8,0},{9,1... | collective-permute-start | bytes 737288 | tf_op jit(solution)/shard_map/ppermute | solution.py:667
  15.1 43.2 %all-to-all-start = ((bf16[4,2,256,768]{3,2,1,0:T(8,128)(2,1)}), bf16[4,2,256,768]{3,2,1,0:T(8,128)(2,1)}, u32[]{:S(2)}, u32[]{:S(2)}) async-start(bf16[4,2,256,768]{3,2,1,0:T(8,128)(2,1)} %pad_maximum_fusion), calls=%async_computation | async-start | bytes 6291456 | tf_op jit(solution)/shard_map/all_to_all | solution.py:736
  28.1 23.8 %collective-permute-start.6 = (bf16[4,96,1280]{2,1,0:T(8,128)(2,1)S(1)}, bf16[4,96,1280]{2,1,0:T(8,128)(2,1)}, u32[]{:S(2)}, u32[]{:S(2)}) collective-permute-start(bf16[4,96,1280]{2,1,0:T(8,128)(2,1)S(1)} %fusion), channel_id=1, source_target_pairs={{0,4},{1,5},{2,6},{3,7},{4,0},{5,1},{6,2},{7,3},{8,12},{9,13},{10,... | collective-permute-start | bytes 2949128 | tf_op jit(solution)/shard_map/ppermute | solution.py:667
  29.7 12.2 %collective-permute-start.3 = (bf16[48,1920]{1,0:T(8,128)(2,1)S(1)}, bf16[48,1920]{1,0:T(8,128)(2,1)S(1)}, u32[]{:S(2)}, u32[]{:S(2)}) collective-permute-start(bf16[48,1920]{1,0:T(8,128)(2,1)S(1)} %pad_maximum_fusion.5), channel_id=1, source_target_pairs={{0,8},{1,9},{2,10},{3,11},{4,12},{5,13},{6,14},{7,15},{8,16},{9,17... | collective-permute-start | bytes 552968 | tf_op jit(solution)/shard_map/ppermute | solution.py:667
  35.4 12.5 %collective-permute-start.4 = (bf16[48,1920]{1,0:T(8,128)(2,1)S(1)}, bf16[48,1920]{1,0:T(8,128)(2,1)S(1)}, u32[]{:S(2)}, u32[]{:S(2)}) collective-permute-start(bf16[48,1920]{1,0:T(8,128)(2,1)S(1)} %pad_maximum_fusion.5), channel_id=1, source_target_pairs={{0,16},{1,17},{2,18},{3,19},{4,20},{5,21},{6,22},{7,23},{8,24},{9,... | collective-permute-start | bytes 552968 | tf_op jit(solution)/shard_map/ppermute | solution.py:667
  37.0 11.0 %collective-permute-start.5 = (bf16[48,1920]{1,0:T(8,128)(2,1)S(1)}, bf16[48,1920]{1,0:T(8,128)(2,1)S(1)}, u32[]{:S(2)}, u32[]{:S(2)}) collective-permute-start(bf16[48,1920]{1,0:T(8,128)(2,1)S(1)} %pad_maximum_fusion.5), channel_id=1, source_target_pairs={{0,24},{1,25},{2,26},{3,27},{4,28},{5,29},{6,30},{7,31},{8,0},{9,1... | collective-permute-start | bytes 552968 | tf_op jit(solution)/shard_map/ppermute | solution.py:667
  53.3 29.7 %collective-permute-start.7 = (bf16[768,1280]{1,0:T(8,128)(2,1)S(1)}, bf16[768,1280]{1,0:T(8,128)(2,1)}, u32[]{:S(2)}, u32[]{:S(2)}) collective-permute-start(bf16[768,1280]{1,0:T(8,128)(2,1)S(1)} %bitcast_select_fusion.1.refs_1_.refs_2_.refs_6_), channel_id=1, source_target_pairs={{0,1},{1,0},{2,3},{3,2},{4,5},{5,4},{6,7},{7,6},{8,9},{9,8},{10,11... | collective-permute-start | bytes 5898248 | tf_op jit(solution)/shard_map/ppermute | solution.py:667
  59.9 60.6 %all-to-all-start.1 = ((bf16[4,2,192,768]{3,2,1,0:T(8,128)(2,1)}), bf16[4,2,192,768]{3,2,1,0:T(8,128)(2,1)}, u32[]{:S(2)}, u32[]{:S(2)}) async-start(bf16[4,2,192,768]{3,2,1,0:T(8,128)(2,1)} %broadcast_in_dim.141), calls=%async_computation.1 | async-start | bytes 4718592 | tf_op jit(solution)/shard_map/all_to_all | solution.py:692
  67.6 26.7 %collective-permute-start.8 = (bf16[4,48,1920]{2,1,0:T(8,128)(2,1)S(1)}, bf16[4,48,1920]{2,1,0:T(8,128)(2,1)S(1)}, u32[]{:S(2)}, u32[]{:S(2)}) collective-permute-start(bf16[4,48,1920]{2,1,0:T(8,128)(2,1)S(1)} %fusion.3), channel_id=1, source_target_pairs={{0,4},{1,5},{2,6},{3,7},{4,0},{5,1},{6,2},{7,3},{8,12},{9,13},{10,... | collective-permute-start | bytes 2211848 | tf_op jit(solution)/shard_map/ppermute | solution.py:667
  69.1 25.1 %collective-permute-start.9 = (bf16[4,48,1920]{2,1,0:T(8,128)(2,1)S(1)}, bf16[4,48,1920]{2,1,0:T(8,128)(2,1)S(1)}, u32[]{:S(2)}, u32[]{:S(2)}) collective-permute-start(bf16[4,48,1920]{2,1,0:T(8,128)(2,1)S(1)} %fusion.3), channel_id=1, source_target_pairs={{0,2},{1,3},{2,0},{3,1},{4,6},{5,7},{6,4},{7,5},{8,10},{9,11},{10,... | collective-permute-start | bytes 2211848 | tf_op jit(solution)/shard_map/ppermute | solution.py:667
  95.1 16.7 %collective-permute-start.10 = (bf16[4,48,1920]{2,1,0:T(8,128)(2,1)S(1)}, bf16[4,48,1920]{2,1,0:T(8,128)(2,1)S(1)}, u32[]{:S(2)}, u32[]{:S(2)}) collective-permute-start(bf16[4,48,1920]{2,1,0:T(8,128)(2,1)S(1)} %collective-permute-done.8), channel_id=1, source_target_pairs={{0,2},{1,3},{2,0},{3,1},{4,6},{5,7},{6,4},{7,5},{8,10},{9,11},{10,... | collective-permute-start | bytes 2211848 | tf_op jit(solution)/shard_map/ppermute | solution.py:667
  151.2 25.9 %collective-permute-start.14 = (bf16[768,1536]{1,0:T(8,128)(2,1)}, bf16[768,1536]{1,0:T(8,128)(2,1)}, u32[]{:S(2)}, u32[]{:S(2)}) collective-permute-start(bf16[768,1536]{1,0:T(8,128)(2,1)} %get-tuple-element.127), channel_id=1, source_target_pairs={{0,1},{1,0},{2,3},{3,2},{4,5},{5,4},{6,7},{7,6},{8,9},{9,8},{10,11... | collective-permute-start | bytes 7077896 | tf_op jit(solution)/shard_map/ppermute | solution.py:667
  151.6 25.4 %collective-permute-start.15 = (bf16[768,1536]{1,0:T(8,128)(2,1)}, bf16[768,1536]{1,0:T(8,128)(2,1)S(1)}, u32[]{:S(2)}, u32[]{:S(2)}) collective-permute-start(bf16[768,1536]{1,0:T(8,128)(2,1)} %get-tuple-element.128), channel_id=1, source_target_pairs={{0,1},{1,0},{2,3},{3,2},{4,5},{5,4},{6,7},{7,6},{8,9},{9,8},{10,11... | collective-permute-start | bytes 7077896 | tf_op jit(solution)/shard_map/ppermute | solution.py:667
  184.8 34.9 %collective-permute-start.17 = (bf16[4,2,48,1536]{3,2,0,1:T(8,128)(2,1)S(1)}, bf16[4,2,48,1536]{3,2,0,1:T(8,128)(2,1)S(1)}, u32[]{:S(2)}, u32[]{:S(2)}) collective-permute-start(bf16[4,2,48,1536]{3,2,0,1:T(8,128)(2,1)S(1)} %get-tuple-element.193), channel_id=1, source_target_pairs={{0,2},{1,3},{2,0},{3,1},{4,6},{5,7},{6,4},{7,5},{8,10},{9,11},{10,... | collective-permute-start | bytes 3538952 | tf_op jit(solution)/shard_map/ppermute | solution.py:667
  186.4 33.4 %collective-permute-start.16 = (bf16[4,2,48,1536]{3,2,1,0:T(8,128)(2,1)}, bf16[4,2,48,1536]{3,2,1,0:T(8,128)(2,1)S(1)}, u32[]{:S(2)}, u32[]{:S(2)}) collective-permute-start(bf16[4,2,48,1536]{3,2,1,0:T(8,128)(2,1)} %fusion.7), channel_id=1, source_target_pairs={{0,4},{1,5},{2,6},{3,7},{4,0},{5,1},{6,2},{7,3},{8,12},{9,13},{10,... | collective-permute-start | bytes 3538952 | tf_op jit(solution)/shard_map/ppermute | solution.py:667
  198.3 21.5 %collective-permute-start.18 = (bf16[768,384]{1,0:T(8,128)(2,1)}, bf16[768,384]{1,0:T(8,128)(2,1)}, u32[]{:S(2)}, u32[]{:S(2)}) collective-permute-start(bf16[768,384]{1,0:T(8,128)(2,1)} %get-tuple-element.135), channel_id=1, source_target_pairs={{0,1},{1,0},{2,3},{3,2},{4,5},{5,4},{6,7},{7,6},{8,9},{9,8},{10,11... | collective-permute-start | bytes 1769480 | tf_op jit(solution)/shard_map/ppermute | solution.py:667
  222.1 37.3 %all-to-all-start.2 = ((bf16[4,256,768]{2,1,0:T(8,128)(2,1)}), bf16[4,256,768]{2,1,0:T(8,128)(2,1)}, u32[]{:S(2)}, u32[]{:S(2)}) async-start(bf16[4,256,768]{2,1,0:T(8,128)(2,1)} %bitcast.145), calls=%async_computation.2 | async-start | bytes 3145728 | tf_op jit(solution)/shard_map/all_to_all | solution.py:736
  227.2 31.1 %collective-permute-start.20 = (bf16[4,48,1536]{2,1,0:T(8,128)(2,1)}, bf16[4,48,1536]{2,1,0:T(8,128)(2,1)}, u32[]{:S(2)}, u32[]{:S(2)}) collective-permute-start(bf16[4,48,1536]{2,1,0:T(8,128)(2,1)} %select_bitcast_fusion.2), channel_id=1, source_target_pairs={{0,4},{1,5},{2,6},{3,7},{4,0},{5,1},{6,2},{7,3},{8,12},{9,13},{10,... | collective-permute-start | bytes 1769480 | tf_op jit(solution)/shard_map/ppermute | solution.py:667
  227.7 31.7 %collective-permute-start.19 = (bf16[4,48,1536]{2,1,0:T(8,128)(2,1)}, bf16[4,48,1536]{2,1,0:T(8,128)(2,1)}, u32[]{:S(2)}, u32[]{:S(2)}) collective-permute-start(bf16[4,48,1536]{2,1,0:T(8,128)(2,1)} %fusion.10), channel_id=1, source_target_pairs={{0,2},{1,3},{2,0},{3,1},{4,6},{5,7},{6,4},{7,5},{8,10},{9,11},{10,... | collective-permute-start | bytes 1769480 | tf_op jit(solution)/shard_map/ppermute | solution.py:667
  256.2 17.7 %collective-permute-start.24 = (bf16[384,896]{1,0:T(8,128)(2,1)}, bf16[384,896]{1,0:T(8,128)(2,1)}, u32[]{:S(2)}, u32[]{:S(2)}) collective-permute-start(bf16[384,896]{1,0:T(8,128)(2,1)} %get-tuple-element.155), channel_id=1, source_target_pairs={{0,4},{1,5},{2,6},{3,7},{4,0},{5,1},{6,2},{7,3},{8,12},{9,13},{10,... | collective-permute-start | bytes 2064392 | tf_op jit(solution)/shard_map/ppermute | solution.py:667
  257.7 15.1 %collective-permute-start.23 = (bf16[384,768]{1,0:T(8,128)(2,1)}, bf16[384,768]{1,0:T(8,128)(2,1)}, u32[]{:S(2)}, u32[]{:S(2)}) collective-permute-start(bf16[384,768]{1,0:T(8,128)(2,1)} %get-tuple-element.154), channel_id=1, source_target_pairs={{0,2},{1,3},{2,0},{3,1},{4,6},{5,7},{6,4},{7,5},{8,10},{9,11},{10,... | collective-permute-start | bytes 1769480 | tf_op jit(solution)/shard_map/ppermute | solution.py:667
  262.5 17.7 %collective-permute-start.29 = (bf16[48,3072]{1,0:T(8,128)(2,1)S(1)}, bf16[48,3072]{1,0:T(8,128)(2,1)S(1)}, u32[]{:S(2)}, u32[]{:S(2)}) collective-permute-start(bf16[48,3072]{1,0:T(8,128)(2,1)S(1)} %pad_maximum_fusion.4), channel_id=1, source_target_pairs={{0,24},{1,25},{2,26},{3,27},{4,28},{5,29},{6,30},{7,31},{8,0},{9,1... | collective-permute-start | bytes 884744 | tf_op jit(solution)/shard_map/ppermute | solution.py:667
  265.8 24.1 %collective-permute-start.28 = (bf16[48,3072]{1,0:T(8,128)(2,1)S(1)}, bf16[48,3072]{1,0:T(8,128)(2,1)S(1)}, u32[]{:S(2)}, u32[]{:S(2)}) collective-permute-start(bf16[48,3072]{1,0:T(8,128)(2,1)S(1)} %pad_maximum_fusion.3), channel_id=1, source_target_pairs={{0,16},{1,17},{2,18},{3,19},{4,20},{5,21},{6,22},{7,23},{8,24},{9,... | collective-permute-start | bytes 884744 | tf_op jit(solution)/shard_map/ppermute | solution.py:667
  266.0 24.0 %collective-permute-start.27 = (bf16[48,3072]{1,0:T(8,128)(2,1)S(1)}, bf16[48,3072]{1,0:T(8,128)(2,1)S(1)}, u32[]{:S(2)}, u32[]{:S(2)}) collective-permute-start(bf16[48,3072]{1,0:T(8,128)(2,1)S(1)} %pad_maximum_fusion.2), channel_id=1, source_target_pairs={{0,8},{1,9},{2,10},{3,11},{4,12},{5,13},{6,14},{7,15},{8,16},{9,17... | collective-permute-start | bytes 884744 | tf_op jit(solution)/shard_map/ppermute | solution.py:667
  275.9 14.2 %collective-permute-start.26 = (bf16[4,48,896]{2,1,0:T(8,128)(2,1)S(1)}, bf16[4,48,896]{2,1,0:T(8,128)(2,1)S(1)}, u32[]{:S(2)}, u32[]{:S(2)}) collective-permute-start(bf16[4,48,896]{2,1,0:T(8,128)(2,1)S(1)} %get-tuple-element.199), channel_id=1, source_target_pairs={{0,2},{1,3},{2,0},{3,1},{4,6},{5,7},{6,4},{7,5},{8,10},{9,11},{10,... | collective-permute-start | bytes 1032200 | tf_op jit(solution)/shard_map/ppermute | solution.py:667
  293.1 10.7 %collective-permute-start.36 = (bf16[48,3072]{1,0:T(8,128)(2,1)S(1)}, bf16[48,3072]{1,0:T(8,128)(2,1)S(1)}, u32[]{:S(2)}, u32[]{:S(2)}) collective-permute-start(bf16[48,3072]{1,0:T(8,128)(2,1)S(1)} %add_convert_fusion.9), channel_id=1, source_target_pairs={{0,2},{1,3},{2,0},{3,1},{4,6},{5,7},{6,4},{7,5},{8,10},{9,11},{10,... | collective-permute-start | bytes 884744 | tf_op jit(solution)/shard_map/ppermute | solution.py:667
  293.8 23.9 %all-to-all-start.3 = ((bf16[4,256,768]{2,1,0:T(8,128)(2,1)}), bf16[4,256,768]{2,1,0:T(8,128)(2,1)S(1)}, u32[]{:S(2)}, u32[]{:S(2)}) async-start(bf16[4,256,768]{2,1,0:T(8,128)(2,1)} %bitcast.146), calls=%async_computation.3 | async-start | bytes 3145728 | tf_op jit(solution)/shard_map/all_to_all | solution.py:736
  299.0 13.8 %collective-permute-start.31 = (bf16[48,1664]{1,0:T(8,128)(2,1)}, bf16[48,1664]{1,0:T(8,128)(2,1)S(1)}, u32[]{:S(2)}, u32[]{:S(2)}) collective-permute-start(bf16[48,1664]{1,0:T(8,128)(2,1)} %get-tuple-element.166), channel_id=1, source_target_pairs={{0,16},{1,17},{2,18},{3,19},{4,20},{5,21},{6,22},{7,23},{8,24},{9,... | collective-permute-start | bytes 479240 | tf_op jit(solution)/shard_map/ppermute | solution.py:667
  301.0 11.8 %collective-permute-start.32 = (bf16[48,1664]{1,0:T(8,128)(2,1)}, bf16[48,1664]{1,0:T(8,128)(2,1)S(1)}, u32[]{:S(2)}, u32[]{:S(2)}) collective-permute-start(bf16[48,1664]{1,0:T(8,128)(2,1)} %get-tuple-element.167), channel_id=1, source_target_pairs={{0,24},{1,25},{2,26},{3,27},{4,28},{5,29},{6,30},{7,31},{8,0},{9,1... | collective-permute-start | bytes 479240 | tf_op jit(solution)/shard_map/ppermute | solution.py:667
  304.0 16.0 %collective-permute-start.37 = (bf16[2,48,3072]{2,1,0:T(8,128)(2,1)S(1)}, bf16[2,48,3072]{2,1,0:T(8,128)(2,1)S(1)}, u32[]{:S(2)}, u32[]{:S(2)}) collective-permute-start(bf16[2,48,3072]{2,1,0:T(8,128)(2,1)S(1)} %broadcast_select_fusion.3), channel_id=1, source_target_pairs={{0,1},{1,0},{2,3},{3,2},{4,5},{5,4},{6,7},{7,6},{8,9},{9,8},{10,11... | collective-permute-start | bytes 1769480 | tf_op jit(solution)/shard_map/ppermute | solution.py:667
  (45 other events, 267.6 us)

commit v6 on v5

--- a/solution.py
+++ b/solution.py
@@ -878,15 +878,14 @@
     ffn_x = grid.send(sum_ffn, x=1)
     qkv_got = [grid.send(part, z=step) for step, part in enumerate(qkv_parts) if step]
     qkv_got, grad_home = after((qkv_got, grad_home), grad_home)
-    sum_qkv = grid.total([qkv_parts[0], *qkv_got])
     ffn_x = grid.join(sum_ffn, ffn_x, grid.x, 0)
     all_ffn = grid.join(ffn_x, grid.send(ffn_x, c=1), grid.c, 0)
+    shard_up, shard_down = finish(
+        functools.partial(finish_ffn, fan), where_head, [all_ffn], (share, hidden), (2 * fan, dim)
+    )
+    sum_qkv = grid.total([qkv_parts[0], *after(qkv_got, shard_up)])
     shares = grid.share(sum_qkv)
     grad_home = after(grad_home, sum_qkv).astype(F32)
-    shard_up, shard_down = finish(
-        functools.partial(finish_ffn, fan), where_head, [after(all_ffn, sum_qkv)],
-        (share, hidden), (2 * fan, dim),
-    )
     shard_qkv, shard_proj, *norms = finish(
         functools.partial(finish_qkv, pairs), where_head, after(shares, shard_up),
         (share, 3 * dim), (share, dim), *[(share,)] * 4,

time: 337 us -> 344 us (1.021)
  the two profiles are of different devices: /device:TPU:0 before, /device:TPU:17 now
where the time goes in v6:
time: 344 us; the launch traced here: 338 us
  Pallas kernels  146 us (42%)
  waiting for transfers between devices  83.5 us (24%)
  starting transfers between devices  59.8 us (17%)
  other arithmetic  28.9 us (8%)
  local copies, waits for them, and re-layouts  18 us (5%)
    ppermute x38, waiting for transfers between devices, send(): return lax.ppermute(value, BOTH, pairs)  76.6 us
    pallas_call x2, Pallas kernels, attend_back(): pl.pallas_call(functools.partial(attend_back_kernel, carry is not None, b...  47.1 us
    pallas_call x2, Pallas kernels, feed_forward(): pl.pallas_call(functools.partial(ffn_kernel, int(final), paired), grid=(2...  46 us
    ppermute x38, starting transfers between devices, send(): return lax.ppermute(value, BOTH, pairs)  40.2 us
    pallas_call x2, Pallas kernels, attend(): pl.pallas_call(functools.partial(attend_kernel, first), grid=(pairs,), in...  23.6 us
    all_to_all x3, starting transfers between devices, exchange(): lax.all_to_all(value, 'head', split_axis=0, concat_axis=0, tiled=True)  14.5 us
    pallas_call x1, Pallas kernels, middle_back(): pl.pallas_call(middle_kernel, grid_spec=pltpu.PrefetchScalarGridSpec(num_...  10.3 us
    select_n x7, other arithmetic, halves(): return (jnp.where(index == 0, high, low), jnp.where(index == 0, low, high))  9.95 us
  transfers between devices with their start and end apart: 42, of which 20 were waited for; matrix products, arithmetic and copies ran while one was open for 9% of the time, Pallas kernels for 35%

profile of v6, /device:TPU:17, one launch (start us, length us, event | category | flops | bytes accessed | tf_op | source)
XLA Modules:
  0.0 337.8 jit_solution(8734652069298461688)
XLA Ops:
  7.3 3.4 pad_maximum_fusion
  10.7 5.8 %all-to-all-start = ((bf16[4,2,256,768]{3,2,1,0:T(8,128)(2,1)}), bf16[4,2,256,768]{3,2,1,0:T(8,128)(2,1)}, u32[]{:S(2)}, u32[]{:S(2)}) async-start(bf16[4,2,256,768]{3,2,1,0:T(8,128)(2,1)} %pad_maximum_fusion), calls=%async_computation | async-start | bytes 6291456 | tf_op jit(solution)/shard_map/all_to_all | solution.py:736
  22.0 5.3 %collective-permute-done.2 = bf16[96,1280]{1,0:T(8,128)(2,1)} collective-permute-done((bf16[96,1280]{1,0:T(8,128)(2,1)S(1)}, bf16[96,1280]{1,0:T(8,128)(2,1)}, u32[]{:S(2)}, u32[]{:S(2)}) %collective-permute-start.2) | collective-permute-done | bytes 245792 | tf_op jit(solution)/shard_map/ppermute | solution.py:667
  33.6 3.2 collective-permute-done.3
  36.8 6.7 %collective-permute-done.4 = bf16[48,1920]{1,0:T(8,128)(2,1)S(1)} collective-permute-done((bf16[48,1920]{1,0:T(8,128)(2,1)S(1)}, bf16[48,1920]{1,0:T(8,128)(2,1)S(1)}, u32[]{:S(2)}, u32[]{:S(2)}) %collective-permute-start.4) | collective-permute-done | bytes 184352 | tf_op jit(solution)/shard_map/ppermute | solution.py:667
  43.5 3.9 %collective-permute-done.5 = bf16[48,1920]{1,0:T(8,128)(2,1)S(1)} collective-permute-done((bf16[48,1920]{1,0:T(8,128)(2,1)S(1)}, bf16[48,1920]{1,0:T(8,128)(2,1)S(1)}, u32[]{:S(2)}, u32[]{:S(2)}) %collective-permute-start.5) | collective-permute-done | bytes 184352 | tf_op jit(solution)/shard_map/ppermute | solution.py:667
  48.6 3.3 collective-permute-done.6
  53.3 2.3 collective-permute-start.7
  55.6 2.4 collective-permute-done.12
  59.8 5.1 %all-to-all-start.1 = ((bf16[4,2,192,768]{3,2,1,0:T(8,128)(2,1)}), bf16[4,2,192,768]{3,2,1,0:T(8,128)(2,1)}, u32[]{:S(2)}, u32[]{:S(2)}) async-start(bf16[4,2,192,768]{3,2,1,0:T(8,128)(2,1)} %broadcast_in_dim.141), calls=%async_computation.1 | async-start | bytes 4718592 | tf_op jit(solution)/shard_map/all_to_all | solution.py:692
  67.7 12.4 %shard_map.177 = (bf16[1024,768]{1,0:T(8,128)(2,1)}, bf16[1024,1152]{1,0:T(8,128)(2,1)}, bf16[1024,384]{1,0:T(8,128)(2,1)}, f32[3,2,1024]{2,1,0:T(2,128)}, f32[8,768]{1,0:T(8,128)}) custom-call(bf16[4,2,256,768]{3,2,1,0:T(8,128)(2,1)} %all-to-all-done.refs_0_.x_ref.refs_1_.cot_ref.refs_8_, bf16[768,1280]{1,0:T(8,128)(2,1)} %copy-done.3, ...), custom_call_target="tpu_custom_call" | custom-call | flops 11000000 | bytes 30000 | tf_op jit(solution)/shard_map/pallas_call | solution.py:256
  80.1 11.2 %shard_map.178 = (bf16[1024,1152]{1,0:T(8,128)(2,1)}, bf16[1024,384]{1,0:T(8,128)(2,1)}, f32[3,2,1024]{2,1,0:T(2,128)}) custom-call(bf16[1024,768]{1,0:T(8,128)(2,1)} %get-tuple-element.115.refs_0_.refs_4_.refs_5_, bf16[768,1280]{1,0:T(8,128)(2,1)} %collective-permute-done.7.refs_1_.refs_5_), custom_call_target="tpu_custom_call" | custom-call | flops 11000000 | bytes 30000 | tf_op jit(solution)/shard_map/pallas_call | solution.py:256
  92.6 15.2 %collective-permute-done.10 = bf16[4,48,1920]{2,1,0:T(8,128)(2,1)S(1)} collective-permute-done((bf16[4,48,1920]{2,1,0:T(8,128)(2,1)S(1)}, bf16[4,48,1920]{2,1,0:T(8,128)(2,1)S(1)}, u32[]{:S(2)}, u32[]{:S(2)}) %collective-permute-start.10) | collective-permute-done | bytes 737312 | tf_op jit(solution)/shard_map/ppermute | solution.py:667
  109.7 3.3 collective-permute-start.11
  118.2 6.5 %shard_map.179 = (bf16[1024,768]{1,0:T(8,128)(2,1)}, bf16[1024,768]{1,0:T(8,128)(2,1)}) custom-call(s32[1]{0:T(128)} %bitcast.core_ref, bf16[4,2,256,768]{3,2,1,0:T(8,128)(2,1)} %all-to-all-done.refs_0_.x_ref.refs_1_.cot_ref.refs_8_, bf16[1024,384]{1,0:T(8,128)(2,1)} %get-tuple-element.114.am_ref.refs_3_, ...), custom_call_target="tpu_custom_call" | custom-call | flops 11000000 | bytes 30000 | tf_op jit(solution)/shard_map/pallas_call | solution.py:105
  126.1 22.7 %shard_map.180 = (f32[1024,768]{1,0:T(8,128)}, bf16[1024,768]{1,0:T(8,128)(2,1)}, bf16[768,1536]{1,0:T(8,128)(2,1)}, bf16[768,1536]{1,0:T(8,128)(2,1)}) custom-call(bf16[1024,768]{1,0:T(8,128)(2,1)} %get-tuple-element.120.refs_0_, bf16[4,2,256,768]{3,2,1,0:T(8,128)(2,1)} %all-to-all-done.refs_0_.x_ref.refs_1_.cot_ref.refs_8_, ...), custom_call_target="tpu_custom_call" | custom-call | flops 11000000 | bytes 30000 | tf_op jit(solution)/shard_map/pallas_call | solution.py:511
  149.4 23.3 %shard_map.181 = (bf16[1024,768]{1,0:T(8,128)(2,1)}, bf16[1024,768]{1,0:T(8,128)(2,1)}, bf16[768,1536]{1,0:T(8,128)(2,1)}, bf16[768,1536]{1,0:T(8,128)(2,1)}) custom-call(bf16[1024,768]{1,0:T(8,128)(2,1)} %get-tuple-element.120.refs_0_, bf16[4,2,256,768]{3,2,1,0:T(8,128)(2,1)} %all-to-all-done.refs_0_.x_ref.refs_1_.cot_ref.refs_8_, ...), custom_call_target="tpu_custom_call" | custom-call | flops 11000000 | bytes 30000 | tf_op jit(solution)/shard_map/pallas_call | solution.py:511
  183.5 10.3 %shard_map.182 = (bf16[1024,768]{1,0:T(8,128)(2,1)}, bf16[1024,384]{1,0:T(8,128)(2,1)}, bf16[1024,384]{1,0:T(8,128)(2,1)}, bf16[768,384]{1,0:T(8,128)(2,1)}, bf16[768,384]{1,0:T(8,128)(2,1)}, /*index=5*/f32[8,768]{1,0:T(8,128)}) custom-call(s32[1]{0:T(128)} %bitcast.core_ref, bf16[1024,768]{1,0:T(8,128)(2,1)} %get-tuple-element.125.refs_4_.mid_ref, ...), custom_call_target="tpu_custom_call" | custom-call | flops 11000000 | bytes 30000 | tf_op jit(solution)/shard_map/pallas_call | solution.py:162
  194.5 20.9 %shard_map.183 = (bf16[768,768]{1,0:T(8,128)(2,1)}, bf16[768,512]{1,0:T(8,128)(2,1)}, bf16[1024,768]{1,0:T(8,128)(2,1)}) custom-call(bf16[1024,1152]{1,0:T(8,128)(2,1)} %get-tuple-element.138.refs_0_, bf16[1024,384]{1,0:T(8,128)(2,1)} %get-tuple-element.139.refs_1_, bf16[1024,384]{1,0:T(8,128)(2,1)} %get-tuple-element.116.at_ref.refs_2_, ...), custom_call_target="tpu_custom_call" | custom-call | flops 11000000 | bytes 30000 | tf_op jit(solution)/shard_map/pallas_call | solution.py:419
  217.8 5.0 %all-to-all-start.2 = ((bf16[4,256,768]{2,1,0:T(8,128)(2,1)}), bf16[4,256,768]{2,1,0:T(8,128)(2,1)}, u32[]{:S(2)}, u32[]{:S(2)}) async-start(bf16[4,256,768]{2,1,0:T(8,128)(2,1)} %bitcast.145), calls=%async_computation.2 | async-start | bytes 3145728 | tf_op jit(solution)/shard_map/all_to_all | solution.py:736
  226.4 26.2 %shard_map.184 = (bf16[384,768]{1,0:T(8,128)(2,1)}, bf16[384,768]{1,0:T(8,128)(2,1)}, bf16[384,896]{1,0:T(8,128)(2,1)}, bf16[384,896]{1,0:T(8,128)(2,1)}, bf16[1024,768]{1,0:T(8,128)(2,1)}, /*index=5*/f32[8,768]{1,0:T(8,128)}) custom-call(s32[2]{0:T(128)} %pad_add_fusion.refs_0_, bf16[1024,1152]{1,0:T(8,128)(2,1)} %get-tuple-element.146.refs_1_, ...), custom_call_target="tpu_custom_call" | custom-call | flops 11000000 | bytes 30000 | tf_op jit(solution)/shard_map/pallas_call | solution.py:419
  260.0 4.1 %collective-permute-start.28 = (bf16[48,3072]{1,0:T(8,128)(2,1)S(1)}, bf16[48,3072]{1,0:T(8,128)(2,1)S(1)}, u32[]{:S(2)}, u32[]{:S(2)}) collective-permute-start(bf16[48,3072]{1,0:T(8,128)(2,1)S(1)} %pad_maximum_fusion.3), channel_id=1, source_target_pairs={{0,16},{1,17},{2,18},{3,19},{4,20},{5,21},{6,22},{7,23},{8,24},{9,... | collective-permute-start | bytes 884744 | tf_op jit(solution)/shard_map/ppermute | solution.py:667
  264.1 3.6 %shard_map.185 = bf16[4,256,768]{2,1,0:T(8,128)(2,1)} custom-call(bf16[4,256,768]{2,1,0:T(8,128)(2,1)} %all-to-all-done.2.in_ref), custom_call_target="tpu_custom_call" | custom-call | flops 11000000 | bytes 30000 | tf_op jit(solution)/shard_map/pallas_call | solution.py:629
  275.8 8.5 %collective-permute-done.28 = bf16[48,3072]{1,0:T(8,128)(2,1)S(1)} collective-permute-done((bf16[48,3072]{1,0:T(8,128)(2,1)S(1)}, bf16[48,3072]{1,0:T(8,128)(2,1)S(1)}, u32[]{:S(2)}, u32[]{:S(2)}) %collective-permute-start.28) | collective-permute-done | bytes 294944 | tf_op jit(solution)/shard_map/ppermute | solution.py:667
  284.4 4.4 %collective-permute-done.27 = bf16[48,3072]{1,0:T(8,128)(2,1)S(1)} collective-permute-done((bf16[48,3072]{1,0:T(8,128)(2,1)S(1)}, bf16[48,3072]{1,0:T(8,128)(2,1)S(1)}, u32[]{:S(2)}, u32[]{:S(2)}) %collective-permute-start.27) | collective-permute-done | bytes 294944 | tf_op jit(solution)/shard_map/ppermute | solution.py:667
  292.4 6.8 %collective-permute-done.33 = bf16[48,3072]{1,0:T(8,128)(2,1)S(1)} collective-permute-done((bf16[48,3072]{1,0:T(8,128)(2,1)S(1)}, bf16[48,3072]{1,0:T(8,128)(2,1)S(1)}, u32[]{:S(2)}, u32[]{:S(2)}) %collective-permute-start.33) | collective-permute-done | bytes 294944 | tf_op jit(solution)/shard_map/ppermute | solution.py:667
  301.6 3.7 %all-to-all-start.3 = ((bf16[4,256,768]{2,1,0:T(8,128)(2,1)}), bf16[4,256,768]{2,1,0:T(8,128)(2,1)S(1)}, u32[]{:S(2)}, u32[]{:S(2)}) async-start(bf16[4,256,768]{2,1,0:T(8,128)(2,1)} %bitcast.146), calls=%async_computation.3 | async-start | bytes 3145728 | tf_op jit(solution)/shard_map/all_to_all | solution.py:736
  308.6 3.7 %shard_map.187 = (f32[96,3072]{1,0:T(8,128)}, f32[384,768]{1,0:T(8,128)}) custom-call(s32[2]{0:T(128)} %pad_add_fusion.1.where_ref, bf16[2,2,48,3072]{3,2,1,0:T(8,128)(2,1)} %broadcast_select_fusion.2.all_ref), custom_call_target="tpu_custom_call" | custom-call | flops 11000000 | bytes 30000 | tf_op jit(solution)/shard_map/pallas_call | solution.py:640
  312.3 6.3 %collective-permute-done.30 = bf16[48,1664]{1,0:T(8,128)(2,1)S(1)} collective-permute-done((bf16[48,1664]{1,0:T(8,128)(2,1)}, bf16[48,1664]{1,0:T(8,128)(2,1)S(1)}, u32[]{:S(2)}, u32[]{:S(2)}) %collective-permute-start.30) | collective-permute-done | bytes 159776 | tf_op jit(solution)/shard_map/ppermute | solution.py:667
  319.8 4.7 %all-to-all-done.3 = bf16[4,256,768]{2,1,0:T(8,128)(2,1)S(1)} async-done(((bf16[4,256,768]{2,1,0:T(8,128)(2,1)}), bf16[4,256,768]{2,1,0:T(8,128)(2,1)S(1)}, u32[]{:S(2)}, u32[]{:S(2)}) %all-to-all-start.3) | async-done | bytes 1572896 | tf_op jit(solution)/shard_map/all_to_all | solution.py:736
  329.5 4.5 %collective-permute-done.37.refs_3_ = bf16[48,1664]{1,0:T(8,128)(2,1)S(1)} collective-permute-done((bf16[48,1664]{1,0:T(8,128)(2,1)S(1)}, bf16[48,1664]{1,0:T(8,128)(2,1)S(1)}, u32[]{:S(2)}, u32[]{:S(2)}) %collective-permute-start.37) | collective-permute-done | bytes 159776 | tf_op jit(solution)/shard_map/ppermute | solution.py:667
  334.7 2.9 shard_map.188
  (198 shorter events, 84.3 us)
Async XLA Ops:
  4.7 16.0 %collective-permute-start = (bf16[96,1280]{1,0:T(8,128)(2,1)S(1)}, bf16[96,1280]{1,0:T(8,128)(2,1)}, u32[]{:S(2)}, u32[]{:S(2)}) collective-permute-start(bf16[96,1280]{1,0:T(8,128)(2,1)S(1)} %fusion.14), channel_id=1, source_target_pairs={{0,8},{1,9},{2,10},{3,11},{4,12},{5,13},{6,14},{7,15},{8,16},{9,17... | collective-permute-start | bytes 737288 | tf_op jit(solution)/shard_map/ppermute | solution.py:667
  6.1 16.0 %collective-permute-start.1 = (bf16[96,1280]{1,0:T(8,128)(2,1)S(1)}, bf16[96,1280]{1,0:T(8,128)(2,1)}, u32[]{:S(2)}, u32[]{:S(2)}) collective-permute-start(bf16[96,1280]{1,0:T(8,128)(2,1)S(1)} %fusion.14), channel_id=1, source_target_pairs={{0,16},{1,17},{2,18},{3,19},{4,20},{5,21},{6,22},{7,23},{8,24},{9,... | collective-permute-start | bytes 737288 | tf_op jit(solution)/shard_map/ppermute | solution.py:667
  6.1 21.2 %collective-permute-start.2 = (bf16[96,1280]{1,0:T(8,128)(2,1)S(1)}, bf16[96,1280]{1,0:T(8,128)(2,1)}, u32[]{:S(2)}, u32[]{:S(2)}) collective-permute-start(bf16[96,1280]{1,0:T(8,128)(2,1)S(1)} %fusion.14), channel_id=1, source_target_pairs={{0,24},{1,25},{2,26},{3,27},{4,28},{5,29},{6,30},{7,31},{8,0},{9,1... | collective-permute-start | bytes 737288 | tf_op jit(solution)/shard_map/ppermute | solution.py:667
  10.7 47.5 %all-to-all-start = ((bf16[4,2,256,768]{3,2,1,0:T(8,128)(2,1)}), bf16[4,2,256,768]{3,2,1,0:T(8,128)(2,1)}, u32[]{:S(2)}, u32[]{:S(2)}) async-start(bf16[4,2,256,768]{3,2,1,0:T(8,128)(2,1)} %pad_maximum_fusion), calls=%async_computation | async-start | bytes 6291456 | tf_op jit(solution)/shard_map/all_to_all | solution.py:736
  28.8 23.0 %collective-permute-start.6 = (bf16[4,96,1280]{2,1,0:T(8,128)(2,1)S(1)}, bf16[4,96,1280]{2,1,0:T(8,128)(2,1)}, u32[]{:S(2)}, u32[]{:S(2)}) collective-permute-start(bf16[4,96,1280]{2,1,0:T(8,128)(2,1)S(1)} %fusion), channel_id=1, source_target_pairs={{0,4},{1,5},{2,6},{3,7},{4,0},{5,1},{6,2},{7,3},{8,12},{9,13},{10,... | collective-permute-start | bytes 2949128 | tf_op jit(solution)/shard_map/ppermute | solution.py:667
  31.5 12.0 %collective-permute-start.4 = (bf16[48,1920]{1,0:T(8,128)(2,1)S(1)}, bf16[48,1920]{1,0:T(8,128)(2,1)S(1)}, u32[]{:S(2)}, u32[]{:S(2)}) collective-permute-start(bf16[48,1920]{1,0:T(8,128)(2,1)S(1)} %pad_maximum_fusion.5), channel_id=1, source_target_pairs={{0,16},{1,17},{2,18},{3,19},{4,20},{5,21},{6,22},{7,23},{8,24},{9,... | collective-permute-start | bytes 552968 | tf_op jit(solution)/shard_map/ppermute | solution.py:667
  33.6 13.8 %collective-permute-start.5 = (bf16[48,1920]{1,0:T(8,128)(2,1)S(1)}, bf16[48,1920]{1,0:T(8,128)(2,1)S(1)}, u32[]{:S(2)}, u32[]{:S(2)}) collective-permute-start(bf16[48,1920]{1,0:T(8,128)(2,1)S(1)} %pad_maximum_fusion.5), channel_id=1, source_target_pairs={{0,24},{1,25},{2,26},{3,27},{4,28},{5,29},{6,30},{7,31},{8,0},{9,1... | collective-permute-start | bytes 552968 | tf_op jit(solution)/shard_map/ppermute | solution.py:667
  53.3 26.9 %collective-permute-start.7 = (bf16[768,1280]{1,0:T(8,128)(2,1)S(1)}, bf16[768,1280]{1,0:T(8,128)(2,1)}, u32[]{:S(2)}, u32[]{:S(2)}) collective-permute-start(bf16[768,1280]{1,0:T(8,128)(2,1)S(1)} %bitcast_select_fusion.1.refs_1_.refs_2_.refs_6_), channel_id=1, source_target_pairs={{0,1},{1,0},{2,3},{3,2},{4,5},{5,4},{6,7},{7,6},{8,9},{9,8},{10,11... | collective-permute-start | bytes 5898248 | tf_op jit(solution)/shard_map/ppermute | solution.py:667
  59.8 55.4 %all-to-all-start.1 = ((bf16[4,2,192,768]{3,2,1,0:T(8,128)(2,1)}), bf16[4,2,192,768]{3,2,1,0:T(8,128)(2,1)}, u32[]{:S(2)}, u32[]{:S(2)}) async-start(bf16[4,2,192,768]{3,2,1,0:T(8,128)(2,1)} %broadcast_in_dim.141), calls=%async_computation.1 | async-start | bytes 4718592 | tf_op jit(solution)/shard_map/all_to_all | solution.py:692
  65.2 26.1 %collective-permute-start.8 = (bf16[4,48,1920]{2,1,0:T(8,128)(2,1)S(1)}, bf16[4,48,1920]{2,1,0:T(8,128)(2,1)S(1)}, u32[]{:S(2)}, u32[]{:S(2)}) collective-permute-start(bf16[4,48,1920]{2,1,0:T(8,128)(2,1)S(1)} %fusion.3), channel_id=1, source_target_pairs={{0,4},{1,5},{2,6},{3,7},{4,0},{5,1},{6,2},{7,3},{8,12},{9,13},{10,... | collective-permute-start | bytes 2211848 | tf_op jit(solution)/shard_map/ppermute | solution.py:667
  66.5 24.8 %collective-permute-start.9 = (bf16[4,48,1920]{2,1,0:T(8,128)(2,1)S(1)}, bf16[4,48,1920]{2,1,0:T(8,128)(2,1)S(1)}, u32[]{:S(2)}, u32[]{:S(2)}) collective-permute-start(bf16[4,48,1920]{2,1,0:T(8,128)(2,1)S(1)} %fusion.3), channel_id=1, source_target_pairs={{0,2},{1,3},{2,0},{3,1},{4,6},{5,7},{6,4},{7,5},{8,10},{9,11},{10,... | collective-permute-start | bytes 2211848 | tf_op jit(solution)/shard_map/ppermute | solution.py:667
  92.2 15.6 %collective-permute-start.10 = (bf16[4,48,1920]{2,1,0:T(8,128)(2,1)S(1)}, bf16[4,48,1920]{2,1,0:T(8,128)(2,1)S(1)}, u32[]{:S(2)}, u32[]{:S(2)}) collective-permute-start(bf16[4,48,1920]{2,1,0:T(8,128)(2,1)S(1)} %collective-permute-done.8), channel_id=1, source_target_pairs={{0,2},{1,3},{2,0},{3,1},{4,6},{5,7},{6,4},{7,5},{8,10},{9,11},{10,... | collective-permute-start | bytes 2211848 | tf_op jit(solution)/shard_map/ppermute | solution.py:667
  148.9 25.8 %collective-permute-start.14 = (bf16[768,1536]{1,0:T(8,128)(2,1)}, bf16[768,1536]{1,0:T(8,128)(2,1)}, u32[]{:S(2)}, u32[]{:S(2)}) collective-permute-start(bf16[768,1536]{1,0:T(8,128)(2,1)} %get-tuple-element.129), channel_id=1, source_target_pairs={{0,1},{1,0},{2,3},{3,2},{4,5},{5,4},{6,7},{7,6},{8,9},{9,8},{10,11... | collective-permute-start | bytes 7077896 | tf_op jit(solution)/shard_map/ppermute | solution.py:667
  149.2 25.4 %collective-permute-start.15 = (bf16[768,1536]{1,0:T(8,128)(2,1)}, bf16[768,1536]{1,0:T(8,128)(2,1)S(1)}, u32[]{:S(2)}, u32[]{:S(2)}) collective-permute-start(bf16[768,1536]{1,0:T(8,128)(2,1)} %get-tuple-element.130), channel_id=1, source_target_pairs={{0,1},{1,0},{2,3},{3,2},{4,5},{5,4},{6,7},{7,6},{8,9},{9,8},{10,11... | collective-permute-start | bytes 7077896 | tf_op jit(solution)/shard_map/ppermute | solution.py:667
  182.5 33.0 %collective-permute-start.17 = (bf16[4,2,48,1536]{3,2,0,1:T(8,128)(2,1)S(1)}, bf16[4,2,48,1536]{3,2,0,1:T(8,128)(2,1)S(1)}, u32[]{:S(2)}, u32[]{:S(2)}) collective-permute-start(bf16[4,2,48,1536]{3,2,0,1:T(8,128)(2,1)S(1)} %get-tuple-element.197), channel_id=1, source_target_pairs={{0,2},{1,3},{2,0},{3,1},{4,6},{5,7},{6,4},{7,5},{8,10},{9,11},{10,... | collective-permute-start | bytes 3538952 | tf_op jit(solution)/shard_map/ppermute | solution.py:667
  182.8 32.7 %collective-permute-start.16 = (bf16[4,2,48,1536]{3,2,1,0:T(8,128)(2,1)}, bf16[4,2,48,1536]{3,2,1,0:T(8,128)(2,1)S(1)}, u32[]{:S(2)}, u32[]{:S(2)}) collective-permute-start(bf16[4,2,48,1536]{3,2,1,0:T(8,128)(2,1)} %fusion.7), channel_id=1, source_target_pairs={{0,4},{1,5},{2,6},{3,7},{4,0},{5,1},{6,2},{7,3},{8,12},{9,13},{10,... | collective-permute-start | bytes 3538952 | tf_op jit(solution)/shard_map/ppermute | solution.py:667
  193.8 21.6 %collective-permute-start.18 = (bf16[768,384]{1,0:T(8,128)(2,1)}, bf16[768,384]{1,0:T(8,128)(2,1)}, u32[]{:S(2)}, u32[]{:S(2)}) collective-permute-start(bf16[768,384]{1,0:T(8,128)(2,1)} %get-tuple-element.137), channel_id=1, source_target_pairs={{0,1},{1,0},{2,3},{3,2},{4,5},{5,4},{6,7},{7,6},{8,9},{9,8},{10,11... | collective-permute-start | bytes 1769480 | tf_op jit(solution)/shard_map/ppermute | solution.py:667
  215.5 11.0 %collective-permute-start.21 = (bf16[768,768]{1,0:T(8,128)(2,1)}, bf16[768,768]{1,0:T(8,128)(2,1)}, u32[]{:S(2)}, u32[]{:S(2)}) collective-permute-start(bf16[768,768]{1,0:T(8,128)(2,1)} %get-tuple-element.152), channel_id=1, source_target_pairs={{0,1},{1,0},{2,3},{3,2},{4,5},{5,4},{6,7},{7,6},{8,9},{9,8},{10,11... | collective-permute-start | bytes 3538952 | tf_op jit(solution)/shard_map/ppermute | solution.py:667
  217.8 36.9 %all-to-all-start.2 = ((bf16[4,256,768]{2,1,0:T(8,128)(2,1)}), bf16[4,256,768]{2,1,0:T(8,128)(2,1)}, u32[]{:S(2)}, u32[]{:S(2)}) async-start(bf16[4,256,768]{2,1,0:T(8,128)(2,1)} %bitcast.145), calls=%async_computation.2 | async-start | bytes 3145728 | tf_op jit(solution)/shard_map/all_to_all | solution.py:736
  222.9 31.7 %collective-permute-start.20 = (bf16[4,48,1536]{2,1,0:T(8,128)(2,1)}, bf16[4,48,1536]{2,1,0:T(8,128)(2,1)}, u32[]{:S(2)}, u32[]{:S(2)}) collective-permute-start(bf16[4,48,1536]{2,1,0:T(8,128)(2,1)} %select_bitcast_fusion.2), channel_id=1, source_target_pairs={{0,4},{1,5},{2,6},{3,7},{4,0},{5,1},{6,2},{7,3},{8,12},{9,13},{10,... | collective-permute-start | bytes 1769480 | tf_op jit(solution)/shard_map/ppermute | solution.py:667
  224.1 30.6 %collective-permute-start.19 = (bf16[4,48,1536]{2,1,0:T(8,128)(2,1)}, bf16[4,48,1536]{2,1,0:T(8,128)(2,1)}, u32[]{:S(2)}, u32[]{:S(2)}) collective-permute-start(bf16[4,48,1536]{2,1,0:T(8,128)(2,1)} %fusion.10), channel_id=1, source_target_pairs={{0,2},{1,3},{2,0},{3,1},{4,6},{5,7},{6,4},{7,5},{8,10},{9,11},{10,... | collective-permute-start | bytes 1769480 | tf_op jit(solution)/shard_map/ppermute | solution.py:667
  252.6 16.6 %collective-permute-start.24 = (bf16[384,896]{1,0:T(8,128)(2,1)}, bf16[384,896]{1,0:T(8,128)(2,1)}, u32[]{:S(2)}, u32[]{:S(2)}) collective-permute-start(bf16[384,896]{1,0:T(8,128)(2,1)} %get-tuple-element.157), channel_id=1, source_target_pairs={{0,4},{1,5},{2,6},{3,7},{4,0},{5,1},{6,2},{7,3},{8,12},{9,13},{10,... | collective-permute-start | bytes 2064392 | tf_op jit(solution)/shard_map/ppermute | solution.py:667
  253.1 14.7 %collective-permute-start.23 = (bf16[384,768]{1,0:T(8,128)(2,1)}, bf16[384,768]{1,0:T(8,128)(2,1)}, u32[]{:S(2)}, u32[]{:S(2)}) collective-permute-start(bf16[384,768]{1,0:T(8,128)(2,1)} %get-tuple-element.156), channel_id=1, source_target_pairs={{0,2},{1,3},{2,0},{3,1},{4,6},{5,7},{6,4},{7,5},{8,10},{9,11},{10,... | collective-permute-start | bytes 1769480 | tf_op jit(solution)/shard_map/ppermute | solution.py:667
  257.9 17.9 %collective-permute-start.29 = (bf16[48,3072]{1,0:T(8,128)(2,1)S(1)}, bf16[48,3072]{1,0:T(8,128)(2,1)S(1)}, u32[]{:S(2)}, u32[]{:S(2)}) collective-permute-start(bf16[48,3072]{1,0:T(8,128)(2,1)S(1)} %pad_maximum_fusion.4), channel_id=1, source_target_pairs={{0,24},{1,25},{2,26},{3,27},{4,28},{5,29},{6,30},{7,31},{8,0},{9,1... | collective-permute-start | bytes 884744 | tf_op jit(solution)/shard_map/ppermute | solution.py:667
  260.0 24.4 %collective-permute-start.28 = (bf16[48,3072]{1,0:T(8,128)(2,1)S(1)}, bf16[48,3072]{1,0:T(8,128)(2,1)S(1)}, u32[]{:S(2)}, u32[]{:S(2)}) collective-permute-start(bf16[48,3072]{1,0:T(8,128)(2,1)S(1)} %pad_maximum_fusion.3), channel_id=1, source_target_pairs={{0,16},{1,17},{2,18},{3,19},{4,20},{5,21},{6,22},{7,23},{8,24},{9,... | collective-permute-start | bytes 884744 | tf_op jit(solution)/shard_map/ppermute | solution.py:667
  264.1 24.7 %collective-permute-start.27 = (bf16[48,3072]{1,0:T(8,128)(2,1)S(1)}, bf16[48,3072]{1,0:T(8,128)(2,1)S(1)}, u32[]{:S(2)}, u32[]{:S(2)}) collective-permute-start(bf16[48,3072]{1,0:T(8,128)(2,1)S(1)} %pad_maximum_fusion.2), channel_id=1, source_target_pairs={{0,8},{1,9},{2,10},{3,11},{4,12},{5,13},{6,14},{7,15},{8,16},{9,17... | collective-permute-start | bytes 884744 | tf_op jit(solution)/shard_map/ppermute | solution.py:667
  271.3 17.7 %collective-permute-start.26 = (bf16[4,48,896]{2,1,0:T(8,128)(2,1)S(1)}, bf16[4,48,896]{2,1,0:T(8,128)(2,1)S(1)}, u32[]{:S(2)}, u32[]{:S(2)}) collective-permute-start(bf16[4,48,896]{2,1,0:T(8,128)(2,1)S(1)} %get-tuple-element.203), channel_id=1, source_target_pairs={{0,2},{1,3},{2,0},{3,1},{4,6},{5,7},{6,4},{7,5},{8,10},{9,11},{10,... | collective-permute-start | bytes 1032200 | tf_op jit(solution)/shard_map/ppermute | solution.py:667
  274.7 14.3 %collective-permute-start.25 = (bf16[4,48,768]{2,1,0:T(8,128)(2,1)S(1)}, bf16[4,48,768]{2,1,0:T(8,128)(2,1)S(1)}, u32[]{:S(2)}, u32[]{:S(2)}) collective-permute-start(bf16[4,48,768]{2,1,0:T(8,128)(2,1)S(1)} %get-tuple-element.204), channel_id=1, source_target_pairs={{0,4},{1,5},{2,6},{3,7},{4,0},{5,1},{6,2},{7,3},{8,12},{9,13},{10,... | collective-permute-start | bytes 884744 | tf_op jit(solution)/shard_map/ppermute | solution.py:667
  301.6 22.9 %all-to-all-start.3 = ((bf16[4,256,768]{2,1,0:T(8,128)(2,1)}), bf16[4,256,768]{2,1,0:T(8,128)(2,1)S(1)}, u32[]{:S(2)}, u32[]{:S(2)}) async-start(bf16[4,256,768]{2,1,0:T(8,128)(2,1)} %bitcast.146), calls=%async_computation.3 | async-start | bytes 3145728 | tf_op jit(solution)/shard_map/all_to_all | solution.py:736
  305.9 12.8 %collective-permute-start.30 = (bf16[48,1664]{1,0:T(8,128)(2,1)}, bf16[48,1664]{1,0:T(8,128)(2,1)S(1)}, u32[]{:S(2)}, u32[]{:S(2)}) collective-permute-start(bf16[48,1664]{1,0:T(8,128)(2,1)} %get-tuple-element.167), channel_id=1, source_target_pairs={{0,8},{1,9},{2,10},{3,11},{4,12},{5,13},{6,14},{7,15},{8,16},{9,17... | collective-permute-start | bytes 479240 | tf_op jit(solution)/shard_map/ppermute | solution.py:667
  305.9 12.7 %collective-permute-start.31 = (bf16[48,1664]{1,0:T(8,128)(2,1)S(1)}, bf16[48,1664]{1,0:T(8,128)(2,1)S(1)}, u32[]{:S(2)}, u32[]{:S(2)}) collective-permute-start(bf16[48,1664]{1,0:T(8,128)(2,1)S(1)} %copy-done.36), channel_id=1, source_target_pairs={{0,16},{1,17},{2,18},{3,19},{4,20},{5,21},{6,22},{7,23},{8,24},{9,... | collective-permute-start | bytes 479240 | tf_op jit(solution)/shard_map/ppermute | solution.py:667
  306.4 13.4 %collective-permute-start.32 = (bf16[48,1664]{1,0:T(8,128)(2,1)S(1)}, bf16[48,1664]{1,0:T(8,128)(2,1)S(1)}, u32[]{:S(2)}, u32[]{:S(2)}) collective-permute-start(bf16[48,1664]{1,0:T(8,128)(2,1)S(1)} %copy-done.35), channel_id=1, source_target_pairs={{0,24},{1,25},{2,26},{3,27},{4,28},{5,29},{6,30},{7,31},{8,0},{9,1... | collective-permute-start | bytes 479240 | tf_op jit(solution)/shard_map/ppermute | solution.py:667
  (47 other events, 260.5 us)
